TPU v7x, 32 devices: a whole 2x2x4 slice. The times are simulated.
32 devices in a mesh: groups: 2 (over y), ops: 4 (over z), sec: 2 (over x), rep: 2 (over core).
Axes of the slice: x: 2, y: 2, z: 4, core: 2. Of those that a mesh axis runs over, the one named last changes fastest.
Arguments:
- correction: float32 [3, 64, 128, 128], P(None, ('groups', 'sec', 'rep'), 'ops'), parts along dimension 1, may hold values from -80 to 80
- left_blocks: float32 [1280, 128, 128], P(('groups', 'ops', 'sec', 'rep')), parts along dimension 0, may hold values from -0.5 to 0.5
- right_blocks: float32 [32, 128, 128], P(('groups', 'ops')), parts along dimension 0, may hold values from -0.125 to 0.125
- send_sector: int32 [8, 4, 2], P(('groups', 'sec', 'rep')), parts along dimension 0, may hold values from -1 to 7, as said below
- pair_slot: int32 [1280], P(('groups', 'ops', 'sec', 'rep')), parts along dimension 0, may hold values from 0 to 7, as said below
- pair_term: int32 [1280], P(('groups', 'ops', 'sec', 'rep')), parts along dimension 0, may hold values from 0 to 3
- pair_dst: int32 [1280], P(('groups', 'ops', 'sec', 'rep')), parts along dimension 0, may hold values from 0 to 7
- pair_live: int32 [1280], P(('groups', 'ops', 'sec', 'rep')), parts along dimension 0, may hold values from 0 to 1, as said below
Outputs:
- search_basis: float32 [3, 64, 128, 128], P(None, ('groups', 'sec', 'rep'), 'ops'), parts along dimension 1
- sigma_blocks: float32 [3, 64, 128, 128], P(None, ('groups', 'sec', 'rep'), 'ops'), parts along dimension 1
There are 2 independent parts, one for each index of `groups`. A program takes and returns all parts, laid end to end along the dimension named above; each array names one. Nothing has to cross between parts.
Inputs may be any that keep to these rules, and one draw needn't show every extreme that they name: `send_sector`: slot 0 of every sender and receiver holds a sector; the two sectors of one sender and receiver differ; -1 marks an empty slot; some receiver gets 2 filled slots from every sender. `pair_slot`: every pair names a filled slot of its own holder's received slots, slot e * 2 + c being slot c from sender e. `pair_live`: the share of live pairs differs from device to device; some device has all 40 pairs live.
All inputs are finite; a program needn't handle non-finite values.
Results may differ from a plain program's by a relative error of at most 0.0003.
Values sent between devices are 32-bit elements; how exact they have to be, the bound alone decides.
No kernel may reach another device: no remote copies, remote signals or barrier semaphores. Data moves between devices by JAX's collectives and lax.ppermute only.
A program may use at most 64 MiB of HBM per device.

v0:
```python
import jax
import jax.numpy as jnp
from jax import lax
from jax.sharding import PartitionSpec as P

epsilon = 1e-06
highest = lax.Precision.HIGHEST


def inverse_factor(gram_matrix):
    u_zero = jnp.sqrt(gram_matrix[0, 0])
    u_one = gram_matrix[0, 1] / u_zero
    u_two = gram_matrix[0, 2] / u_zero
    u_four = jnp.sqrt(gram_matrix[1, 1] - u_one * u_one)
    u_five = (gram_matrix[1, 2] - u_one * u_two) / u_four
    u_eight = jnp.sqrt(gram_matrix[2, 2] - u_two * u_two - u_five * u_five)
    v_zero = 1.0 / u_zero
    v_four = 1.0 / u_four
    v_eight = 1.0 / u_eight
    v_one = -u_one * v_zero * v_four
    v_five = -u_five * v_four * v_eight
    v_two = -(u_one * v_five + u_two * v_eight) * v_zero
    nought = jnp.zeros((), jnp.float32)
    return jnp.stack(
        [
            jnp.stack([v_zero, v_one, v_two]),
            jnp.stack([nought, v_four, v_five]),
            jnp.stack([nought, nought, v_eight]),
        ]
    )


def local(
    correction, left_blocks, right_blocks, send_sector, pair_slot, pair_term, pair_dst, pair_live
):
    holders = lax.axis_size(("sec", "rep"))
    sector_count = correction.shape[1]
    width = correction.shape[3]
    entry_count = float(sector_count * holders * width * width)
    local_gram = jnp.einsum("kabc,jabc->kj", correction, correction, precision=highest)
    gram_matrix = lax.psum(local_gram, ("ops", "sec", "rep")) / entry_count
    gram_matrix = gram_matrix + epsilon * jnp.eye(3, dtype=jnp.float32)
    inverse = inverse_factor(gram_matrix)
    search_basis = jnp.einsum("jabc,jk->kabc", correction, inverse, precision=highest)
    table = send_sector[0]
    filled = (table >= 0).astype(jnp.float32)
    whole_rows = lax.all_gather(search_basis, "ops", axis=2, tiled=True)
    taken = whole_rows[:, jnp.maximum(table, 0)]
    received = lax.all_to_all(
        taken * filled[None, :, :, None, None],
        ("sec", "rep"),
        split_axis=1,
        concat_axis=1,
        tiled=True,
    )
    received = received.reshape(3, received.shape[1] * received.shape[2], width, width)
    right_chosen = right_blocks[pair_term]
    alive = pair_live.astype(jnp.float32)
    placer = (pair_dst[None, :] == jnp.arange(sector_count)[:, None]).astype(jnp.float32) * alive[
        None, :
    ]
    partials = []
    for vector in range(3):
        source = received[vector][pair_slot]
        halfway = jnp.einsum("pij,pjl->pil", left_blocks, source, precision=highest)
        product = jnp.einsum("pil,pml->pim", halfway, right_chosen, precision=highest)
        partials.append(jnp.einsum("sp,pim->sim", placer, product, precision=highest))
    partial_sums = jnp.stack(partials)
    sigma_blocks = lax.psum_scatter(partial_sums, "ops", scatter_dimension=2, tiled=True)
    return (search_basis, sigma_blocks)


def solution(mesh):
    placed = (
        P(None, ("groups", "sec", "rep"), "ops", None),
        P(("groups", "ops", "sec", "rep"), None, None),
        P(("groups", "ops"), None, None),
        P(("groups", "sec", "rep"), None, None),
        P(("groups", "ops", "sec", "rep")),
        P(("groups", "ops", "sec", "rep")),
        P(("groups", "ops", "sec", "rep")),
        P(("groups", "ops", "sec", "rep")),
    )
    return jax.shard_map(
        local,
        mesh=mesh,
        in_specs=placed,
        out_specs=(
            P(None, ("groups", "sec", "rep"), "ops", None),
            P(None, ("groups", "sec", "rep"), "ops", None),
        ),
        check_vma=False,
    )
```

profile of v0, /device:TPU:0, one launch (start us, length us, event | category | flops | bytes accessed | tf_op | source)
XLA Modules:
  0.0 224.8 jit_solution(8885693569362438614)
XLA Ops:
  7.2 0.0 copy-start
  7.2 0.0 all-gather.2.cloned.1.call-start
  7.2 3.8 %convolution_bitcast_fusion = f32[3,3]{1,0:T(4,128)S(1)} fusion(f32[3,8,32,128]{3,2,1,0:T(8,128)} %param.8), kind=kOutput, calls=%fused_computation.18 | convolution fusion | flops 3538944 | bytes 393252 | tf_op jit(solution)/shard_map/kabc,jabc->kj/dot_general | solution.py:40
  11.1 34.9 %psum.7 = f32[3,3]{1,0:T(4,128)S(1)} all-reduce(f32[3,3]{1,0:T(4,128)S(1)} %convolution_bitcast_fusion), channel_id=1, replica_groups=mesh['groups'=2,'ops'=4,'sec'=2,'rep'=2] {'ops','sec','rep'}, use_global_device_ids=true, to_apply=%region_0.0 | all-reduce | flops 9 | bytes 72 | tf_op jit(solution)/shard_map/psum | solution.py:41
  46.0 0.7 fusion.44
  50.7 0.1 pad_bitcast_fusion
  50.8 0.1 copy.51
  50.9 0.1 maximum_bitcast_fusion.3
  51.0 0.1 copy.50
  51.1 0.1 maximum_bitcast_fusion.2
  51.2 0.1 copy.49
  51.3 3.0 %fusion.16 = f32[3,8,32,128]{3,0,2,1:T(4,128)} fusion(f32[3,8,32,128]{3,2,1,0:T(8,128)} %param.8, f32[1,3]{0,1:T(4,128)S(1)} %copy.51, f32[1,3]{0,1:T(4,128)S(1)} %copy.50, f32[1,3]{0,1:T(4,128)S(1)} %copy.49), kind=kOutput, calls=%fused_computation.19 | convolution fusion | flops 3538962 | bytes 786468 | tf_op jit(solution)/shard_map/jabc,jk->kabc/dot_general | solution.py:44
  54.4 0.0 all-gather.2.cloned.1.call-update
  54.4 0.7 broadcast_maximum_fusion
  55.1 0.1 copy.53
  55.2 0.1 reshape.44
  55.2 0.7 fusion.38
  55.9 0.1 copy.54
  56.0 41.7 %all-gather.2.cloned.1.call-done = f32[3,8,128,128]{3,0,2,1:T(4,128)} async-done(((f32[3,8,32,128]{3,0,2,1:T(4,128)}), f32[3,8,128,128]{3,0,2,1:T(4,128)}) %all-gather.2.cloned.1.call-update) | async-done | bytes 1572880 | tf_op jit(solution)/shard_map/all_gather | solution.py:47
  97.8 4.6 %gather_fusion = f32[8,3,128,128]{3,1,2,0:T(4,128)} fusion(f32[3,8,128,128]{3,0,2,1:T(4,128)} %all-gather.2.cloned.1.call-done, s32[1024]{0:T(1024)S(1)} %pad_clamp_fusion.2), kind=kCustom, calls=%fused_computation | custom fusion | bytes 3145760 | tf_op jit(solution)/shard_map/gather | solution.py:48
  102.4 3.1 %fusion.6 = f32[3,4,2,128,128]{4,3,2,0,1:T(8,128)} fusion(f32[4,2,3,128,128]{4,2,3,1,0:T(4,128)} %bitcast.77, f32[4,2]{1,0:T(4,128)S(1)} %copy.54), kind=kLoop, calls=%fused_computation.14 | loop fusion | flops 393216 | bytes 3145760 | tf_op jit(solution)/shard_map/mul | solution.py:50
  105.4 4.3 %all-to-all-start = ((f32[3,4,2,128,128]{4,3,2,0,1:T(8,128)}), f32[3,4,2,128,128]{4,3,2,0,1:T(8,128)}, u32[]{:S(2)}, u32[]{:S(2)}) async-start(f32[3,4,2,128,128]{4,3,2,0,1:T(8,128)} %fusion.6), calls=%async_computation | async-start | bytes 3145728 | tf_op jit(solution)/shard_map/all_to_all | solution.py:49
  109.8 0.2 reduce-scatter.5.cloned.1.call-start
  110.1 0.0 copy-start.11
  110.1 2.2 gather_fusion.2
  112.3 0.0 copy-done.11
  112.3 17.6 %all-to-all-done = f32[3,4,2,128,128]{4,3,2,0,1:T(8,128)} async-done(((f32[3,4,2,128,128]{4,3,2,0,1:T(8,128)}), f32[3,4,2,128,128]{4,3,2,0,1:T(8,128)}, u32[]{:S(2)}, u32[]{:S(2)}) %all-to-all-start) | async-done | bytes 1572896 | tf_op jit(solution)/shard_map/all_to_all | solution.py:49
  129.9 2.5 %fusion.43 = (f32[1,4,2,128,128]{4,3,2,0,1:T(8,128)S(1)}, f32[1,4,2,128,128]{4,3,2,0,1:T(8,128)}, f32[1,4,2,128,128]{4,3,2,0,1:T(8,128)}) fusion(f32[3,4,2,128,128]{4,3,2,0,1:T(8,128)} %all-to-all-done), kind=kLoop, calls=%fused_computation.60 | loop fusion | bytes 3145728 | tf_op jit(solution)/shard_map/slice | solution.py:64
  132.4 3.3 %gather_fusion.4 = f32[40,128,128]{2,1,0:T(8,128)} fusion(f32[8,128,128]{2,1,0:T(8,128)} %bitcast.76, s32[1024]{0:T(1024)S(1)} %pad_clamp_fusion.1), kind=kCustom, calls=%fused_computation.4 | custom fusion | bytes 5243040 | tf_op jit(solution)/shard_map/gather | solution.py:64
  135.7 3.2 %gather_fusion.3 = f32[40,128,128]{2,1,0:T(8,128)} fusion(f32[8,128,128]{2,1,0:T(8,128)} %bitcast.75, s32[1024]{0:T(1024)S(1)} %pad_clamp_fusion.1), kind=kCustom, calls=%fused_computation.3 | custom fusion | bytes 5243040 | tf_op jit(solution)/shard_map/gather | solution.py:64
  138.9 4.7 %fusion.49 = f32[40,128,128]{1,2,0:T(8,128)S(1)} fusion(f32[40,128,128]{2,1,0:T(8,128)} %gather_fusion.4, f32[40,128,128]{2,1,0:T(8,128)S(1)} %copy-done), kind=kOutput, calls=%fused_computation.66 | convolution fusion | flops 1006632960 | bytes 7864320 | tf_op jit(solution)/shard_map/pij,pjl->pil/dot_general | solution.py:65
  143.7 2.9 %fusion.47 = f32[40,128,128]{1,2,0:T(8,128)S(1)} fusion(f32[40,128,128]{2,1,0:T(8,128)S(1)} %copy-done.4, f32[40,128,128]{2,1,0:T(8,128)S(1)} %copy-done), kind=kOutput, calls=%fused_computation.64 | convolution fusion | flops 1006632960 | bytes 7864320 | tf_op jit(solution)/shard_map/pij,pjl->pil/dot_general | solution.py:65
  146.6 5.6 %fusion.50 = f32[40,128,128]{2,1,0:T(8,128)S(1)} fusion(f32[40,128,128]{1,2,0:T(8,128)S(1)} %fusion.49, f32[40,128,128]{2,1,0:T(8,128)S(1)} %copy-done.1), kind=kOutput, calls=%fused_computation.67 | convolution fusion | flops 1006632960 | bytes 7864320 | tf_op jit(solution)/shard_map/pil,pml->pim/dot_general | solution.py:66
  152.2 5.9 %fusion.48 = f32[40,128,128]{2,1,0:T(8,128)S(1)} fusion(f32[40,128,128]{1,2,0:T(8,128)S(1)} %fusion.47, f32[40,128,128]{2,1,0:T(8,128)S(1)} %copy-done.1), kind=kOutput, calls=%fused_computation.65 | convolution fusion | flops 1006632960 | bytes 7864320 | tf_op jit(solution)/shard_map/pil,pml->pim/dot_general | solution.py:66
  158.1 3.6 %fusion.13 = f32[1,8,128,128]{3,1,2,0:T(8,128)} fusion(f32[40,128,128]{2,1,0:T(8,128)S(1)} %fusion.50, f32[40]{0:T(128)S(1)} %convert_element_type.15, s32[40]{0:T(128)S(1)} %copy-done.8), kind=kOutput, calls=%fused_computation.17 | convolution fusion | flops 62915200 | bytes 3146048 | tf_op jit(solution)/shard_map/sp,pim->sim/dot_general | solution.py:67
  161.7 3.6 %fusion.10 = f32[1,8,128,128]{3,1,2,0:T(8,128)} fusion(f32[40,128,128]{2,1,0:T(8,128)S(1)} %fusion.48, f32[40]{0:T(128)S(1)} %convert_element_type.15, s32[40]{0:T(128)S(1)} %copy-done.8), kind=kOutput, calls=%fused_computation.16 | convolution fusion | flops 62915200 | bytes 3146048 | tf_op jit(solution)/shard_map/sp,pim->sim/dot_general | solution.py:67
  165.4 2.2 gather_fusion.1
  167.6 4.7 %fusion.45 = f32[40,128,128]{1,2,0:T(8,128)S(1)} fusion(f32[40,128,128]{2,1,0:T(8,128)} %gather_fusion.1, f32[40,128,128]{2,1,0:T(8,128)S(1)} %copy-done), kind=kOutput, calls=%fused_computation.62 | convolution fusion | flops 1006632960 | bytes 7864320 | tf_op jit(solution)/shard_map/pij,pjl->pil/dot_general | solution.py:65
  172.3 5.9 %fusion.46 = f32[40,128,128]{2,1,0:T(8,128)S(1)} fusion(f32[40,128,128]{1,2,0:T(8,128)S(1)} %fusion.45, f32[40,128,128]{2,1,0:T(8,128)S(1)} %copy-done.2), kind=kOutput, calls=%fused_computation.63 | convolution fusion | flops 1006632960 | bytes 7864320 | tf_op jit(solution)/shard_map/pil,pml->pim/dot_general | solution.py:66
  178.2 2.8 %fusion.7 = f32[1,8,128,128]{3,1,2,0:T(8,128)S(1)} fusion(f32[40,128,128]{2,1,0:T(8,128)S(1)} %fusion.46, f32[40]{0:T(128)S(1)} %convert_element_type.15, s32[40]{0:T(128)S(1)} %copy-done.8), kind=kOutput, calls=%fused_computation.15 | convolution fusion | flops 62915200 | bytes 3146048 | tf_op jit(solution)/shard_map/sp,pim->sim/dot_general | solution.py:67
  181.1 0.1 pad_maximum_fusion
  181.2 0.1 copy.75
  181.3 1.5 copy.100
  182.8 0.0 reduce-scatter.5.cloned.1.call-update
  182.8 0.8 copy.65
  183.6 32.5 %reduce-scatter.5.cloned.1.call-done = f32[32,3072]{1,0:T(8,128)} async-done(((f32[128,3072]{1,0:T(8,128)}), f32[32,3072]{1,0:T(8,128)}) %reduce-scatter.5.cloned.1.call-update) | async-done | bytes 393232
  216.0 1.1 copy.79
  217.1 0.8 copy.66
  (28 shorter events, 0.1 us)
Async XLA Ops:
  7.2 131.8 %copy-start = (f32[40,128,128]{2,1,0:T(8,128)S(1)}, f32[40,128,128]{2,1,0:T(8,128)}, u32[]{:S(2)}) copy-start(f32[40,128,128]{2,1,0:T(8,128)} %param.9) | copy-start | bytes 7864324
  7.2 90.6 %all-gather.2.cloned.1.call-start = ((), (), s32[]{:S(2)}) async-start(), calls=%async_computation.2 | async-start | bytes 2621440 | tf_op jit(solution)/shard_map/all_gather | solution.py:47
  102.3 7.7 %copy-start.9 = (s32[40]{0:T(128)S(1)}, s32[40]{0:T(128)}, u32[]{:S(2)}) copy-start(s32[40]{0:T(128)} %param.15) | copy-start | bytes 484
  102.3 7.7 %copy-start.10 = (s32[40]{0:T(128)S(1)}, s32[40]{0:T(128)}, u32[]{:S(2)}) copy-start(s32[40]{0:T(128)} %param.13) | copy-start | bytes 484
  102.3 7.7 %copy-start.3 = (f32[4,128,128]{2,1,0:T(8,128)S(1)}, f32[4,128,128]{2,1,0:T(8,128)}, u32[]{:S(2)}) copy-start(f32[4,128,128]{2,1,0:T(8,128)} %param.10) | copy-start | bytes 786436
  105.4 24.5 %all-to-all-start = ((f32[3,4,2,128,128]{4,3,2,0,1:T(8,128)}), f32[3,4,2,128,128]{4,3,2,0,1:T(8,128)}, u32[]{:S(2)}, u32[]{:S(2)}) async-start(f32[3,4,2,128,128]{4,3,2,0,1:T(8,128)} %fusion.6), calls=%async_computation | async-start | bytes 3145728 | tf_op jit(solution)/shard_map/all_to_all | solution.py:49
  109.8 106.3 %reduce-scatter.5.cloned.1.call-start = ((), (), s32[]{:S(2)}) async-start(), calls=%async_computation.3 | async-start | bytes 1966080
  110.1 2.2 copy-start.11
  138.9 4.7 %copy-start.4 = (f32[40,128,128]{2,1,0:T(8,128)S(1)}, f32[40,128,128]{2,1,0:T(8,128)}, u32[]{:S(2)}) copy-start(f32[40,128,128]{2,1,0:T(8,128)} %gather_fusion.3) | copy-start | bytes 7864324
  143.6 2.9 %copy-start.1 = (f32[40,128,128]{2,1,0:T(8,128)S(1)}, f32[40,128,128]{2,1,0:T(8,128)}, u32[]{:S(2)}) copy-start(f32[40,128,128]{2,1,0:T(8,128)} %gather_fusion.2) | copy-start | bytes 7864324
  152.2 5.9 %copy-start.8 = (s32[40]{0:T(128)S(1)}, s32[40]{0:T(128)}, u32[]{:S(2)}) copy-start(s32[40]{0:T(128)} %param.14) | copy-start | bytes 484
  167.6 4.7 %copy-start.2 = (f32[40,128,128]{2,1,0:T(8,128)S(1)}, f32[40,128,128]{2,1,0:T(8,128)}, u32[]{:S(2)}) copy-start(f32[40,128,128]{2,1,0:T(8,128)} %gather_fusion.2) | copy-start | bytes 7864324
  178.2 2.8 %copy-start.6 = (f32[1,8,128,128]{3,1,2,0:T(8,128)S(1)}, f32[1,8,128,128]{3,1,2,0:T(8,128)}, u32[]{:S(2)}) copy-start(f32[1,8,128,128]{3,1,2,0:T(8,128)} %fusion.13) | copy-start | bytes 1572868
  178.2 2.8 %copy-start.7 = (f32[1,8,128,128]{3,1,2,0:T(8,128)S(1)}, f32[1,8,128,128]{3,1,2,0:T(8,128)}, u32[]{:S(2)}) copy-start(f32[1,8,128,128]{3,1,2,0:T(8,128)} %fusion.10) | copy-start | bytes 1572868
  181.3 1.5 copy-start.5
Sparse Core Ops, SparseCore 0:
  54.5 43.2 all-gather.1
  182.9 33.0 reduce-scatter.4
where the time goes:
time: 225 us
  waiting for transfers between devices  91.8 us (41%)
  matrix products  46.7 us (21%)
  blocking collectives  34.9 us (16%)
  local copies, waits for them, and re-layouts  23.6 us (10%)
  between operations  18.4 us (8%)
  other arithmetic  4.73 us (2%)
  starting transfers between devices  4.61 us (2%)
    all_gather x1, waiting for transfers between devices, local(): whole_rows = lax.all_gather(search_basis, 'ops', axis=2, tiled=True)  41.7 us
    psum x1, blocking collectives, local(): gram_matrix = lax.psum(local_gram, ('ops', 'sec', 'rep')) / entry_count  34.9 us
    unnamed x3, waiting for transfers between devices  32.5 us
    all_to_all x1, waiting for transfers between devices, local(): lax.all_to_all(taken * filled[None, :, :, None, None], ('sec', 'rep'), sp...  17.6 us
    dot_general x3, matrix products, local(): jnp.einsum('pil,pml->pim', halfway, right_chosen, precision=highest)  17.4 us
    dot_general x3, matrix products, local(): halfway = jnp.einsum('pij,pjl->pil', left_blocks, source, precision=highest)  12.3 us
    dot_general x3, matrix products, local(): jnp.einsum('sp,pim->sim', placer, product, precision=highest)  10.1 us
    gather x3, local copies, waits for them, and re-layouts, local(): source = received[vector][pair_slot]  8.73 us
  transfers between devices with their start and end apart: 3, of which 3 were waited for; matrix products, arithmetic and copies ran while one was open for 2% of the time, Pallas kernels for 0%

commit v1 on v0

v1 whole, which is shorter than its diff:
```python
import functools

import jax
import jax.numpy as jnp
from jax import lax
from jax.experimental import pallas as pl
from jax.experimental.pallas import tpu as pltpu
from jax.sharding import PartitionSpec as P

epsilon = 1e-06
vmem = pl.BlockSpec(memory_space=pltpu.VMEM)
smem = pl.BlockSpec(memory_space=pltpu.SMEM)
limit = pltpu.CompilerParams(vmem_limit_bytes=48 * 1024 * 1024)
pairs_of_three = ((0, 0), (0, 1), (0, 2), (1, 1), (1, 2), (2, 2))


def low_bit(mask):
    return mask & -mask


def swap(value, axes, size, mask):
    return lax.ppermute(value, axes, [(i, i ^ mask) for i in range(size)])


def holder_index():
    return lax.axis_index("sec") * lax.axis_size("rep") + lax.axis_index("rep")


def pack_kernel(holders, table_ref, correction_ref, *outs):
    vectors, _, rows, width = correction_ref.shape
    here = holder_index()
    tiles = []
    for i, j in pairs_of_three:
        total = jnp.sum(correction_ref[i] * correction_ref[j], axis=(0, 1))[None, :]
        total = jnp.sum(total, axis=1, keepdims=True)
        tiles.append(jnp.broadcast_to(total, (1, width)))
    tiles.append(jnp.zeros((2, width), jnp.float32))
    gram = jnp.concatenate(tiles, axis=0)
    for mask in range(holders):
        receiver = here ^ mask
        for slot in range(table_ref.shape[1]):
            sector = table_ref[receiver, slot]
            filled = (sector >= 0).astype(jnp.float32)
            sector = jnp.maximum(sector, 0)
            for vector in range(vectors):
                start = (vector * table_ref.shape[1] + slot) * rows
                outs[mask][start : start + rows, :] = correction_ref[vector, sector] * filled
        outs[mask][outs[mask].shape[0] - 8 :, :] = gram


def join_kernel(holders, cap, rows, *refs):
    received, outs = refs[:holders], refs[holders:]
    for vector, out in enumerate(outs):
        for mask in range(holders):
            part = received[mask][vector * cap * rows : (vector + 1) * cap * rows, :]
            out[mask * cap * rows : (mask + 1) * cap * rows, :] = part
    height = received[0].shape[0]
    gram = received[0][height - 8 :, :]
    for mask in range(1, holders):
        gram = gram + received[mask][height - 8 :, :]
    outs[0][holders * cap * rows :, :] = gram


def split(value):
    high = value.astype(jnp.bfloat16)
    return high, (value - high.astype(jnp.float32)).astype(jnp.bfloat16)


def operator_kernel(live_ref, left_ref, right_ref, high_ref, low_ref, right_high_ref, right_low_ref):
    width = left_ref.shape[1]

    def step(pair, carry):
        high, low = split(left_ref[pair] * live_ref[pair].astype(jnp.float32))
        high_ref[pair] = high
        low_ref[pair] = low
        return carry

    lax.fori_loop(0, left_ref.shape[0], step, 0, unroll=4)
    for term in range(right_ref.shape[0]):
        high, low = split(right_ref[term].T)
        right_high_ref[:, term * width : (term + 1) * width] = high
        right_low_ref[:, term * width : (term + 1) * width] = low


def inverse_rows(gram, entry_count):
    row = [gram[i : i + 1, :] / entry_count for i in range(6)]
    u_zero = jnp.sqrt(row[0] + epsilon)
    u_one = row[1] / u_zero
    u_two = row[2] / u_zero
    u_four = jnp.sqrt(row[3] + epsilon - u_one * u_one)
    u_five = (row[4] - u_one * u_two) / u_four
    u_eight = jnp.sqrt(row[5] + epsilon - u_two * u_two - u_five * u_five)
    v_zero = 1.0 / u_zero
    v_four = 1.0 / u_four
    v_eight = 1.0 / u_eight
    v_one = -u_one * v_zero * v_four
    v_five = -u_five * v_four * v_eight
    v_two = -(u_one * v_five + u_two * v_eight) * v_zero
    return [v_zero, v_one, v_two, v_four, v_five, v_eight]


def apply_kernel(vector, ops, rows, entry_count, *refs):
    refs = list(refs)
    slot_ref, term_ref, dst_ref = refs[:3]
    del refs[:3]
    pieces = [[refs.pop(0) for _ in range(ops)] for _ in range(vector + 1)]
    inverse_in = refs.pop(0) if vector else None
    high_ref, low_ref, right_high_ref, right_low_ref = refs[:4]
    del refs[:4]
    outs = [refs.pop(0) for _ in range(ops)]
    inverse_out = None if vector else refs.pop(0)
    source_ref, chosen_ref, total_ref = refs
    here, place = holder_index(), lax.axis_index("ops")
    slots, width, _ = source_ref.shape
    terms = right_high_ref.shape[1] // width
    count = slots * rows
    if vector:
        inverse = inverse_in[...]
    else:
        gram = pieces[0][0][count:, :]
        for mask in range(1, ops):
            gram = gram + pieces[0][mask][count:, :]
        inverse = jnp.concatenate(inverse_rows(gram, entry_count) + [gram[6:]], axis=0)
        inverse_out[...] = inverse
    factors = [
        inverse[i : i + 1, :] for i, (_, j) in enumerate(pairs_of_three) if j == vector
    ]
    for mask in range(ops):
        value = sum(pieces[j][mask][:count, :] * factors[j] for j in range(vector + 1))
        start = pl.multiple_of((place ^ mask) * rows, rows)
        source_ref[:, pl.ds(start, rows), :] = value.reshape(slots, rows, width)

    def right_step(slot, carry):
        high, low = split(source_ref[slot])
        product = jnp.dot(high, right_high_ref[...], preferred_element_type=jnp.float32)
        product += jnp.dot(low, right_high_ref[...], preferred_element_type=jnp.float32)
        product += jnp.dot(high, right_low_ref[...], preferred_element_type=jnp.float32)
        for term in range(terms):
            high, low = split(product[:, term * width : (term + 1) * width])
            chosen_ref[slot * terms + term, :, :width] = high
            chosen_ref[slot * terms + term, :, width:] = low
        return carry

    lax.fori_loop(0, slots, right_step, 0, unroll=2)
    total_ref[...] = jnp.zeros_like(total_ref)
    cap = slots // (lax.axis_size("sec") * lax.axis_size("rep"))

    def pair_step(pair, carry):
        slot = slot_ref[pair]
        slot = ((slot // cap) ^ here) * cap + slot % cap
        index = slot * terms + term_ref[pair]
        both = jnp.dot(high_ref[pair], chosen_ref[index], preferred_element_type=jnp.float32)
        rest = jnp.dot(low_ref[pair], chosen_ref[index, :, :width], preferred_element_type=jnp.float32)
        total_ref[dst_ref[pair]] += both[:, :width] + both[:, width:] + rest
        return carry

    lax.fori_loop(0, high_ref.shape[0], pair_step, 0, unroll=4)
    for mask in range(ops):
        start = pl.multiple_of((place ^ mask) * rows, rows)
        outs[mask][...] = total_ref[:, pl.ds(start, rows), :]


def local(
    correction, left_blocks, right_blocks, send_sector, pair_slot, pair_term, pair_dst, pair_live
):
    ops, holders = lax.axis_size("ops"), lax.axis_size(("sec", "rep"))
    vectors, sectors, rows, width = correction.shape
    cap = send_sector.shape[2]
    terms, pair_count = right_blocks.shape[0], left_blocks.shape[0]
    slots = holders * cap
    entry_count = float(sectors * holders * width * width)
    f32, bf16 = jnp.float32, jnp.bfloat16

    packed = pl.pallas_call(
        functools.partial(pack_kernel, holders),
        out_shape=[jax.ShapeDtypeStruct((vectors * cap * rows + 8, width), f32)] * holders,
        in_specs=[smem, vmem],
        out_specs=[vmem] * holders,
        compiler_params=limit,
        name="pack",
    )(send_sector[0], correction)
    received = [packed[0]] + [
        swap(packed[mask], ("sec", "rep"), holders, mask) for mask in range(1, holders)
    ]
    operators = pl.pallas_call(
        operator_kernel,
        out_shape=[jax.ShapeDtypeStruct((pair_count, width, width), bf16)] * 2
        + [jax.ShapeDtypeStruct((width, terms * width), bf16)] * 2,
        in_specs=[smem, vmem, vmem],
        out_specs=[vmem] * 4,
        compiler_params=limit,
        name="operators",
    )(pair_live, left_blocks, right_blocks)
    joined = pl.pallas_call(
        functools.partial(join_kernel, holders, cap, rows),
        out_shape=[
            jax.ShapeDtypeStruct((slots * rows + (0 if vector else 8), width), f32)
            for vector in range(vectors)
        ],
        in_specs=[vmem] * holders,
        out_specs=[vmem] * vectors,
        compiler_params=limit,
        name="join",
    )(*received)

    pieces = []
    for vector in range(vectors):
        piece = [joined[vector]] + [None] * (ops - 1)
        for mask in sorted(range(1, ops), key=lambda m: (bin(m).count("1"), -m)):
            bit = low_bit(mask)
            piece[mask] = swap(piece[mask ^ bit], "ops", ops, bit)
        pieces.append(piece)

    inverse = None
    sums = []
    for vector in range(vectors):
        arguments = [pair_slot, pair_term, pair_dst]
        for piece in pieces[: vector + 1]:
            arguments += piece
        if vector:
            arguments.append(inverse)
        arguments += operators
        out_shape = [jax.ShapeDtypeStruct((sectors, rows, width), f32)] * ops
        if not vector:
            out_shape = out_shape + [jax.ShapeDtypeStruct((8, width), f32)]
        parts = pl.pallas_call(
            functools.partial(apply_kernel, vector, ops, rows, entry_count),
            out_shape=out_shape,
            in_specs=[smem] * 3 + [vmem] * (len(arguments) - 3),
            out_specs=[vmem] * len(out_shape),
            scratch_shapes=[
                pltpu.VMEM((slots, width, width), f32),
                pltpu.VMEM((slots * terms, width, 2 * width), bf16),
                pltpu.VMEM((sectors, width, width), f32),
            ],
            compiler_params=limit,
            name="apply",
        )(*arguments)
        if not vector:
            inverse = parts[ops]
        parts = list(parts[:ops])
        for mask in sorted(range(1, ops), key=lambda m: (-bin(m).count("1"), -m)):
            bit = low_bit(mask)
            parts[mask ^ bit] = parts[mask ^ bit] + swap(parts[mask], "ops", ops, bit)
        sums.append(parts[0])

    column = inverse[:6, 0]
    search_basis = []
    for k in range(vectors):
        picked = [(i, a) for i, (a, b) in enumerate(pairs_of_three) if b == k]
        search_basis.append(sum(correction[a] * column[i] for i, a in picked))
    return (jnp.stack(search_basis), jnp.stack(sums))


def solution(mesh):
    placed = (
        P(None, ("groups", "sec", "rep"), "ops", None),
        P(("groups", "ops", "sec", "rep"), None, None),
        P(("groups", "ops"), None, None),
        P(("groups", "sec", "rep"), None, None),
        P(("groups", "ops", "sec", "rep")),
        P(("groups", "ops", "sec", "rep")),
        P(("groups", "ops", "sec", "rep")),
        P(("groups", "ops", "sec", "rep")),
    )
    return jax.shard_map(
        local,
        mesh=mesh,
        in_specs=placed,
        out_specs=(
            P(None, ("groups", "sec", "rep"), "ops", None),
            P(None, ("groups", "sec", "rep"), "ops", None),
        ),
        check_vma=False,
    )
```

time: 225 us -> 81.3 us (0.36)
  waiting for transfers between devices: 91.8 us -> 26.5 us
  matrix products: 46.7 us -> 0 us
  blocking collectives: 34.9 us -> 0 us
  starting transfers between devices: 4.61 us -> 26 us
  local copies, waits for them, and re-layouts: 23.6 us -> 5.71 us
  between operations: 18.4 us -> 0.78 us
  Pallas kernels: 0 us -> 16.4 us
    dot_general x11 -> x0, matrix products: 46.7 us -> none  [the longest x3 17.4 us: local(): jnp.einsum('pil,pml->pim', halfway, right_chosen, precision=highest)]
    all_gather x1 -> x0, waiting for transfers between devices: 41.7 us -> none  [local(): whole_rows = lax.all_gather(search_basis, 'ops', axis=2, tiled=True)]
    psum x1 -> x0, blocking collectives: 34.9 us -> none  [local(): gram_matrix = lax.psum(local_gram, ('ops', 'sec', 'rep')) / entry_count]
    unnamed x3 -> x0, waiting for transfers between devices: 32.5 us -> none
    ppermute x0 -> x21, waiting for transfers between devices: none -> 26.5 us  [swap(): return lax.ppermute(value, axes, [(i, i ^ mask) for i in range(size)])]
    ppermute x0 -> x21, starting transfers between devices: none -> 26 us  [swap(): return lax.ppermute(value, axes, [(i, i ^ mask) for i in range(size)])]
    all_to_all x1 -> x0, waiting for transfers between devices: 17.6 us -> none  [local(): lax.all_to_all(taken * filled[None, :, :, None, None], ('sec', 'rep'), sp...]
    pallas_call x0 -> x6, Pallas kernels: none -> 16.4 us  [the longest x3 14.6 us: local(): pl.pallas_call(functools.partial(apply_kernel, vector, ops, rows, entry_c...]
  transfers between devices with their start and end apart: 3 -> 21, of which waited for: 3 -> 7; matrix products, arithmetic and copies ran while one was open for 2% -> 7% of each run, Pallas kernels for 0% -> 19%
where the time goes in v1:
time: 81.3 us; the launch traced here: 81 us
  waiting for transfers between devices  26.5 us (33%)
  starting transfers between devices  26 us (32%)
  Pallas kernels  16.4 us (20%)
  local copies, waits for them, and re-layouts  5.71 us (7%)
  other arithmetic  5.57 us (7%)
    ppermute x21, waiting for transfers between devices, swap(): return lax.ppermute(value, axes, [(i, i ^ mask) for i in range(size)])  26.5 us
    ppermute x21, starting transfers between devices, swap(): return lax.ppermute(value, axes, [(i, i ^ mask) for i in range(size)])  26 us
    pallas_call x3, Pallas kernels, local(): pl.pallas_call(functools.partial(apply_kernel, vector, ops, rows, entry_c...  14.6 us
    unnamed x16, local copies, waits for them, and re-layouts  4.35 us
    mul x1, other arithmetic, local(): search_basis.append(sum((correction[a] * column[i] for i, a in picked)))  3.87 us
    another operation x5, other arithmetic, local(): return (jnp.stack(search_basis), jnp.stack(sums))  1.64 us
  transfers between devices with their start and end apart: 21, of which 7 were waited for; matrix products, arithmetic and copies ran while one was open for 7% of the time, Pallas kernels for 19%

profile of v1, /device:TPU:0, one launch (start us, length us, event | category | flops | bytes accessed | tf_op | source)
XLA Modules:
  0.0 81.0 jit_solution(16320335824708608489)
XLA Ops:
  0.6 0.8 copy.10.table_ref
  1.4 1.0 %copy-done.1 = f32[3,8,32,128]{3,2,1,0:T(8,128)S(1)} copy-done((f32[3,8,32,128]{3,2,1,0:T(8,128)S(1)}, f32[3,8,32,128]{3,2,1,0:T(8,128)}, u32[]{:S(2)}) %copy-start.1) | copy-done | bytes 393240
  2.4 0.7 pack.1
  3.1 0.5 collective-permute-start
  3.6 2.6 %collective-permute-start.1 = (f32[200,128]{1,0:T(8,128)S(1)}, f32[200,128]{1,0:T(8,128)S(1)}, u32[]{:S(2)}, u32[]{:S(2)}) collective-permute-start(f32[200,128]{1,0:T(8,128)S(1)} %get-tuple-element.28), channel_id=1, source_target_pairs={{0,2},{1,3},{2,0},{3,1},{4,6},{5,7},{6,4},{7,5},{8,10},{9,11},{10,... | collective-permute-start | bytes 307208 | tf_op jit(solution)/shard_map/ppermute | solution.py:22
  6.1 0.1 collective-permute-start.2
  6.2 0.0 collective-permute-done.refs_1_
  6.2 3.7 %collective-permute-done.1.refs_2_ = f32[200,128]{1,0:T(8,128)S(1)} collective-permute-done((f32[200,128]{1,0:T(8,128)S(1)}, f32[200,128]{1,0:T(8,128)S(1)}, u32[]{:S(2)}, u32[]{:S(2)}) %collective-permute-start.1) | collective-permute-done | bytes 102432 | tf_op jit(solution)/shard_map/ppermute | solution.py:22
  9.9 1.7 %collective-permute-done.2.refs_3_ = f32[200,128]{1,0:T(8,128)S(1)} collective-permute-done((f32[200,128]{1,0:T(8,128)S(1)}, f32[200,128]{1,0:T(8,128)S(1)}, u32[]{:S(2)}, u32[]{:S(2)}) %collective-permute-start.2) | collective-permute-done | bytes 102432 | tf_op jit(solution)/shard_map/ppermute | solution.py:22
  11.6 2.7 %collective-permute-start.4 = (f32[264,128]{1,0:T(8,128)S(1)}, f32[264,128]{1,0:T(8,128)S(1)}, u32[]{:S(2)}, u32[]{:S(2)}) collective-permute-start(f32[264,128]{1,0:T(8,128)S(1)} %get-tuple-element.30.refs_3_), channel_id=1, source_target_pairs={{0,8},{4,12},{8,0},{12,4},{1,9},{5,13},{9,1},{13,5},{2,10},{6,14},... | collective-permute-start | bytes 405512 | tf_op jit(solution)/shard_map/ppermute | solution.py:22
  14.3 1.6 %collective-permute-start.3 = (f32[264,128]{1,0:T(8,128)S(1)}, f32[264,128]{1,0:T(8,128)S(1)}, u32[]{:S(2)}, u32[]{:S(2)}) collective-permute-start(f32[264,128]{1,0:T(8,128)S(1)} %get-tuple-element.30.refs_3_), channel_id=1, source_target_pairs={{0,4},{4,0},{8,12},{12,8},{1,5},{5,1},{9,13},{13,9},{2,6},{6,2},{1... | collective-permute-start | bytes 405512 | tf_op jit(solution)/shard_map/ppermute | solution.py:22
  15.9 0.3 collective-permute-start.10
  16.2 2.6 %collective-permute-start.16 = (f32[256,128]{1,0:T(8,128)S(1)}, f32[256,128]{1,0:T(8,128)S(1)}, u32[]{:S(2)}, u32[]{:S(2)}) collective-permute-start(f32[256,128]{1,0:T(8,128)S(1)} %get-tuple-element.45.refs_11_), channel_id=1, source_target_pairs={{0,8},{4,12},{8,0},{12,4},{1,9},{5,13},{9,1},{13,5},{2,10},{6,14},... | collective-permute-start | bytes 393224 | tf_op jit(solution)/shard_map/ppermute | solution.py:22
  18.8 3.3 %collective-permute-done.4.refs_5_ = f32[264,128]{1,0:T(8,128)S(1)} collective-permute-done((f32[264,128]{1,0:T(8,128)S(1)}, f32[264,128]{1,0:T(8,128)S(1)}, u32[]{:S(2)}, u32[]{:S(2)}) %collective-permute-start.4) | collective-permute-done | bytes 135200 | tf_op jit(solution)/shard_map/ppermute | solution.py:22
  22.1 0.3 collective-permute-start.5
  22.4 1.7 %collective-permute-start.9 = (f32[256,128]{1,0:T(8,128)S(1)}, f32[256,128]{1,0:T(8,128)S(1)}, u32[]{:S(2)}, u32[]{:S(2)}) collective-permute-start(f32[256,128]{1,0:T(8,128)S(1)} %get-tuple-element.40.refs_7_), channel_id=1, source_target_pairs={{0,4},{4,0},{8,12},{12,8},{1,5},{5,1},{9,13},{13,9},{2,6},{6,2},{1... | collective-permute-start | bytes 393224 | tf_op jit(solution)/shard_map/ppermute | solution.py:22
  24.1 6.3 %collective-permute-done.10.refs_9_ = f32[256,128]{1,0:T(8,128)S(1)} collective-permute-done((f32[256,128]{1,0:T(8,128)S(1)}, f32[256,128]{1,0:T(8,128)S(1)}, u32[]{:S(2)}, u32[]{:S(2)}) %collective-permute-start.10) | collective-permute-done | bytes 131104 | tf_op jit(solution)/shard_map/ppermute | solution.py:22
  30.4 0.1 collective-permute-start.11
  30.5 2.1 %collective-permute-done.16.refs_13_ = f32[256,128]{1,0:T(8,128)S(1)} collective-permute-done((f32[256,128]{1,0:T(8,128)S(1)}, f32[256,128]{1,0:T(8,128)S(1)}, u32[]{:S(2)}, u32[]{:S(2)}) %collective-permute-start.16) | collective-permute-done | bytes 131104 | tf_op jit(solution)/shard_map/ppermute | solution.py:22
  32.6 0.6 collective-permute-start.15
  33.3 1.4 %collective-permute-start.17 = (f32[256,128]{1,0:T(8,128)S(1)}, f32[256,128]{1,0:T(8,128)S(1)}, u32[]{:S(2)}, u32[]{:S(2)}) collective-permute-start(f32[256,128]{1,0:T(8,128)S(1)} %collective-permute-done.16.refs_13_), channel_id=1, source_target_pairs={{0,4},{4,0},{8,12},{12,8},{1,5},{5,1},{9,13},{13,9},{2,6},{6,2},{1... | collective-permute-start | bytes 393224 | tf_op jit(solution)/shard_map/ppermute | solution.py:22
  34.7 1.7 %copy-done = f32[40,128,128]{2,1,0:T(8,128)S(1)} copy-done((f32[40,128,128]{2,1,0:T(8,128)S(1)}, f32[40,128,128]{2,1,0:T(8,128)}, u32[]{:S(2)}) %copy-start) | copy-done | bytes 2621464
  36.4 0.9 %copy-done.3 = f32[4,128,128]{2,1,0:T(8,128)S(1)} copy-done((f32[4,128,128]{2,1,0:T(8,128)S(1)}, f32[4,128,128]{2,1,0:T(8,128)}, u32[]{:S(2)}) %copy-start.3) | copy-done | bytes 262168
  37.4 0.7 copy-done.7
  38.0 1.1 %operators.1 = (bf16[40,128,128]{2,1,0:T(8,128)(2,1)S(1)}, bf16[40,128,128]{2,1,0:T(8,128)(2,1)S(1)}, bf16[128,512]{1,0:T(8,128)(2,1)S(1)}, bf16[128,512]{1,0:T(8,128)(2,1)S(1)}) custom-call(s32[40]{0:T(128)S(1)} %copy-done.7, f32[40,128,128]{2,1,0:T(8,128)S(1)} %copy-done, f32[4,128,128]{2,1,0:T(8,128)S(1)} %copy-done.3), custom_call_target="tpu_custom_call" | custom-call | tf_op jit(solution)/shard_map/operators/pallas_call | solution.py:185
  39.2 4.9 %apply.3 = (f32[8,32,128]{2,1,0:T(8,128)S(1)}, f32[8,32,128]{2,1,0:T(8,128)S(1)}, f32[8,32,128]{2,1,0:T(8,128)S(1)}, f32[8,32,128]{2,1,0:T(8,128)S(1)}, f32[8,128]{1,0:T(8,128)S(1)}) custom-call(s32[40]{0:T(128)S(1)} %copy-done.4, s32[40]{0:T(128)S(1)} %copy-done.5, s32[40]{0:T(128)S(1)} %copy-done.6, f32[264,128]{1,0:T(8,128)S(1)} %get-tuple-element.30.refs_3_, ...), custom_call_target="tpu_custom_call" | custom-call | tf_op jit(solution)/shard_map/apply/pallas_call | solution.py:226
  44.1 0.7 collective-permute-start.6
  44.7 1.4 %collective-permute-start.8 = (f32[8,32,128]{2,1,0:T(8,128)S(1)}, f32[8,32,128]{2,1,0:T(8,128)S(1)}, u32[]{:S(2)}, u32[]{:S(2)}) collective-permute-start(f32[8,32,128]{2,1,0:T(8,128)S(1)} %get-tuple-element.39), channel_id=1, source_target_pairs={{0,4},{4,0},{8,12},{12,8},{1,5},{5,1},{9,13},{13,9},{2,6},{6,2},{1... | collective-permute-start | bytes 393224 | tf_op jit(solution)/shard_map/ppermute | solution.py:22
  46.1 4.8 %apply.4 = (f32[8,32,128]{2,1,0:T(8,128)S(1)}, f32[8,32,128]{2,1,0:T(8,128)S(1)}, f32[8,32,128]{2,1,0:T(8,128)S(1)}, f32[8,32,128]{2,1,0:T(8,128)S(1)}) custom-call(s32[40]{0:T(128)S(1)} %copy-done.4, s32[40]{0:T(128)S(1)} %copy-done.5, s32[40]{0:T(128)S(1)} %copy-done.6, f32[264,128]{1,0:T(8,128)S(1)} %get-tuple-element.30.refs_3_, ...), custom_call_target="tpu_custom_call" | custom-call | tf_op jit(solution)/shard_map/apply/pallas_call | solution.py:226
  51.0 0.7 collective-permute-start.12
  51.7 0.0 collective-permute-done.15.refs_12_
  51.7 1.4 %collective-permute-start.14 = (f32[8,32,128]{2,1,0:T(8,128)S(1)}, f32[8,32,128]{2,1,0:T(8,128)S(1)}, u32[]{:S(2)}, u32[]{:S(2)}) collective-permute-start(f32[8,32,128]{2,1,0:T(8,128)S(1)} %get-tuple-element.44), channel_id=1, source_target_pairs={{0,4},{4,0},{8,12},{12,8},{1,5},{5,1},{9,13},{13,9},{2,6},{6,2},{1... | collective-permute-start | bytes 393224 | tf_op jit(solution)/shard_map/ppermute | solution.py:22
  53.1 0.0 collective-permute-done.17.refs_14_
  53.1 4.9 %apply.5 = (f32[8,32,128]{2,1,0:T(8,128)S(1)}, f32[8,32,128]{2,1,0:T(8,128)S(1)}, f32[8,32,128]{2,1,0:T(8,128)S(1)}, f32[8,32,128]{2,1,0:T(8,128)S(1)}) custom-call(s32[40]{0:T(128)S(1)} %copy-done.4, s32[40]{0:T(128)S(1)} %copy-done.5, s32[40]{0:T(128)S(1)} %copy-done.6, f32[264,128]{1,0:T(8,128)S(1)} %get-tuple-element.30.refs_3_, ...), custom_call_target="tpu_custom_call" | custom-call | tf_op jit(solution)/shard_map/apply/pallas_call | solution.py:226
  58.0 0.7 collective-permute-start.18
  58.7 0.6 fusion
  59.3 3.5 %collective-permute-start.7 = (f32[8,32,128]{2,1,0:T(8,128)S(1)}, f32[8,32,128]{2,1,0:T(8,128)S(1)}, u32[]{:S(2)}, u32[]{:S(2)}) collective-permute-start(f32[8,32,128]{2,1,0:T(8,128)S(1)} %add.42), channel_id=1, source_target_pairs={{0,8},{4,12},{8,0},{12,4},{1,9},{5,13},{9,1},{13,5},{2,10},{6,14},... | collective-permute-start | bytes 393224 | tf_op jit(solution)/shard_map/ppermute | solution.py:22
  62.8 3.9 %slice_multiply_fusion = (f32[1,8,32,128]{3,2,1,0:T(8,128)S(1)}, f32[1,8,32,128]{3,2,1,0:T(8,128)S(1)}, f32[1,8,32,128]{3,2,1,0:T(8,128)S(1)}) fusion(f32[3,8,32,128]{3,2,1,0:T(8,128)S(1)} %copy-done.2, f32[]{:T(128)} %bitcast.1, f32[]{:T(128)} %bitcast.6, f32[]{:T(128)} %bitcast.5, f32[]{:T(128)} %bitcast.4, f32[]{:T(128)} %bitcast.3, f32[]{:T(128)} %bitcast.2), kind=kLoop, calls=%fused_computation.7 | loop fusion | flops 294912 | bytes 786456 | tf_op jit(solution)/shard_map/mul | solution.py:251
  66.7 0.8 pad_maximum_fusion
  67.5 0.1 collective-permute-start.20
  67.6 0.0 collective-permute-done.18
  67.6 0.9 %collective-permute-start.13 = (f32[8,32,128]{2,1,0:T(8,128)S(1)}, f32[8,32,128]{2,1,0:T(8,128)S(1)}, u32[]{:S(2)}, u32[]{:S(2)}) collective-permute-start(f32[8,32,128]{2,1,0:T(8,128)S(1)} %add.45), channel_id=1, source_target_pairs={{0,8},{4,12},{8,0},{12,4},{1,9},{5,13},{9,1},{13,5},{2,10},{6,14},... | collective-permute-start | bytes 393224 | tf_op jit(solution)/shard_map/ppermute | solution.py:22
  68.5 0.0 collective-permute-done.8
  68.5 2.2 %collective-permute-start.19 = (f32[8,32,128]{2,1,0:T(8,128)S(1)}, f32[8,32,128]{2,1,0:T(8,128)S(1)}, u32[]{:S(2)}, u32[]{:S(2)}) collective-permute-start(f32[8,32,128]{2,1,0:T(8,128)S(1)} %add.48), channel_id=1, source_target_pairs={{0,8},{4,12},{8,0},{12,4},{1,9},{5,13},{9,1},{13,5},{2,10},{6,14},... | collective-permute-start | bytes 393224 | tf_op jit(solution)/shard_map/ppermute | solution.py:22
  70.7 0.0 collective-permute-done.7
  70.7 8.1 %collective-permute-done.13 = f32[8,32,128]{2,1,0:T(8,128)S(1)} collective-permute-done((f32[8,32,128]{2,1,0:T(8,128)S(1)}, f32[8,32,128]{2,1,0:T(8,128)S(1)}, u32[]{:S(2)}, u32[]{:S(2)}) %collective-permute-start.13) | collective-permute-done | bytes 131104 | tf_op jit(solution)/shard_map/ppermute | solution.py:22
  78.8 1.4 %collective-permute-done.19 = f32[8,32,128]{2,1,0:T(8,128)S(1)} collective-permute-done((f32[8,32,128]{2,1,0:T(8,128)S(1)}, f32[8,32,128]{2,1,0:T(8,128)S(1)}, u32[]{:S(2)}, u32[]{:S(2)}) %collective-permute-start.19) | collective-permute-done | bytes 131104 | tf_op jit(solution)/shard_map/ppermute | solution.py:22
  80.2 0.8 pad_maximum_fusion.1
  (27 shorter events, 0.2 us)
Async XLA Ops:
  1.4 1.0 %copy-start.1 = (f32[3,8,32,128]{3,2,1,0:T(8,128)S(1)}, f32[3,8,32,128]{3,2,1,0:T(8,128)}, u32[]{:S(2)}) copy-start(f32[3,8,32,128]{3,2,1,0:T(8,128)} %correction_ref.1) | copy-start | bytes 1179652
  3.1 3.1 %collective-permute-start = (f32[200,128]{1,0:T(8,128)S(1)}, f32[200,128]{1,0:T(8,128)S(1)}, u32[]{:S(2)}, u32[]{:S(2)}) collective-permute-start(f32[200,128]{1,0:T(8,128)S(1)} %get-tuple-element.27), channel_id=1, source_target_pairs={{0,1},{1,0},{2,3},{3,2},{4,5},{5,4},{6,7},{7,6},{8,9},{9,8},{10,11... | collective-permute-start | bytes 307208 | tf_op jit(solution)/shard_map/ppermute | solution.py:22
  3.6 6.3 %collective-permute-start.1 = (f32[200,128]{1,0:T(8,128)S(1)}, f32[200,128]{1,0:T(8,128)S(1)}, u32[]{:S(2)}, u32[]{:S(2)}) collective-permute-start(f32[200,128]{1,0:T(8,128)S(1)} %get-tuple-element.28), channel_id=1, source_target_pairs={{0,2},{1,3},{2,0},{3,1},{4,6},{5,7},{6,4},{7,5},{8,10},{9,11},{10,... | collective-permute-start | bytes 307208 | tf_op jit(solution)/shard_map/ppermute | solution.py:22
  6.1 5.4 %collective-permute-start.2 = (f32[200,128]{1,0:T(8,128)S(1)}, f32[200,128]{1,0:T(8,128)S(1)}, u32[]{:S(2)}, u32[]{:S(2)}) collective-permute-start(f32[200,128]{1,0:T(8,128)S(1)} %get-tuple-element.29), channel_id=1, source_target_pairs={{0,3},{1,2},{2,1},{3,0},{4,7},{5,6},{6,5},{7,4},{8,11},{9,10},{10,... | collective-permute-start | bytes 307208 | tf_op jit(solution)/shard_map/ppermute | solution.py:22
  11.6 10.5 %collective-permute-start.4 = (f32[264,128]{1,0:T(8,128)S(1)}, f32[264,128]{1,0:T(8,128)S(1)}, u32[]{:S(2)}, u32[]{:S(2)}) collective-permute-start(f32[264,128]{1,0:T(8,128)S(1)} %get-tuple-element.30.refs_3_), channel_id=1, source_target_pairs={{0,8},{4,12},{8,0},{12,4},{1,9},{5,13},{9,1},{13,5},{2,10},{6,14},... | collective-permute-start | bytes 405512 | tf_op jit(solution)/shard_map/ppermute | solution.py:22
  14.3 18.9 %collective-permute-start.3 = (f32[264,128]{1,0:T(8,128)S(1)}, f32[264,128]{1,0:T(8,128)S(1)}, u32[]{:S(2)}, u32[]{:S(2)}) collective-permute-start(f32[264,128]{1,0:T(8,128)S(1)} %get-tuple-element.30.refs_3_), channel_id=1, source_target_pairs={{0,4},{4,0},{8,12},{12,8},{1,5},{5,1},{9,13},{13,9},{2,6},{6,2},{1... | collective-permute-start | bytes 405512 | tf_op jit(solution)/shard_map/ppermute | solution.py:22
  15.9 14.5 %collective-permute-start.10 = (f32[256,128]{1,0:T(8,128)S(1)}, f32[256,128]{1,0:T(8,128)S(1)}, u32[]{:S(2)}, u32[]{:S(2)}) collective-permute-start(f32[256,128]{1,0:T(8,128)S(1)} %get-tuple-element.40.refs_7_), channel_id=1, source_target_pairs={{0,8},{4,12},{8,0},{12,4},{1,9},{5,13},{9,1},{13,5},{2,10},{6,14},... | collective-permute-start | bytes 393224 | tf_op jit(solution)/shard_map/ppermute | solution.py:22
  16.2 22.9 %copy-start.4 = (s32[40]{0:T(128)S(1)}, s32[40]{0:T(128)}, u32[]{:S(2)}) copy-start(s32[40]{0:T(128)} %refs_0_.5) | copy-start | bytes 484
  16.2 22.9 %copy-start.5 = (s32[40]{0:T(128)S(1)}, s32[40]{0:T(128)}, u32[]{:S(2)}) copy-start(s32[40]{0:T(128)} %refs_1_.5) | copy-start | bytes 484
  16.2 22.9 %copy-start.6 = (s32[40]{0:T(128)S(1)}, s32[40]{0:T(128)}, u32[]{:S(2)}) copy-start(s32[40]{0:T(128)} %refs_2_.5) | copy-start | bytes 484
  16.2 16.4 %collective-permute-start.16 = (f32[256,128]{1,0:T(8,128)S(1)}, f32[256,128]{1,0:T(8,128)S(1)}, u32[]{:S(2)}, u32[]{:S(2)}) collective-permute-start(f32[256,128]{1,0:T(8,128)S(1)} %get-tuple-element.45.refs_11_), channel_id=1, source_target_pairs={{0,8},{4,12},{8,0},{12,4},{1,9},{5,13},{9,1},{13,5},{2,10},{6,14},... | collective-permute-start | bytes 393224 | tf_op jit(solution)/shard_map/ppermute | solution.py:22
  22.1 17.0 %collective-permute-start.5 = (f32[264,128]{1,0:T(8,128)S(1)}, f32[264,128]{1,0:T(8,128)S(1)}, u32[]{:S(2)}, u32[]{:S(2)}) collective-permute-start(f32[264,128]{1,0:T(8,128)S(1)} %collective-permute-done.4.refs_5_), channel_id=1, source_target_pairs={{0,4},{4,0},{8,12},{12,8},{1,5},{5,1},{9,13},{13,9},{2,6},{6,2},{1... | collective-permute-start | bytes 405512 | tf_op jit(solution)/shard_map/ppermute | solution.py:22
  22.4 22.3 %collective-permute-start.9 = (f32[256,128]{1,0:T(8,128)S(1)}, f32[256,128]{1,0:T(8,128)S(1)}, u32[]{:S(2)}, u32[]{:S(2)}) collective-permute-start(f32[256,128]{1,0:T(8,128)S(1)} %get-tuple-element.40.refs_7_), channel_id=1, source_target_pairs={{0,4},{4,0},{8,12},{12,8},{1,5},{5,1},{9,13},{13,9},{2,6},{6,2},{1... | collective-permute-start | bytes 393224 | tf_op jit(solution)/shard_map/ppermute | solution.py:22
  30.4 15.7 %collective-permute-start.11 = (f32[256,128]{1,0:T(8,128)S(1)}, f32[256,128]{1,0:T(8,128)S(1)}, u32[]{:S(2)}, u32[]{:S(2)}) collective-permute-start(f32[256,128]{1,0:T(8,128)S(1)} %collective-permute-done.10.refs_9_), channel_id=1, source_target_pairs={{0,4},{4,0},{8,12},{12,8},{1,5},{5,1},{9,13},{13,9},{2,6},{6,2},{1... | collective-permute-start | bytes 393224 | tf_op jit(solution)/shard_map/ppermute | solution.py:22
  32.6 19.0 %collective-permute-start.15 = (f32[256,128]{1,0:T(8,128)S(1)}, f32[256,128]{1,0:T(8,128)S(1)}, u32[]{:S(2)}, u32[]{:S(2)}) collective-permute-start(f32[256,128]{1,0:T(8,128)S(1)} %get-tuple-element.45.refs_11_), channel_id=1, source_target_pairs={{0,4},{4,0},{8,12},{12,8},{1,5},{5,1},{9,13},{13,9},{2,6},{6,2},{1... | collective-permute-start | bytes 393224 | tf_op jit(solution)/shard_map/ppermute | solution.py:22
  33.3 19.8 %collective-permute-start.17 = (f32[256,128]{1,0:T(8,128)S(1)}, f32[256,128]{1,0:T(8,128)S(1)}, u32[]{:S(2)}, u32[]{:S(2)}) collective-permute-start(f32[256,128]{1,0:T(8,128)S(1)} %collective-permute-done.16.refs_13_), channel_id=1, source_target_pairs={{0,4},{4,0},{8,12},{12,8},{1,5},{5,1},{9,13},{13,9},{2,6},{6,2},{1... | collective-permute-start | bytes 393224 | tf_op jit(solution)/shard_map/ppermute | solution.py:22
  34.7 1.7 %copy-start = (f32[40,128,128]{2,1,0:T(8,128)S(1)}, f32[40,128,128]{2,1,0:T(8,128)}, u32[]{:S(2)}) copy-start(f32[40,128,128]{2,1,0:T(8,128)} %left_ref.1) | copy-start | bytes 7864324
  36.4 0.9 %copy-start.3 = (f32[4,128,128]{2,1,0:T(8,128)S(1)}, f32[4,128,128]{2,1,0:T(8,128)}, u32[]{:S(2)}) copy-start(f32[4,128,128]{2,1,0:T(8,128)} %right_ref.1) | copy-start | bytes 786436
  37.4 0.7 copy-start.7
  44.1 15.2 %collective-permute-start.6 = (f32[8,32,128]{2,1,0:T(8,128)S(1)}, f32[8,32,128]{2,1,0:T(8,128)S(1)}, u32[]{:S(2)}, u32[]{:S(2)}) collective-permute-start(f32[8,32,128]{2,1,0:T(8,128)S(1)} %get-tuple-element.38), channel_id=1, source_target_pairs={{0,4},{4,0},{8,12},{12,8},{1,5},{5,1},{9,13},{13,9},{2,6},{6,2},{1... | collective-permute-start | bytes 393224 | tf_op jit(solution)/shard_map/ppermute | solution.py:22
  44.7 23.8 %collective-permute-start.8 = (f32[8,32,128]{2,1,0:T(8,128)S(1)}, f32[8,32,128]{2,1,0:T(8,128)S(1)}, u32[]{:S(2)}, u32[]{:S(2)}) collective-permute-start(f32[8,32,128]{2,1,0:T(8,128)S(1)} %get-tuple-element.39), channel_id=1, source_target_pairs={{0,4},{4,0},{8,12},{12,8},{1,5},{5,1},{9,13},{13,9},{2,6},{6,2},{1... | collective-permute-start | bytes 393224 | tf_op jit(solution)/shard_map/ppermute | solution.py:22
  51.0 16.5 %collective-permute-start.12 = (f32[8,32,128]{2,1,0:T(8,128)S(1)}, f32[8,32,128]{2,1,0:T(8,128)S(1)}, u32[]{:S(2)}, u32[]{:S(2)}) collective-permute-start(f32[8,32,128]{2,1,0:T(8,128)S(1)} %get-tuple-element.43), channel_id=1, source_target_pairs={{0,4},{4,0},{8,12},{12,8},{1,5},{5,1},{9,13},{13,9},{2,6},{6,2},{1... | collective-permute-start | bytes 393224 | tf_op jit(solution)/shard_map/ppermute | solution.py:22
  51.7 11.1 %copy-start.2 = (f32[3,8,32,128]{3,2,1,0:T(8,128)S(1)}, f32[3,8,32,128]{3,2,1,0:T(8,128)}, u32[]{:S(2)}) copy-start(f32[3,8,32,128]{3,2,1,0:T(8,128)} %correction_ref.1) | copy-start | bytes 1179652
  51.7 19.0 %collective-permute-start.14 = (f32[8,32,128]{2,1,0:T(8,128)S(1)}, f32[8,32,128]{2,1,0:T(8,128)S(1)}, u32[]{:S(2)}, u32[]{:S(2)}) collective-permute-start(f32[8,32,128]{2,1,0:T(8,128)S(1)} %get-tuple-element.44), channel_id=1, source_target_pairs={{0,4},{4,0},{8,12},{12,8},{1,5},{5,1},{9,13},{13,9},{2,6},{6,2},{1... | collective-permute-start | bytes 393224 | tf_op jit(solution)/shard_map/ppermute | solution.py:22
  58.0 9.6 %collective-permute-start.18 = (f32[8,32,128]{2,1,0:T(8,128)S(1)}, f32[8,32,128]{2,1,0:T(8,128)S(1)}, u32[]{:S(2)}, u32[]{:S(2)}) collective-permute-start(f32[8,32,128]{2,1,0:T(8,128)S(1)} %get-tuple-element.48), channel_id=1, source_target_pairs={{0,4},{4,0},{8,12},{12,8},{1,5},{5,1},{9,13},{13,9},{2,6},{6,2},{1... | collective-permute-start | bytes 393224 | tf_op jit(solution)/shard_map/ppermute | solution.py:22
  59.3 11.4 %collective-permute-start.7 = (f32[8,32,128]{2,1,0:T(8,128)S(1)}, f32[8,32,128]{2,1,0:T(8,128)S(1)}, u32[]{:S(2)}, u32[]{:S(2)}) collective-permute-start(f32[8,32,128]{2,1,0:T(8,128)S(1)} %add.42), channel_id=1, source_target_pairs={{0,8},{4,12},{8,0},{12,4},{1,9},{5,13},{9,1},{13,5},{2,10},{6,14},... | collective-permute-start | bytes 393224 | tf_op jit(solution)/shard_map/ppermute | solution.py:22
  67.5 11.4 %collective-permute-start.20 = (f32[8,32,128]{2,1,0:T(8,128)S(1)}, f32[8,32,128]{2,1,0:T(8,128)S(1)}, u32[]{:S(2)}, u32[]{:S(2)}) collective-permute-start(f32[8,32,128]{2,1,0:T(8,128)S(1)} %get-tuple-element.49), channel_id=1, source_target_pairs={{0,4},{4,0},{8,12},{12,8},{1,5},{5,1},{9,13},{13,9},{2,6},{6,2},{1... | collective-permute-start | bytes 393224 | tf_op jit(solution)/shard_map/ppermute | solution.py:22
  67.6 11.2 %collective-permute-start.13 = (f32[8,32,128]{2,1,0:T(8,128)S(1)}, f32[8,32,128]{2,1,0:T(8,128)S(1)}, u32[]{:S(2)}, u32[]{:S(2)}) collective-permute-start(f32[8,32,128]{2,1,0:T(8,128)S(1)} %add.45), channel_id=1, source_target_pairs={{0,8},{4,12},{8,0},{12,4},{1,9},{5,13},{9,1},{13,5},{2,10},{6,14},... | collective-permute-start | bytes 393224 | tf_op jit(solution)/shard_map/ppermute | solution.py:22
  68.5 11.7 %collective-permute-start.19 = (f32[8,32,128]{2,1,0:T(8,128)S(1)}, f32[8,32,128]{2,1,0:T(8,128)S(1)}, u32[]{:S(2)}, u32[]{:S(2)}) collective-permute-start(f32[8,32,128]{2,1,0:T(8,128)S(1)} %add.48), channel_id=1, source_target_pairs={{0,8},{4,12},{8,0},{12,4},{1,9},{5,13},{9,1},{13,5},{2,10},{6,14},... | collective-permute-start | bytes 393224 | tf_op jit(solution)/shard_map/ppermute | solution.py:22

commit v2 on v0

v2 whole, which is shorter than its diff:
```python
import functools

import jax
import jax.numpy as jnp
from jax import lax
from jax.experimental import pallas as pl
from jax.experimental.pallas import tpu as pltpu
from jax.sharding import PartitionSpec as P

epsilon = 1e-06
vmem = pl.BlockSpec(memory_space=pltpu.VMEM)
smem = pl.BlockSpec(memory_space=pltpu.SMEM)
anywhere = pl.BlockSpec(memory_space=pl.ANY)
limit = pltpu.CompilerParams(vmem_limit_bytes=48 * 1024 * 1024)
pairs_of_three = ((0, 0), (0, 1), (0, 2), (1, 1), (1, 2), (2, 2))
f32, bf16 = jnp.float32, jnp.bfloat16
dot = functools.partial(jnp.dot, preferred_element_type=f32)
parcels = ((0,), (1, 2))


def ring_order(ops):
    return [0] + list(range(1, ops, 2)) + list(range(ops - 2, 0, -2))


def ring_step(value, ops):
    order = ring_order(ops)
    return lax.ppermute(value, "ops", [(order[i - 1], order[i]) for i in range(ops)])


def shard_before(place, ops, steps):
    at = jnp.where(place % 2 == 1, (place + 1) // 2, (ops - place // 2) % ops)
    at = (at - steps + ops) % ops
    return jnp.where(at == 0, 0, jnp.where(at <= ops // 2, 2 * at - 1, 2 * (ops - at)))


def holder_index():
    return lax.axis_index("sec") * lax.axis_size("rep") + lax.axis_index("rep")


def follow(value, others):
    return lax.optimization_barrier((value,) + tuple(others))[0] if others else value


def split(value):
    high = value.astype(bf16)
    return high, (value - high.astype(f32)).astype(bf16)


def pack_kernel(holders, table_ref, correction_ref, *outs):
    rows, width = correction_ref.shape[2:]
    cap = table_ref.shape[0]
    here = holder_index()
    for turn, vectors in enumerate(parcels):
        for mask in range(holders):
            out = outs[turn * holders + mask]
            for slot in range(cap):
                sector = table_ref[slot, here ^ mask]
                filled = (sector >= 0).astype(f32)
                sector = jnp.maximum(sector, 0)
                for index, vector in enumerate(vectors):
                    start = (index * cap + slot) * rows
                    out[start : start + rows, :] = correction_ref[vector, sector] * filled
    tiles = []
    for i, j in pairs_of_three:
        total = jnp.sum(correction_ref[i] * correction_ref[j], axis=(0, 1))[None, :]
        total = jnp.sum(total, axis=1, keepdims=True)
        tiles.append(jnp.broadcast_to(total, (1, width)))
    tiles.append(jnp.zeros((2, width), f32))
    gram = jnp.concatenate(tiles, axis=0)
    for mask in range(holders):
        outs[mask][outs[mask].shape[0] - 8 :, :] = gram


def join_kernel(holders, block, with_gram, *refs):
    received, outs = refs[:holders], refs[holders + 1 :]
    for index, out in enumerate(outs):
        for sender, part_ref in enumerate(received):
            out[sender * block : (sender + 1) * block, :] = part_ref[index * block : (index + 1) * block, :]
    if with_gram:
        outs[0][holders * block :, :] = sum(ref[ref.shape[0] - 8 :, :] for ref in received)


def plan_kernel(pairs, sectors, cap, terms, packed_ref, plan_ref, next_ref):
    width = 5
    couples = plan_ref.shape[0] // width
    base = holder_index() * cap
    for sector in range(sectors):
        next_ref[sector] = 0

    def count_step(pair, carry):
        target = packed_ref[pair] & (sectors - 1)
        next_ref[target] += 1
        return carry

    def clear_step(couple, carry):
        for entry in range(3):
            plan_ref[width * couple + entry] = 0
        plan_ref[width * couple + 3] = -1
        plan_ref[width * couple + 4] = -1
        return carry

    lax.fori_loop(0, pairs, count_step, 0, unroll=4)
    lax.fori_loop(0, couples, clear_step, 0, unroll=4)
    start = jnp.int32(0)
    for sector in range(sectors):
        count = next_ref[sector]
        next_ref[sector] = start
        start = start + ((count + 1) & -2)

    def place_step(pair, carry):
        packed = packed_ref[pair]
        target = packed & (sectors - 1)
        packed = packed >> (sectors.bit_length() - 1)
        at = next_ref[target]
        next_ref[target] = at + 1
        first, side = (at >> 1) * width, at & 1
        slot = (packed >> (terms.bit_length() - 1)) ^ base
        plan_ref[first + side] = slot * terms + (packed & (terms - 1))
        plan_ref[first + 2] = target
        plan_ref[first + 3 + side] = pair
        return carry

    lax.fori_loop(0, pairs, place_step, 0, unroll=4)


def operator_kernel(plan_ref, live_ref, left_ref, right_ref, high_ref, low_ref, right_both_ref, right_low_ref):
    width, terms = left_ref.shape[1], right_ref.shape[0]

    def couple_step(couple, carry):
        for side in range(2):
            pair = plan_ref[5 * couple + 3 + side]
            kept = jnp.where(pair >= 0, 1, 0)
            pair = jnp.maximum(pair, 0)
            scale = (live_ref[pair] * kept).astype(f32)
            high, low = split(left_ref[pair] * scale)
            high_ref[couple, :, side * width : (side + 1) * width] = high
            low_ref[couple, :, side * width : (side + 1) * width] = low
        return carry

    lax.fori_loop(0, high_ref.shape[0], couple_step, 0, unroll=4)
    for term in range(terms):
        high, low = split(right_ref[term].T)
        columns = slice(term * width, (term + 1) * width)
        right_both_ref[:width, columns] = high
        right_both_ref[width:, columns] = high
        right_low_ref[:, columns] = low


def inverse_rows(gram, entry_count):
    row = [gram[i : i + 1, :] / entry_count for i in range(6)]
    u_zero = jnp.sqrt(row[0] + epsilon)
    u_one = row[1] / u_zero
    u_two = row[2] / u_zero
    u_four = jnp.sqrt(row[3] + epsilon - u_one * u_one)
    u_five = (row[4] - u_one * u_two) / u_four
    u_eight = jnp.sqrt(row[5] + epsilon - u_two * u_two - u_five * u_five)
    v_zero = 1.0 / u_zero
    v_four = 1.0 / u_four
    v_eight = 1.0 / u_eight
    v_one = -u_one * v_zero * v_four
    v_five = -u_five * v_four * v_eight
    v_two = -(u_one * v_five + u_two * v_eight) * v_zero
    return [v_zero, v_one, v_two, v_four, v_five, v_eight]


def apply_kernel(vector, ops, rows, entry_count, *refs):
    refs = list(refs)
    take = lambda count: [refs.pop(0) for _ in range(count)]
    plan_ref, high_ref, low_ref, right_both_ref, right_low_ref = take(5)
    pieces = [take(ops) for _ in range(vector + 1)]
    inverse_in = take(1)[0] if vector else None
    outs = take(ops)
    inverse_out = None if vector else take(1)[0]
    source_ref, chosen_ref, total_ref = refs
    place = lax.axis_index("ops")
    slots, width, _ = source_ref.shape
    terms = right_low_ref.shape[1] // width
    count = slots * rows
    if vector:
        inverse = inverse_in[...]
    else:
        gram = sum(piece[count:, :] for piece in pieces[0])
        inverse = jnp.concatenate(inverse_rows(gram, entry_count) + [gram[6:]], axis=0)
        inverse_out[...] = inverse
    for steps in range(ops):
        value = 0.0
        for earlier in range(vector + 1):
            at = pairs_of_three.index((earlier, vector))
            value += pieces[earlier][steps][:count, :] * inverse[at : at + 1, :]
        start = pl.multiple_of(shard_before(place, ops, steps) * rows, rows)
        source_ref[:, pl.ds(start, rows), :] = value.reshape(slots, rows, width)

    def right_step(slot, carry):
        high, low = split(source_ref[slot])
        product = dot(jnp.concatenate([high, low], axis=1), right_both_ref[...])
        product += dot(high, right_low_ref[...])
        for term in range(terms):
            high, low = split(product[:, term * width : (term + 1) * width])
            chosen_ref[slot * terms + term, :, :width] = high
            chosen_ref[slot * terms + term, :, width:] = low
        return carry

    lax.fori_loop(0, slots, right_step, 0, unroll=8)
    total_ref[...] = jnp.zeros_like(total_ref)

    def couple_step(couple, carry):
        first, second = plan_ref[5 * couple], plan_ref[5 * couple + 1]
        chosen = jnp.concatenate([chosen_ref[first], chosen_ref[second]], axis=0)
        both = dot(high_ref[couple], chosen)
        rest = dot(low_ref[couple], chosen[:, :width])
        total_ref[plan_ref[5 * couple + 2]] += both[:, :width] + both[:, width:] + rest
        return carry

    lax.fori_loop(0, high_ref.shape[0], couple_step, 0, unroll=True)
    for steps in range(ops):
        start = pl.multiple_of(shard_before(place, ops, steps) * rows, rows)
        outs[steps][...] = total_ref[:, pl.ds(start, rows), :]


def basis_kernel(inverse_ref, correction_ref, out_ref):
    inverse = inverse_ref[...]
    for k in range(out_ref.shape[0]):
        picked = [(i, j) for i, (j, column) in enumerate(pairs_of_three) if column == k]
        out_ref[k] = sum(correction_ref[j] * inverse[i : i + 1, :] for i, j in picked)


def finish_kernel(*refs):
    out, terms = refs[-1], refs[:-1]
    for vector in range(out.shape[0]):
        out[vector] = terms[2 * vector][...] + terms[2 * vector + 1][...]


def call(kernel, out, inputs, specs, out_specs, name, scratch=()):
    return pl.pallas_call(
        kernel,
        out_shape=[jax.ShapeDtypeStruct(shape, dtype) for shape, dtype in out],
        in_specs=specs,
        out_specs=out_specs,
        scratch_shapes=list(scratch),
        compiler_params=limit,
        name=name,
    )(*inputs)


def local(
    correction, left_blocks, right_blocks, send_sector, pair_slot, pair_term, pair_dst, pair_live
):
    ops, holders = lax.axis_size("ops"), lax.axis_size(("sec", "rep"))
    vectors, sectors, rows, width = correction.shape
    cap = send_sector.shape[2]
    terms, pairs = right_blocks.shape[0], left_blocks.shape[0]
    slots, block = holders * cap, cap * rows
    entry_count = float(sectors * holders * width * width)
    couples = (pairs + min(pairs, sectors)) // 2

    packed = call(
        functools.partial(pack_kernel, holders),
        [
            ((len(parcel) * block + (0 if turn else 8), width), f32)
            for turn, parcel in enumerate(parcels)
            for _ in range(holders)
        ],
        (send_sector[0].T, correction),
        [smem, vmem],
        [vmem] * (len(parcels) * holders),
        "pack",
    )
    joined = []
    received = []
    for turn in range(len(parcels)):
        mine = list(packed[turn * holders : (turn + 1) * holders])
        for mask in range(holders - 1, 0, -1):
            mine[mask] = lax.ppermute(
                mine[mask], ("sec", "rep"), [(i, i ^ mask) for i in range(holders)]
            )
        received.append(mine)
    (plan,) = call(
        functools.partial(plan_kernel, pairs, sectors, cap, terms),
        [((5 * couples,), jnp.int32)],
        ((pair_slot * terms + pair_term) * sectors + pair_dst,),
        [smem],
        [smem],
        "plan",
        [pltpu.SMEM((sectors,), jnp.int32)],
    )
    for turn, parcel in enumerate(parcels):
        joined += call(
            functools.partial(join_kernel, holders, block, turn == 0),
            [
                ((slots * rows + (8 if turn == 0 and index == 0 else 0), width), f32)
                for index in range(len(parcel))
            ],
            received[turn] + [plan],
            [vmem] * holders + [anywhere],
            [vmem] * len(parcel),
            "join",
        )
    high, low, right_both, right_low = call(
        operator_kernel,
        [
            ((couples, width, 2 * width), bf16),
            ((couples, width, 2 * width), bf16),
            ((2 * width, terms * width), bf16),
            ((width, terms * width), bf16),
        ],
        (plan, pair_live, left_blocks, right_blocks),
        [smem] * 2 + [vmem] * 2,
        [vmem] * 4,
        "operators",
    )

    pieces = [[value] for value in joined]
    for step in range(1, ops):
        for vector in range(vectors):
            value = pieces[vector][-1]
            if vector == 0 and step == 2:
                value = follow(value, (right_low,))
            pieces[vector].append(ring_step(value, ops))

    inverse = None
    sums = []
    for vector in range(vectors):
        arguments = [plan, high, low, right_both, right_low]
        arguments += sum(pieces[: vector + 1], [])
        arguments += [inverse] if vector else []
        out = [((sectors, rows, width), f32)] * ops + ([] if vector else [((8, width), f32)])
        parts = call(
            functools.partial(apply_kernel, vector, ops, rows, entry_count),
            out,
            arguments,
            [smem] + [vmem] * (len(arguments) - 1),
            [vmem] * len(out),
            "apply",
            [
                pltpu.VMEM((slots, width, width), f32),
                pltpu.VMEM((slots * terms, width, 2 * width), bf16),
                pltpu.VMEM((sectors, width, width), f32),
            ],
        )
        if vector == 0:
            inverse = parts[ops]
            (search_basis,) = call(
                basis_kernel, [(correction.shape, f32)], (inverse, correction), [vmem] * 2, [vmem], "basis"
            )
        total = parts[1]
        for step in range(2, ops):
            if vector == 1 and step == 2:
                total = follow(total, (search_basis,))
            total = parts[step] + ring_step(total, ops)
        sums += [parts[0], ring_step(total, ops)]

    (sigma_blocks,) = call(
        finish_kernel,
        [(correction.shape, f32)],
        sums,
        [vmem] * len(sums),
        [vmem],
        "finish",
    )
    return (search_basis, sigma_blocks)


def solution(mesh):
    placed = (
        P(None, ("groups", "sec", "rep"), "ops", None),
        P(("groups", "ops", "sec", "rep"), None, None),
        P(("groups", "ops"), None, None),
        P(("groups", "sec", "rep"), None, None),
        P(("groups", "ops", "sec", "rep")),
        P(("groups", "ops", "sec", "rep")),
        P(("groups", "ops", "sec", "rep")),
        P(("groups", "ops", "sec", "rep")),
    )
    return jax.shard_map(
        local,
        mesh=mesh,
        in_specs=placed,
        out_specs=(
            P(None, ("groups", "sec", "rep"), "ops", None),
            P(None, ("groups", "sec", "rep"), "ops", None),
        ),
        check_vma=False,
    )
```

time: 225 us -> 71.4 us (0.32)
  waiting for transfers between devices: 91.8 us -> 27.1 us
  matrix products: 46.7 us -> 0 us
  blocking collectives: 34.9 us -> 0 us
  starting transfers between devices: 4.61 us -> 25.1 us
  local copies, waits for them, and re-layouts: 23.6 us -> 3.28 us
  between operations: 18.4 us -> 0.78 us
  Pallas kernels: 0 us -> 14 us
  other arithmetic: 4.73 us -> 0.81 us
    dot_general x11 -> x0, matrix products: 46.7 us -> none  [the longest x3 17.4 us: local(): jnp.einsum('pil,pml->pim', halfway, right_chosen, precision=highest)]
    all_gather x1 -> x0, waiting for transfers between devices: 41.7 us -> none  [local(): whole_rows = lax.all_gather(search_basis, 'ops', axis=2, tiled=True)]
    psum x1 -> x0, blocking collectives: 34.9 us -> none  [local(): gram_matrix = lax.psum(local_gram, ('ops', 'sec', 'rep')) / entry_count]
    unnamed x3 -> x0, waiting for transfers between devices: 32.5 us -> none
    ppermute x0 -> x24, waiting for transfers between devices: none -> 27.1 us  [the longest x18 26.8 us: ring_step(): lax.ppermute(value, 'ops', [(order[i - 1], order[i]) for i in range(ops)])]
    ppermute x0 -> x24, starting transfers between devices: none -> 25.1 us  [the longest x18 19.9 us: ring_step(): lax.ppermute(value, 'ops', [(order[i - 1], order[i]) for i in range(ops)])]
    all_to_all x1 -> x0, waiting for transfers between devices: 17.6 us -> none  [local(): lax.all_to_all(taken * filled[None, :, :, None, None], ('sec', 'rep'), sp...]
    gather x5 -> x0, local copies, waits for them, and re-layouts: 15.5 us -> none  [the longest x3 8.73 us: local(): source = received[vector][pair_slot]]
  transfers between devices with their start and end apart: 3 -> 24, of which waited for: 3 -> 15; matrix products, arithmetic and copies ran while one was open for 2% -> 1% of each run, Pallas kernels for 0% -> 18%
where the time goes in v2:
time: 71.4 us; the launch traced here: 71.1 us
  waiting for transfers between devices  27.1 us (38%)
  starting transfers between devices  25.1 us (35%)
  Pallas kernels  14 us (20%)
  local copies, waits for them, and re-layouts  3.28 us (5%)
  other arithmetic  0.81 us (1%)
  between operations  0.78 us (1%)
    ppermute x18, waiting for transfers between devices, ring_step(): lax.ppermute(value, 'ops', [(order[i - 1], order[i]) for i in range(ops)])  26.8 us
    ppermute x18, starting transfers between devices, ring_step(): lax.ppermute(value, 'ops', [(order[i - 1], order[i]) for i in range(ops)])  19.9 us
    pallas_call x10, Pallas kernels, call(): pl.pallas_call(kernel, out_shape=[jax.ShapeDtypeStruct(shape, dtype) for...  14 us
    ppermute x6, starting transfers between devices, local(): lax.ppermute(mine[mask], ('sec', 'rep'), [(i, i ^ mask) for i in range(ho...  5.2 us
    unnamed x10, local copies, waits for them, and re-layouts  3.28 us
  transfers between devices with their start and end apart: 24, of which 15 were waited for; matrix products, arithmetic and copies ran while one was open for 1% of the time, Pallas kernels for 18%

profile of v2, /device:TPU:0, one launch (start us, length us, event | category | flops | bytes accessed | tf_op | source)
XLA Modules:
  0.0 71.1 jit_solution(14288207525308159101)
XLA Ops:
  0.6 1.0 %copy-done = f32[3,8,32,128]{3,2,1,0:T(8,128)S(1)} copy-done((f32[3,8,32,128]{3,2,1,0:T(8,128)S(1)}, f32[3,8,32,128]{3,2,1,0:T(8,128)}, u32[]{:S(2)}) %copy-start) | copy-done | bytes 393240
  1.6 0.7 copy-done.3
  2.3 0.7 pack.1
  3.0 0.5 collective-permute-start
  3.5 2.6 %collective-permute-start.1 = (f32[72,128]{1,0:T(8,128)S(1)}, f32[72,128]{1,0:T(8,128)S(1)}, u32[]{:S(2)}, u32[]{:S(2)}) collective-permute-start(f32[72,128]{1,0:T(8,128)S(1)} %get-tuple-element.37), channel_id=1, source_target_pairs={{0,2},{1,3},{2,0},{3,1},{4,6},{5,7},{6,4},{7,5},{8,10},{9,11},{10,... | collective-permute-start | bytes 110600 | tf_op jit(solution)/shard_map/ppermute | solution.py:273
  6.1 0.1 collective-permute-start.2
  6.1 0.1 collective-permute-start.9
  6.3 1.9 %collective-permute-start.10 = (f32[128,128]{1,0:T(8,128)S(1)}, f32[128,128]{1,0:T(8,128)S(1)}, u32[]{:S(2)}, u32[]{:S(2)}) collective-permute-start(f32[128,128]{1,0:T(8,128)S(1)} %get-tuple-element.47), channel_id=1, source_target_pairs={{0,2},{1,3},{2,0},{3,1},{4,6},{5,7},{6,4},{7,5},{8,10},{9,11},{10,... | collective-permute-start | bytes 196616 | tf_op jit(solution)/shard_map/ppermute | solution.py:273
  8.2 0.7 multiply_add_fusion.packed_ref
  8.9 1.8 %plan.1.plan_ref.refs_4_.refs_0_ = s32[120]{0:T(128)S(1)} custom-call(s32[40]{0:T(128)S(1)} %multiply_add_fusion.packed_ref), custom_call_target="tpu_custom_call" | custom-call | tf_op jit(solution)/shard_map/plan/pallas_call | solution.py:234
  10.7 1.7 %collective-permute-start.3 = (f32[264,128]{1,0:T(8,128)S(1)}, f32[264,128]{1,0:T(8,128)S(1)}, u32[]{:S(2)}, u32[]{:S(2)}) collective-permute-start(f32[264,128]{1,0:T(8,128)S(1)} %join.2.refs_5_), channel_id=1, source_target_pairs={{8,0},{0,4},{4,12},{12,8},{9,1},{1,5},{5,13},{13,9},{10,2},{2,6},{... | collective-permute-start | bytes 405512 | tf_op jit(solution)/shard_map/ppermute | solution.py:27
  12.4 0.2 collective-permute-done.11.refs_3_
  12.6 2.4 %collective-permute-start.18 = (f32[256,128]{1,0:T(8,128)S(1)}, f32[256,128]{1,0:T(8,128)S(1)}, u32[]{:S(2)}, u32[]{:S(2)}) collective-permute-start(f32[256,128]{1,0:T(8,128)S(1)} %get-tuple-element.55.refs_13_), channel_id=1, source_target_pairs={{8,0},{0,4},{4,12},{12,8},{9,1},{1,5},{5,13},{13,9},{10,2},{2,6},{... | collective-permute-start | bytes 393224 | tf_op jit(solution)/shard_map/ppermute | solution.py:27
  15.1 1.8 %collective-permute-start.12 = (f32[256,128]{1,0:T(8,128)S(1)}, f32[256,128]{1,0:T(8,128)S(1)}, u32[]{:S(2)}, u32[]{:S(2)}) collective-permute-start(f32[256,128]{1,0:T(8,128)S(1)} %get-tuple-element.49.refs_9_), channel_id=1, source_target_pairs={{8,0},{0,4},{4,12},{12,8},{9,1},{1,5},{5,13},{13,9},{10,2},{2,6},{... | collective-permute-start | bytes 393224 | tf_op jit(solution)/shard_map/ppermute | solution.py:27
  16.8 0.9 %copy-done.2 = f32[4,128,128]{2,1,0:T(8,128)S(1)} copy-done((f32[4,128,128]{2,1,0:T(8,128)S(1)}, f32[4,128,128]{2,1,0:T(8,128)}, u32[]{:S(2)}) %copy-start.2) | copy-done | bytes 262168
  17.8 0.7 copy-done.4
  18.4 2.6 %operators.1 = (bf16[24,128,256]{2,1,0:T(8,128)(2,1)S(1)}, bf16[24,128,256]{2,1,0:T(8,128)(2,1)S(1)}, bf16[256,512]{1,0:T(8,128)(2,1)S(1)}, bf16[128,512]{1,0:T(8,128)(2,1)S(1)}) custom-call(s32[120]{0:T(128)S(1)} %plan.1.plan_ref.refs_4_.refs_0_, s32[40]{0:T(128)S(1)} %copy-done.4, f32[40,128,128]{2,1,0:T(8,128)} %left_ref.1, f32[4,128,128]{2,1,0:T(8,128)S(1)} %copy-done.2), custom_call_target="tpu_custom_call" | custom-call | tf_op jit(solution)/shard_map/operators/pallas_call | solution.py:234
  21.0 0.5 collective-permute-start.4
  21.5 0.7 collective-permute-start.19
  22.2 1.1 %collective-permute-done.12.refs_10_ = f32[256,128]{1,0:T(8,128)S(1)} collective-permute-done((f32[256,128]{1,0:T(8,128)S(1)}, f32[256,128]{1,0:T(8,128)S(1)}, u32[]{:S(2)}, u32[]{:S(2)}) %collective-permute-start.12) | collective-permute-done | bytes 131104 | tf_op jit(solution)/shard_map/ppermute | solution.py:27
  23.4 1.7 %collective-permute-start.13 = (f32[256,128]{1,0:T(8,128)S(1)}, f32[256,128]{1,0:T(8,128)S(1)}, u32[]{:S(2)}, u32[]{:S(2)}) collective-permute-start(f32[256,128]{1,0:T(8,128)S(1)} %collective-permute-done.12.refs_10_), channel_id=1, source_target_pairs={{8,0},{0,4},{4,12},{12,8},{9,1},{1,5},{5,13},{13,9},{10,2},{2,6},{... | collective-permute-start | bytes 393224 | tf_op jit(solution)/shard_map/ppermute | solution.py:27
  25.0 3.5 %collective-permute-done.4.refs_7_ = f32[264,128]{1,0:T(8,128)S(1)} collective-permute-done((f32[264,128]{1,0:T(8,128)S(1)}, f32[264,128]{1,0:T(8,128)S(1)}, u32[]{:S(2)}, u32[]{:S(2)}) %collective-permute-start.4) | collective-permute-done | bytes 135200 | tf_op jit(solution)/shard_map/ppermute | solution.py:27
  28.5 2.8 %collective-permute-done.19.refs_15_ = f32[256,128]{1,0:T(8,128)S(1)} collective-permute-done((f32[256,128]{1,0:T(8,128)S(1)}, f32[256,128]{1,0:T(8,128)S(1)}, u32[]{:S(2)}, u32[]{:S(2)}) %collective-permute-start.19) | collective-permute-done | bytes 131104 | tf_op jit(solution)/shard_map/ppermute | solution.py:27
  31.3 2.8 %collective-permute-done.13.refs_11_ = f32[256,128]{1,0:T(8,128)S(1)} collective-permute-done((f32[256,128]{1,0:T(8,128)S(1)}, f32[256,128]{1,0:T(8,128)S(1)}, u32[]{:S(2)}, u32[]{:S(2)}) %collective-permute-start.13) | collective-permute-done | bytes 131104 | tf_op jit(solution)/shard_map/ppermute | solution.py:27
  34.1 2.9 %collective-permute-done.5.refs_8_ = f32[264,128]{1,0:T(8,128)S(1)} collective-permute-done((f32[264,128]{1,0:T(8,128)S(1)}, f32[264,128]{1,0:T(8,128)S(1)}, u32[]{:S(2)}, u32[]{:S(2)}) %collective-permute-start.5) | collective-permute-done | bytes 135200 | tf_op jit(solution)/shard_map/ppermute | solution.py:27
  37.0 2.4 %apply.3 = (f32[8,32,128]{2,1,0:T(8,128)S(1)}, f32[8,32,128]{2,1,0:T(8,128)S(1)}, f32[8,32,128]{2,1,0:T(8,128)S(1)}, f32[8,32,128]{2,1,0:T(8,128)S(1)}, f32[8,128]{1,0:T(8,128)S(1)}) custom-call(s32[120]{0:T(128)S(1)} %plan.1.plan_ref.refs_4_.refs_0_, bf16[24,128,256]{2,1,0:T(8,128)(2,1)S(1)} %get-tuple-element.31.refs_1_, ...), custom_call_target="tpu_custom_call" | custom-call | tf_op jit(solution)/shard_map/apply/pallas_call | solution.py:234
  39.5 0.1 collective-permute-start.6
  39.5 0.8 %basis.1 = f32[3,8,32,128]{3,2,1,0:T(8,128)} custom-call(f32[8,128]{1,0:T(8,128)S(1)} %get-tuple-element.40.inverse_ref.refs_13_.refs_17_, f32[3,8,32,128]{3,2,1,0:T(8,128)S(1)} %copy-done.1), custom_call_target="tpu_custom_call" | custom-call | tf_op jit(solution)/shard_map/basis/pallas_call | solution.py:234
  40.3 1.7 %collective-permute-done.14.refs_12_ = f32[256,128]{1,0:T(8,128)S(1)} collective-permute-done((f32[256,128]{1,0:T(8,128)S(1)}, f32[256,128]{1,0:T(8,128)S(1)}, u32[]{:S(2)}, u32[]{:S(2)}) %collective-permute-start.14) | collective-permute-done | bytes 131104 | tf_op jit(solution)/shard_map/ppermute | solution.py:27
  42.1 2.5 %apply.5 = (f32[8,32,128]{2,1,0:T(8,128)S(1)}, f32[8,32,128]{2,1,0:T(8,128)S(1)}, f32[8,32,128]{2,1,0:T(8,128)S(1)}, f32[8,32,128]{2,1,0:T(8,128)S(1)}) custom-call(s32[120]{0:T(128)S(1)} %plan.1.plan_ref.refs_4_.refs_0_, bf16[24,128,256]{2,1,0:T(8,128)(2,1)S(1)} %get-tuple-element.31.refs_1_, bf16[24,128,256]{2,1,0:T(8,128)(2,1)S(1)} %get-tuple-element.32.refs_2_, ...), custom_call_target="tpu_custom_call" | custom-call | tf_op jit(solution)/shard_map/apply/pallas_call | solution.py:234
  44.6 0.6 collective-permute-start.21
  45.1 2.4 %apply.4 = (f32[8,32,128]{2,1,0:T(8,128)S(1)}, f32[8,32,128]{2,1,0:T(8,128)S(1)}, f32[8,32,128]{2,1,0:T(8,128)S(1)}, f32[8,32,128]{2,1,0:T(8,128)S(1)}) custom-call(s32[120]{0:T(128)S(1)} %plan.1.plan_ref.refs_4_.refs_0_, bf16[24,128,256]{2,1,0:T(8,128)(2,1)S(1)} %get-tuple-element.31.refs_1_, bf16[24,128,256]{2,1,0:T(8,128)(2,1)S(1)} %get-tuple-element.32.refs_2_, ...), custom_call_target="tpu_custom_call" | custom-call | tf_op jit(solution)/shard_map/apply/pallas_call | solution.py:234
  47.6 2.1 %collective-permute-start.15 = (f32[8,32,128]{2,1,0:T(8,128)S(1)}, f32[8,32,128]{2,1,0:T(8,128)S(1)}, u32[]{:S(2)}, u32[]{:S(2)}) collective-permute-start(f32[8,32,128]{2,1,0:T(8,128)S(1)} %get-tuple-element.54), channel_id=1, source_target_pairs={{8,0},{0,4},{4,12},{12,8},{9,1},{1,5},{5,13},{13,9},{10,2},{2,6},{... | collective-permute-start | bytes 393224 | tf_op jit(solution)/shard_map/ppermute | solution.py:27
  49.7 0.7 %collective-permute-start.7 = (f32[8,32,128]{2,1,0:T(8,128)S(1)}, f32[8,32,128]{2,1,0:T(8,128)S(1)}, u32[]{:S(2)}, u32[]{:S(2)}) collective-permute-start(f32[8,32,128]{2,1,0:T(8,128)S(1)} %add.26), channel_id=1, source_target_pairs={{8,0},{0,4},{4,12},{12,8},{9,1},{1,5},{5,13},{13,9},{10,2},{2,6},{... | collective-permute-start | bytes 393224 | tf_op jit(solution)/shard_map/ppermute | solution.py:27
  50.4 0.4 collective-permute-done.21
  50.8 1.4 %collective-permute-start.22 = (f32[8,32,128]{2,1,0:T(8,128)S(1)}, f32[8,32,128]{2,1,0:T(8,128)S(1)}, u32[]{:S(2)}, u32[]{:S(2)}) collective-permute-start(f32[8,32,128]{2,1,0:T(8,128)S(1)} %add.30), channel_id=1, source_target_pairs={{8,0},{0,4},{4,12},{12,8},{9,1},{1,5},{5,13},{13,9},{10,2},{2,6},{... | collective-permute-start | bytes 393224 | tf_op jit(solution)/shard_map/ppermute | solution.py:27
  52.2 2.3 %collective-permute-done.15 = f32[8,32,128]{2,1,0:T(8,128)S(1)} collective-permute-done((f32[8,32,128]{2,1,0:T(8,128)S(1)}, f32[8,32,128]{2,1,0:T(8,128)S(1)}, u32[]{:S(2)}, u32[]{:S(2)}) %collective-permute-start.15) | collective-permute-done | bytes 131104 | tf_op jit(solution)/shard_map/ppermute | solution.py:27
  54.6 1.6 %collective-permute-start.16 = (f32[8,32,128]{2,1,0:T(8,128)S(1)}, f32[8,32,128]{2,1,0:T(8,128)S(1)}, u32[]{:S(2)}, u32[]{:S(2)}) collective-permute-start(f32[8,32,128]{2,1,0:T(8,128)S(1)} %add.28), channel_id=1, source_target_pairs={{8,0},{0,4},{4,12},{12,8},{9,1},{1,5},{5,13},{13,9},{10,2},{2,6},{... | collective-permute-start | bytes 393224 | tf_op jit(solution)/shard_map/ppermute | solution.py:27
  56.2 1.2 %collective-permute-done.7 = f32[8,32,128]{2,1,0:T(8,128)S(1)} collective-permute-done((f32[8,32,128]{2,1,0:T(8,128)S(1)}, f32[8,32,128]{2,1,0:T(8,128)S(1)}, u32[]{:S(2)}, u32[]{:S(2)}) %collective-permute-start.7) | collective-permute-done | bytes 131104 | tf_op jit(solution)/shard_map/ppermute | solution.py:27
  57.4 1.6 %collective-permute-start.8 = (f32[8,32,128]{2,1,0:T(8,128)S(1)}, f32[8,32,128]{2,1,0:T(8,128)S(1)}, u32[]{:S(2)}, u32[]{:S(2)}) collective-permute-start(f32[8,32,128]{2,1,0:T(8,128)S(1)} %add.27), channel_id=1, source_target_pairs={{8,0},{0,4},{4,12},{12,8},{9,1},{1,5},{5,13},{13,9},{10,2},{2,6},{... | collective-permute-start | bytes 393224 | tf_op jit(solution)/shard_map/ppermute | solution.py:27
  59.0 1.2 %collective-permute-done.22 = f32[8,32,128]{2,1,0:T(8,128)S(1)} collective-permute-done((f32[8,32,128]{2,1,0:T(8,128)S(1)}, f32[8,32,128]{2,1,0:T(8,128)S(1)}, u32[]{:S(2)}, u32[]{:S(2)}) %collective-permute-start.22) | collective-permute-done | bytes 131104 | tf_op jit(solution)/shard_map/ppermute | solution.py:27
  60.2 1.6 %collective-permute-start.23 = (f32[8,32,128]{2,1,0:T(8,128)S(1)}, f32[8,32,128]{2,1,0:T(8,128)S(1)}, u32[]{:S(2)}, u32[]{:S(2)}) collective-permute-start(f32[8,32,128]{2,1,0:T(8,128)S(1)} %add.31), channel_id=1, source_target_pairs={{8,0},{0,4},{4,12},{12,8},{9,1},{1,5},{5,13},{13,9},{10,2},{2,6},{... | collective-permute-start | bytes 393224 | tf_op jit(solution)/shard_map/ppermute | solution.py:27
  61.8 1.2 %collective-permute-done.16 = f32[8,32,128]{2,1,0:T(8,128)S(1)} collective-permute-done((f32[8,32,128]{2,1,0:T(8,128)S(1)}, f32[8,32,128]{2,1,0:T(8,128)S(1)}, u32[]{:S(2)}, u32[]{:S(2)}) %collective-permute-start.16) | collective-permute-done | bytes 131104 | tf_op jit(solution)/shard_map/ppermute | solution.py:27
  63.0 1.6 %collective-permute-start.17 = (f32[8,32,128]{2,1,0:T(8,128)S(1)}, f32[8,32,128]{2,1,0:T(8,128)S(1)}, u32[]{:S(2)}, u32[]{:S(2)}) collective-permute-start(f32[8,32,128]{2,1,0:T(8,128)S(1)} %add.29), channel_id=1, source_target_pairs={{8,0},{0,4},{4,12},{12,8},{9,1},{1,5},{5,13},{13,9},{10,2},{2,6},{... | collective-permute-start | bytes 393224 | tf_op jit(solution)/shard_map/ppermute | solution.py:27
  64.6 1.2 %collective-permute-done.8.refs_1_ = f32[8,32,128]{2,1,0:T(8,128)S(1)} collective-permute-done((f32[8,32,128]{2,1,0:T(8,128)S(1)}, f32[8,32,128]{2,1,0:T(8,128)S(1)}, u32[]{:S(2)}, u32[]{:S(2)}) %collective-permute-start.8) | collective-permute-done | bytes 131104 | tf_op jit(solution)/shard_map/ppermute | solution.py:27
  65.8 2.8 %collective-permute-done.23.refs_5_ = f32[8,32,128]{2,1,0:T(8,128)S(1)} collective-permute-done((f32[8,32,128]{2,1,0:T(8,128)S(1)}, f32[8,32,128]{2,1,0:T(8,128)S(1)}, u32[]{:S(2)}, u32[]{:S(2)}) %collective-permute-start.23) | collective-permute-done | bytes 131104 | tf_op jit(solution)/shard_map/ppermute | solution.py:27
  68.6 1.8 %collective-permute-done.17.refs_3_ = f32[8,32,128]{2,1,0:T(8,128)S(1)} collective-permute-done((f32[8,32,128]{2,1,0:T(8,128)S(1)}, f32[8,32,128]{2,1,0:T(8,128)S(1)}, u32[]{:S(2)}, u32[]{:S(2)}) %collective-permute-start.17) | collective-permute-done | bytes 131104 | tf_op jit(solution)/shard_map/ppermute | solution.py:27
  70.3 0.8 %finish.1 = f32[3,8,32,128]{3,2,1,0:T(8,128)} custom-call(f32[8,32,128]{2,1,0:T(8,128)S(1)} %get-tuple-element.41.refs_0_, f32[8,32,128]{2,1,0:T(8,128)S(1)} %collective-permute-done.8.refs_1_, f32[8,32,128]{2,1,0:T(8,128)S(1)} %get-tuple-element.50.refs_2_, f32[8,32,128]{2,1,0:T(8,128)S(1)} %collective-permute-done.17.refs_3_, ...), custom_call_target="tpu_custom_call" | custom-call | tf_op jit(solution)/shard_map/finish/pallas_call | solution.py:234
  (27 shorter events, 0.2 us)
Async XLA Ops:
  0.6 1.0 %copy-start = (f32[3,8,32,128]{3,2,1,0:T(8,128)S(1)}, f32[3,8,32,128]{3,2,1,0:T(8,128)}, u32[]{:S(2)}) copy-start(f32[3,8,32,128]{3,2,1,0:T(8,128)} %correction_ref.3) | copy-start | bytes 1179652
  1.6 0.7 copy-start.3
  3.0 5.2 %collective-permute-start = (f32[72,128]{1,0:T(8,128)S(1)}, f32[72,128]{1,0:T(8,128)S(1)}, u32[]{:S(2)}, u32[]{:S(2)}) collective-permute-start(f32[72,128]{1,0:T(8,128)S(1)} %get-tuple-element.36), channel_id=1, source_target_pairs={{0,1},{1,0},{2,3},{3,2},{4,5},{5,4},{6,7},{7,6},{8,9},{9,8},{10,11... | collective-permute-start | bytes 110600 | tf_op jit(solution)/shard_map/ppermute | solution.py:273
  3.5 7.2 %collective-permute-start.1 = (f32[72,128]{1,0:T(8,128)S(1)}, f32[72,128]{1,0:T(8,128)S(1)}, u32[]{:S(2)}, u32[]{:S(2)}) collective-permute-start(f32[72,128]{1,0:T(8,128)S(1)} %get-tuple-element.37), channel_id=1, source_target_pairs={{0,2},{1,3},{2,0},{3,1},{4,6},{5,7},{6,4},{7,5},{8,10},{9,11},{10,... | collective-permute-start | bytes 110600 | tf_op jit(solution)/shard_map/ppermute | solution.py:273
  6.1 4.6 %collective-permute-start.2 = (f32[72,128]{1,0:T(8,128)S(1)}, f32[72,128]{1,0:T(8,128)S(1)}, u32[]{:S(2)}, u32[]{:S(2)}) collective-permute-start(f32[72,128]{1,0:T(8,128)S(1)} %get-tuple-element.38), channel_id=1, source_target_pairs={{0,3},{1,2},{2,1},{3,0},{4,7},{5,6},{6,5},{7,4},{8,11},{9,10},{10,... | collective-permute-start | bytes 110600 | tf_op jit(solution)/shard_map/ppermute | solution.py:273
  6.1 6.3 %collective-permute-start.9 = (f32[128,128]{1,0:T(8,128)S(1)}, f32[128,128]{1,0:T(8,128)S(1)}, u32[]{:S(2)}, u32[]{:S(2)}) collective-permute-start(f32[128,128]{1,0:T(8,128)S(1)} %get-tuple-element.46), channel_id=1, source_target_pairs={{0,1},{1,0},{2,3},{3,2},{4,5},{5,4},{6,7},{7,6},{8,9},{9,8},{10,11... | collective-permute-start | bytes 196616 | tf_op jit(solution)/shard_map/ppermute | solution.py:273
  6.3 6.1 %collective-permute-start.10 = (f32[128,128]{1,0:T(8,128)S(1)}, f32[128,128]{1,0:T(8,128)S(1)}, u32[]{:S(2)}, u32[]{:S(2)}) collective-permute-start(f32[128,128]{1,0:T(8,128)S(1)} %get-tuple-element.47), channel_id=1, source_target_pairs={{0,2},{1,3},{2,0},{3,1},{4,6},{5,7},{6,4},{7,5},{8,10},{9,11},{10,... | collective-permute-start | bytes 196616 | tf_op jit(solution)/shard_map/ppermute | solution.py:273
  8.2 4.4 %collective-permute-start.11 = (f32[128,128]{1,0:T(8,128)S(1)}, f32[128,128]{1,0:T(8,128)S(1)}, u32[]{:S(2)}, u32[]{:S(2)}) collective-permute-start(f32[128,128]{1,0:T(8,128)S(1)} %get-tuple-element.48), channel_id=1, source_target_pairs={{0,3},{1,2},{2,1},{3,0},{4,7},{5,6},{6,5},{7,4},{8,11},{9,10},{10,... | collective-permute-start | bytes 196616 | tf_op jit(solution)/shard_map/ppermute | solution.py:273
  10.7 10.3 %collective-permute-start.3 = (f32[264,128]{1,0:T(8,128)S(1)}, f32[264,128]{1,0:T(8,128)S(1)}, u32[]{:S(2)}, u32[]{:S(2)}) collective-permute-start(f32[264,128]{1,0:T(8,128)S(1)} %join.2.refs_5_), channel_id=1, source_target_pairs={{8,0},{0,4},{4,12},{12,8},{9,1},{1,5},{5,13},{13,9},{10,2},{2,6},{... | collective-permute-start | bytes 405512 | tf_op jit(solution)/shard_map/ppermute | solution.py:27
  12.6 8.9 %collective-permute-start.18 = (f32[256,128]{1,0:T(8,128)S(1)}, f32[256,128]{1,0:T(8,128)S(1)}, u32[]{:S(2)}, u32[]{:S(2)}) collective-permute-start(f32[256,128]{1,0:T(8,128)S(1)} %get-tuple-element.55.refs_13_), channel_id=1, source_target_pairs={{8,0},{0,4},{4,12},{12,8},{9,1},{1,5},{5,13},{13,9},{10,2},{2,6},{... | collective-permute-start | bytes 393224 | tf_op jit(solution)/shard_map/ppermute | solution.py:27
  15.1 8.3 %collective-permute-start.12 = (f32[256,128]{1,0:T(8,128)S(1)}, f32[256,128]{1,0:T(8,128)S(1)}, u32[]{:S(2)}, u32[]{:S(2)}) collective-permute-start(f32[256,128]{1,0:T(8,128)S(1)} %get-tuple-element.49.refs_9_), channel_id=1, source_target_pairs={{8,0},{0,4},{4,12},{12,8},{9,1},{1,5},{5,13},{13,9},{10,2},{2,6},{... | collective-permute-start | bytes 393224 | tf_op jit(solution)/shard_map/ppermute | solution.py:27
  16.8 0.9 %copy-start.2 = (f32[4,128,128]{2,1,0:T(8,128)S(1)}, f32[4,128,128]{2,1,0:T(8,128)}, u32[]{:S(2)}) copy-start(f32[4,128,128]{2,1,0:T(8,128)} %right_ref.1) | copy-start | bytes 786436
  17.8 0.7 copy-start.4
  21.0 7.5 %collective-permute-start.4 = (f32[264,128]{1,0:T(8,128)S(1)}, f32[264,128]{1,0:T(8,128)S(1)}, u32[]{:S(2)}, u32[]{:S(2)}) collective-permute-start(f32[264,128]{1,0:T(8,128)S(1)} %collective-permute-done.3.refs_6_), channel_id=1, source_target_pairs={{8,0},{0,4},{4,12},{12,8},{9,1},{1,5},{5,13},{13,9},{10,2},{2,6},{... | collective-permute-start | bytes 405512 | tf_op jit(solution)/shard_map/ppermute | solution.py:27
  21.5 9.8 %collective-permute-start.19 = (f32[256,128]{1,0:T(8,128)S(1)}, f32[256,128]{1,0:T(8,128)S(1)}, u32[]{:S(2)}, u32[]{:S(2)}) collective-permute-start(f32[256,128]{1,0:T(8,128)S(1)} %collective-permute-done.18.refs_14_), channel_id=1, source_target_pairs={{8,0},{0,4},{4,12},{12,8},{9,1},{1,5},{5,13},{13,9},{10,2},{2,6},{... | collective-permute-start | bytes 393224 | tf_op jit(solution)/shard_map/ppermute | solution.py:27
  23.4 10.7 %collective-permute-start.13 = (f32[256,128]{1,0:T(8,128)S(1)}, f32[256,128]{1,0:T(8,128)S(1)}, u32[]{:S(2)}, u32[]{:S(2)}) collective-permute-start(f32[256,128]{1,0:T(8,128)S(1)} %collective-permute-done.12.refs_10_), channel_id=1, source_target_pairs={{8,0},{0,4},{4,12},{12,8},{9,1},{1,5},{5,13},{13,9},{10,2},{2,6},{... | collective-permute-start | bytes 393224 | tf_op jit(solution)/shard_map/ppermute | solution.py:27
  28.5 8.5 %collective-permute-start.5 = (f32[264,128]{1,0:T(8,128)S(1)}, f32[264,128]{1,0:T(8,128)S(1)}, u32[]{:S(2)}, u32[]{:S(2)}) collective-permute-start(f32[264,128]{1,0:T(8,128)S(1)} %collective-permute-done.4.refs_7_), channel_id=1, source_target_pairs={{8,0},{0,4},{4,12},{12,8},{9,1},{1,5},{5,13},{13,9},{10,2},{2,6},{... | collective-permute-start | bytes 405512 | tf_op jit(solution)/shard_map/ppermute | solution.py:27
  31.3 9.0 %collective-permute-start.20 = (f32[256,128]{1,0:T(8,128)S(1)}, f32[256,128]{1,0:T(8,128)S(1)}, u32[]{:S(2)}, u32[]{:S(2)}) collective-permute-start(f32[256,128]{1,0:T(8,128)S(1)} %collective-permute-done.19.refs_15_), channel_id=1, source_target_pairs={{8,0},{0,4},{4,12},{12,8},{9,1},{1,5},{5,13},{13,9},{10,2},{2,6},{... | collective-permute-start | bytes 393224 | tf_op jit(solution)/shard_map/ppermute | solution.py:27
  34.1 8.0 %collective-permute-start.14 = (f32[256,128]{1,0:T(8,128)S(1)}, f32[256,128]{1,0:T(8,128)S(1)}, u32[]{:S(2)}, u32[]{:S(2)}) collective-permute-start(f32[256,128]{1,0:T(8,128)S(1)} %collective-permute-done.13.refs_11_), channel_id=1, source_target_pairs={{8,0},{0,4},{4,12},{12,8},{9,1},{1,5},{5,13},{13,9},{10,2},{2,6},{... | collective-permute-start | bytes 393224 | tf_op jit(solution)/shard_map/ppermute | solution.py:27
  37.0 2.5 %copy-start.1 = (f32[3,8,32,128]{3,2,1,0:T(8,128)S(1)}, f32[3,8,32,128]{3,2,1,0:T(8,128)}, u32[]{:S(2)}) copy-start(f32[3,8,32,128]{3,2,1,0:T(8,128)} %correction_ref.3) | copy-start | bytes 1179652
  39.5 10.2 %collective-permute-start.6 = (f32[8,32,128]{2,1,0:T(8,128)S(1)}, f32[8,32,128]{2,1,0:T(8,128)S(1)}, u32[]{:S(2)}, u32[]{:S(2)}) collective-permute-start(f32[8,32,128]{2,1,0:T(8,128)S(1)} %get-tuple-element.44), channel_id=1, source_target_pairs={{8,0},{0,4},{4,12},{12,8},{9,1},{1,5},{5,13},{13,9},{10,2},{2,6},{... | collective-permute-start | bytes 393224 | tf_op jit(solution)/shard_map/ppermute | solution.py:27
  44.6 6.3 %collective-permute-start.21 = (f32[8,32,128]{2,1,0:T(8,128)S(1)}, f32[8,32,128]{2,1,0:T(8,128)S(1)}, u32[]{:S(2)}, u32[]{:S(2)}) collective-permute-start(f32[8,32,128]{2,1,0:T(8,128)S(1)} %get-tuple-element.59), channel_id=1, source_target_pairs={{8,0},{0,4},{4,12},{12,8},{9,1},{1,5},{5,13},{13,9},{10,2},{2,6},{... | collective-permute-start | bytes 393224 | tf_op jit(solution)/shard_map/ppermute | solution.py:27
  47.6 7.0 %collective-permute-start.15 = (f32[8,32,128]{2,1,0:T(8,128)S(1)}, f32[8,32,128]{2,1,0:T(8,128)S(1)}, u32[]{:S(2)}, u32[]{:S(2)}) collective-permute-start(f32[8,32,128]{2,1,0:T(8,128)S(1)} %get-tuple-element.54), channel_id=1, source_target_pairs={{8,0},{0,4},{4,12},{12,8},{9,1},{1,5},{5,13},{13,9},{10,2},{2,6},{... | collective-permute-start | bytes 393224 | tf_op jit(solution)/shard_map/ppermute | solution.py:27
  49.7 7.7 %collective-permute-start.7 = (f32[8,32,128]{2,1,0:T(8,128)S(1)}, f32[8,32,128]{2,1,0:T(8,128)S(1)}, u32[]{:S(2)}, u32[]{:S(2)}) collective-permute-start(f32[8,32,128]{2,1,0:T(8,128)S(1)} %add.26), channel_id=1, source_target_pairs={{8,0},{0,4},{4,12},{12,8},{9,1},{1,5},{5,13},{13,9},{10,2},{2,6},{... | collective-permute-start | bytes 393224 | tf_op jit(solution)/shard_map/ppermute | solution.py:27
  50.8 9.3 %collective-permute-start.22 = (f32[8,32,128]{2,1,0:T(8,128)S(1)}, f32[8,32,128]{2,1,0:T(8,128)S(1)}, u32[]{:S(2)}, u32[]{:S(2)}) collective-permute-start(f32[8,32,128]{2,1,0:T(8,128)S(1)} %add.30), channel_id=1, source_target_pairs={{8,0},{0,4},{4,12},{12,8},{9,1},{1,5},{5,13},{13,9},{10,2},{2,6},{... | collective-permute-start | bytes 393224 | tf_op jit(solution)/shard_map/ppermute | solution.py:27
  54.6 8.4 %collective-permute-start.16 = (f32[8,32,128]{2,1,0:T(8,128)S(1)}, f32[8,32,128]{2,1,0:T(8,128)S(1)}, u32[]{:S(2)}, u32[]{:S(2)}) collective-permute-start(f32[8,32,128]{2,1,0:T(8,128)S(1)} %add.28), channel_id=1, source_target_pairs={{8,0},{0,4},{4,12},{12,8},{9,1},{1,5},{5,13},{13,9},{10,2},{2,6},{... | collective-permute-start | bytes 393224 | tf_op jit(solution)/shard_map/ppermute | solution.py:27
  57.4 8.4 %collective-permute-start.8 = (f32[8,32,128]{2,1,0:T(8,128)S(1)}, f32[8,32,128]{2,1,0:T(8,128)S(1)}, u32[]{:S(2)}, u32[]{:S(2)}) collective-permute-start(f32[8,32,128]{2,1,0:T(8,128)S(1)} %add.27), channel_id=1, source_target_pairs={{8,0},{0,4},{4,12},{12,8},{9,1},{1,5},{5,13},{13,9},{10,2},{2,6},{... | collective-permute-start | bytes 393224 | tf_op jit(solution)/shard_map/ppermute | solution.py:27
  60.2 8.4 %collective-permute-start.23 = (f32[8,32,128]{2,1,0:T(8,128)S(1)}, f32[8,32,128]{2,1,0:T(8,128)S(1)}, u32[]{:S(2)}, u32[]{:S(2)}) collective-permute-start(f32[8,32,128]{2,1,0:T(8,128)S(1)} %add.31), channel_id=1, source_target_pairs={{8,0},{0,4},{4,12},{12,8},{9,1},{1,5},{5,13},{13,9},{10,2},{2,6},{... | collective-permute-start | bytes 393224 | tf_op jit(solution)/shard_map/ppermute | solution.py:27
  63.0 7.4 %collective-permute-start.17 = (f32[8,32,128]{2,1,0:T(8,128)S(1)}, f32[8,32,128]{2,1,0:T(8,128)S(1)}, u32[]{:S(2)}, u32[]{:S(2)}) collective-permute-start(f32[8,32,128]{2,1,0:T(8,128)S(1)} %add.29), channel_id=1, source_target_pairs={{8,0},{0,4},{4,12},{12,8},{9,1},{1,5},{5,13},{13,9},{10,2},{2,6},{... | collective-permute-start | bytes 393224 | tf_op jit(solution)/shard_map/ppermute | solution.py:27

commit v3 on v2

--- a/solution.py
+++ b/solution.py
@@ -15,7 +15,6 @@
 pairs_of_three = ((0, 0), (0, 1), (0, 2), (1, 1), (1, 2), (2, 2))
 f32, bf16 = jnp.float32, jnp.bfloat16
 dot = functools.partial(jnp.dot, preferred_element_type=f32)
-parcels = ((0,), (1, 2))
 
 
 def ring_order(ops):
@@ -47,19 +46,17 @@
 
 
 def pack_kernel(holders, table_ref, correction_ref, *outs):
-    rows, width = correction_ref.shape[2:]
+    vectors, _, rows, width = correction_ref.shape
     cap = table_ref.shape[0]
     here = holder_index()
-    for turn, vectors in enumerate(parcels):
-        for mask in range(holders):
-            out = outs[turn * holders + mask]
-            for slot in range(cap):
-                sector = table_ref[slot, here ^ mask]
-                filled = (sector >= 0).astype(f32)
-                sector = jnp.maximum(sector, 0)
-                for index, vector in enumerate(vectors):
-                    start = (index * cap + slot) * rows
-                    out[start : start + rows, :] = correction_ref[vector, sector] * filled
+    for mask, out in enumerate(outs):
+        for slot in range(cap):
+            sector = table_ref[slot, here ^ mask]
+            filled = (sector >= 0).astype(f32)
+            sector = jnp.maximum(sector, 0)
+            for vector in range(vectors):
+                start = (vector * cap + slot) * rows
+                out[start : start + rows, :] = correction_ref[vector, sector] * filled
     tiles = []
     for i, j in pairs_of_three:
         total = jnp.sum(correction_ref[i] * correction_ref[j], axis=(0, 1))[None, :]
@@ -67,17 +64,16 @@
         tiles.append(jnp.broadcast_to(total, (1, width)))
     tiles.append(jnp.zeros((2, width), f32))
     gram = jnp.concatenate(tiles, axis=0)
-    for mask in range(holders):
-        outs[mask][outs[mask].shape[0] - 8 :, :] = gram
-
-
-def join_kernel(holders, block, with_gram, *refs):
+    for out in outs:
+        out[out.shape[0] - 8 :, :] = gram
+
+
+def join_kernel(holders, block, *refs):
     received, outs = refs[:holders], refs[holders + 1 :]
     for index, out in enumerate(outs):
         for sender, part_ref in enumerate(received):
             out[sender * block : (sender + 1) * block, :] = part_ref[index * block : (index + 1) * block, :]
-    if with_gram:
-        outs[0][holders * block :, :] = sum(ref[ref.shape[0] - 8 :, :] for ref in received)
+    outs[0][holders * block :, :] = sum(ref[ref.shape[0] - 8 :, :] for ref in received)
 
 
 def plan_kernel(pairs, sectors, cap, terms, packed_ref, plan_ref, next_ref):
@@ -123,7 +119,8 @@
     lax.fori_loop(0, pairs, place_step, 0, unroll=4)
 
 
-def operator_kernel(plan_ref, live_ref, left_ref, right_ref, high_ref, low_ref, right_both_ref, right_low_ref):
+def operator_kernel(plan_ref, live_ref, left_ref, right_ref, *refs):
+    high_ref, low_ref, right_both_ref, right_low_ref = refs[-4:]
     width, terms = left_ref.shape[1], right_ref.shape[0]
 
     def couple_step(couple, carry):
@@ -163,11 +160,12 @@
     return [v_zero, v_one, v_two, v_four, v_five, v_eight]
 
 
-def apply_kernel(vector, ops, rows, entry_count, *refs):
+def apply_kernel(vector, holders, ops, rows, entry_count, *refs):
     refs = list(refs)
     take = lambda count: [refs.pop(0) for _ in range(count)]
     plan_ref, high_ref, low_ref, right_both_ref, right_low_ref = take(5)
-    pieces = [take(ops) for _ in range(vector + 1)]
+    near = take(holders)
+    pieces = [take(ops - 1) for _ in range(vector + 1)]
     inverse_in = take(1)[0] if vector else None
     outs = take(ops)
     inverse_out = None if vector else take(1)[0]
@@ -179,14 +177,18 @@
     if vector:
         inverse = inverse_in[...]
     else:
-        gram = sum(piece[count:, :] for piece in pieces[0])
+        gram = sum(ref[ref.shape[0] - 8 :, :] for ref in near + pieces[0])
         inverse = jnp.concatenate(inverse_rows(gram, entry_count) + [gram[6:]], axis=0)
         inverse_out[...] = inverse
-    for steps in range(ops):
-        value = 0.0
-        for earlier in range(vector + 1):
-            at = pairs_of_three.index((earlier, vector))
-            value += pieces[earlier][steps][:count, :] * inverse[at : at + 1, :]
+    factors = [inverse[i : i + 1, :] for i, (_, column) in enumerate(pairs_of_three) if column == vector]
+    cap = slots // holders
+    block = cap * rows
+    start = pl.multiple_of(place * rows, rows)
+    for sender, ref in enumerate(near):
+        value = sum(ref[j * block : (j + 1) * block, :] * factor for j, factor in enumerate(factors))
+        source_ref[sender * cap : (sender + 1) * cap, pl.ds(start, rows), :] = value.reshape(cap, rows, width)
+    for steps in range(1, ops):
+        value = sum(pieces[j][steps - 1][:count, :] * factor for j, factor in enumerate(factors))
         start = pl.multiple_of(shard_before(place, ops, steps) * rows, rows)
         source_ref[:, pl.ds(start, rows), :] = value.reshape(slots, rows, width)
 
@@ -224,13 +226,20 @@
         out_ref[k] = sum(correction_ref[j] * inverse[i : i + 1, :] for i, j in picked)
 
 
-def finish_kernel(*refs):
-    out, terms = refs[-1], refs[:-1]
-    for vector in range(out.shape[0]):
-        out[vector] = terms[2 * vector][...] + terms[2 * vector + 1][...]
-
-
-def call(kernel, out, inputs, specs, out_specs, name, scratch=()):
+def part_kernel(kept_ref, arrived_ref, out_ref):
+    out_ref[...] = kept_ref[...] + arrived_ref[...]
+
+
+def finish_kernel(counts, *refs):
+    refs, out = list(refs[:-1]), refs[-1]
+    for vector, count in enumerate(counts):
+        out[vector] = sum(refs.pop(0)[...] for _ in range(count))
+
+
+small = pl.CostEstimate(flops=1, bytes_accessed=1, transcendentals=0)
+
+
+def call(kernel, out, inputs, specs, out_specs, name, scratch=(), cost=None):
     return pl.pallas_call(
         kernel,
         out_shape=[jax.ShapeDtypeStruct(shape, dtype) for shape, dtype in out],
@@ -238,6 +247,7 @@
         out_specs=out_specs,
         scratch_shapes=list(scratch),
         compiler_params=limit,
+        cost_estimate=cost,
         name=name,
     )(*inputs)
 
@@ -255,25 +265,29 @@
 
     packed = call(
         functools.partial(pack_kernel, holders),
-        [
-            ((len(parcel) * block + (0 if turn else 8), width), f32)
-            for turn, parcel in enumerate(parcels)
-            for _ in range(holders)
-        ],
+        [((vectors * block + 8, width), f32)] * holders,
         (send_sector[0].T, correction),
         [smem, vmem],
-        [vmem] * (len(parcels) * holders),
+        [vmem] * holders,
         "pack",
     )
-    joined = []
-    received = []
-    for turn in range(len(parcels)):
-        mine = list(packed[turn * holders : (turn + 1) * holders])
-        for mask in range(holders - 1, 0, -1):
-            mine[mask] = lax.ppermute(
-                mine[mask], ("sec", "rep"), [(i, i ^ mask) for i in range(holders)]
-            )
-        received.append(mine)
+    order = ring_order(ops)
+    received = [
+        lax.ppermute(
+            packed[mask],
+            ("ops", "sec", "rep"),
+            [
+                (order[i - 1] * holders + e, order[i] * holders + (e ^ mask))
+                for i in range(ops)
+                for e in range(holders)
+            ],
+        )
+        for mask in range(holders)
+    ]
+    near = [packed[0]] + [
+        lax.ppermute(packed[mask], ("sec", "rep"), [(e, e ^ mask) for e in range(holders)])
+        for mask in range(1, holders)
+    ]
     (plan,) = call(
         functools.partial(plan_kernel, pairs, sectors, cap, terms),
         [((5 * couples,), jnp.int32)],
@@ -283,18 +297,6 @@
         "plan",
         [pltpu.SMEM((sectors,), jnp.int32)],
     )
-    for turn, parcel in enumerate(parcels):
-        joined += call(
-            functools.partial(join_kernel, holders, block, turn == 0),
-            [
-                ((slots * rows + (8 if turn == 0 and index == 0 else 0), width), f32)
-                for index in range(len(parcel))
-            ],
-            received[turn] + [plan],
-            [vmem] * holders + [anywhere],
-            [vmem] * len(parcel),
-            "join",
-        )
     high, low, right_both, right_low = call(
         operator_kernel,
         [
@@ -309,23 +311,31 @@
         "operators",
     )
 
+    joined = call(
+        functools.partial(join_kernel, holders, block),
+        [((slots * rows + (0 if vector else 8), width), f32) for vector in range(vectors)],
+        received + [right_low],
+        [vmem] * holders + [anywhere],
+        [vmem] * vectors,
+        "join",
+    )
     pieces = [[value] for value in joined]
-    for step in range(1, ops):
+    for step in range(2, ops):
         for vector in range(vectors):
             value = pieces[vector][-1]
-            if vector == 0 and step == 2:
-                value = follow(value, (right_low,))
+            if vector == 2 and step == 3:
+                value = follow(value, near[1:])
             pieces[vector].append(ring_step(value, ops))
 
     inverse = None
     sums = []
     for vector in range(vectors):
         arguments = [plan, high, low, right_both, right_low]
-        arguments += sum(pieces[: vector + 1], [])
+        arguments += near + sum(pieces[: vector + 1], [])
         arguments += [inverse] if vector else []
         out = [((sectors, rows, width), f32)] * ops + ([] if vector else [((8, width), f32)])
         parts = call(
-            functools.partial(apply_kernel, vector, ops, rows, entry_count),
+            functools.partial(apply_kernel, vector, holders, ops, rows, entry_count),
             out,
             arguments,
             [smem] + [vmem] * (len(arguments) - 1),
@@ -336,6 +346,7 @@
                 pltpu.VMEM((slots * terms, width, 2 * width), bf16),
                 pltpu.VMEM((sectors, width, width), f32),
             ],
+            small,
         )
         if vector == 0:
             inverse = parts[ops]
@@ -344,16 +355,20 @@
             )
         total = parts[1]
         for step in range(2, ops):
-            if vector == 1 and step == 2:
+            if vector == 2 and step == 3:
                 total = follow(total, (search_basis,))
             total = parts[step] + ring_step(total, ops)
-        sums += [parts[0], ring_step(total, ops)]
-
+        ends = [parts[0], ring_step(total, ops)]
+        if vector < 2:
+            ends = list(call(
+                part_kernel, [((sectors, rows, width), f32)], ends, [vmem] * 2, [vmem], "part", cost=small)
+            )
+        sums.append(ends)
     (sigma_blocks,) = call(
-        finish_kernel,
+        functools.partial(finish_kernel, [len(ends) for ends in sums]),
         [(correction.shape, f32)],
-        sums,
-        [vmem] * len(sums),
+        sum(sums, []),
+        [vmem] * sum(len(ends) for ends in sums),
         [vmem],
         "finish",
     )

time: 71.4 us -> 67.9 us (0.951)
  starting transfers between devices: 25.1 us -> 23.3 us
  waiting for transfers between devices: 27.1 us -> 25.5 us
    ppermute x18 -> x15, starting transfers between devices: 19.9 us -> 15 us  [ring_step(): lax.ppermute(value, 'ops', [(order[i - 1], order[i]) for i in range(ops)])]
    ppermute x6 -> x7, starting transfers between devices: 5.2 us -> 8.29 us  [the longest x4 6.65 us: local(): lax.ppermute(packed[mask], ('ops', 'sec', 'rep'), [(order[i - 1] * holder...]
    ppermute x18 -> x15, waiting for transfers between devices: 26.8 us -> 24.8 us  [ring_step(): lax.ppermute(value, 'ops', [(order[i - 1], order[i]) for i in range(ops)])]
    pallas_call x10 -> x11, Pallas kernels: 14 us -> 14 us  [call(): pl.pallas_call(kernel, out_shape=[jax.ShapeDtypeStruct(shape, dtype) for...]
  transfers between devices with their start and end apart: 24 -> 22, of which waited for: 15 -> 12; matrix products, arithmetic and copies ran while one was open for 1% -> 1% of each run, Pallas kernels for 18% -> 19%
where the time goes in v3:
time: 67.9 us; the launch traced here: 67.7 us
  waiting for transfers between devices  25.5 us (38%)
  starting transfers between devices  23.3 us (34%)
  Pallas kernels  14 us (21%)
  local copies, waits for them, and re-layouts  3.28 us (5%)
  other arithmetic  0.81 us (1%)
  between operations  0.8 us (1%)
    ppermute x15, waiting for transfers between devices, ring_step(): lax.ppermute(value, 'ops', [(order[i - 1], order[i]) for i in range(ops)])  24.8 us
    ppermute x15, starting transfers between devices, ring_step(): lax.ppermute(value, 'ops', [(order[i - 1], order[i]) for i in range(ops)])  15 us
    pallas_call x11, Pallas kernels, call(): pl.pallas_call(kernel, out_shape=[jax.ShapeDtypeStruct(shape, dtype) for...  14 us
    ppermute x4, starting transfers between devices, local(): lax.ppermute(packed[mask], ('ops', 'sec', 'rep'), [(order[i - 1] * holder...  6.65 us
    unnamed x10, local copies, waits for them, and re-layouts  3.28 us
    ppermute x3, starting transfers between devices, local(): lax.ppermute(packed[mask], ('sec', 'rep'), [(e, e ^ mask) for e in range(...  1.64 us
  transfers between devices with their start and end apart: 22, of which 12 were waited for; matrix products, arithmetic and copies ran while one was open for 1% of the time, Pallas kernels for 19%

profile of v3, /device:TPU:0, one launch (start us, length us, event | category | flops | bytes accessed | tf_op | source)
XLA Modules:
  0.0 67.7 jit_solution(13725633876795044357)
XLA Ops:
  0.6 0.0 copy-start
  0.6 1.0 %copy-done = f32[3,8,32,128]{3,2,1,0:T(8,128)S(1)} copy-done((f32[3,8,32,128]{3,2,1,0:T(8,128)S(1)}, f32[3,8,32,128]{3,2,1,0:T(8,128)}, u32[]{:S(2)}) %copy-start) | copy-done | bytes 393240
  1.6 0.7 copy-done.3
  2.3 0.7 %pack.1 = (f32[200,128]{1,0:T(8,128)S(1)}, f32[200,128]{1,0:T(8,128)S(1)}, f32[200,128]{1,0:T(8,128)S(1)}, f32[200,128]{1,0:T(8,128)S(1)}) custom-call(s32[2,4]{1,0:T(2,128)S(1)} %bitcast.3, f32[3,8,32,128]{3,2,1,0:T(8,128)S(1)} %copy-done), custom_call_target="tpu_custom_call" | custom-call | tf_op jit(solution)/shard_map/pack/pallas_call | solution.py:243
  3.0 0.5 collective-permute-start
  3.5 2.7 %collective-permute-start.4 = (f32[200,128]{1,0:T(8,128)S(1)}, f32[200,128]{1,0:T(8,128)S(1)}, u32[]{:S(2)}, u32[]{:S(2)}) collective-permute-start(f32[200,128]{1,0:T(8,128)S(1)} %get-tuple-element.33), channel_id=1, source_target_pairs={{8,1},{9,0},{10,3},{11,2},{0,5},{1,4},{2,7},{3,6},{4,13},{5,12},{6... | collective-permute-start | bytes 307208 | tf_op jit(solution)/shard_map/ppermute | solution.py:276
  6.2 2.6 %collective-permute-start.3 = (f32[200,128]{1,0:T(8,128)S(1)}, f32[200,128]{1,0:T(8,128)S(1)}, u32[]{:S(2)}, u32[]{:S(2)}) collective-permute-start(f32[200,128]{1,0:T(8,128)S(1)} %get-tuple-element.32.refs_5_), channel_id=1, source_target_pairs={{8,0},{9,1},{10,2},{11,3},{0,4},{1,5},{2,6},{3,7},{4,12},{5,13},{6... | collective-permute-start | bytes 307208 | tf_op jit(solution)/shard_map/ppermute | solution.py:276
  8.8 1.4 %collective-permute-start.5 = (f32[200,128]{1,0:T(8,128)S(1)}, f32[200,128]{1,0:T(8,128)S(1)}, u32[]{:S(2)}, u32[]{:S(2)}) collective-permute-start(f32[200,128]{1,0:T(8,128)S(1)} %get-tuple-element.34), channel_id=1, source_target_pairs={{8,2},{9,3},{10,0},{11,1},{0,6},{1,7},{2,4},{3,5},{4,14},{5,15},{6... | collective-permute-start | bytes 307208 | tf_op jit(solution)/shard_map/ppermute | solution.py:276
  10.1 0.7 %multiply_add_fusion.packed_ref = s32[40]{0:T(128)S(1)} fusion(s32[40]{0:T(128)} %param.14, s32[40]{0:T(128)} %param.13, s32[40]{0:T(128)} %param.12), kind=kLoop, calls=%fused_computation | loop fusion | flops 160 | bytes 640 | tf_op jit(solution)/shard_map/add | solution.py:294
  10.8 1.8 %plan.1.plan_ref.refs_0_ = s32[120]{0:T(128)S(1)} custom-call(s32[40]{0:T(128)S(1)} %multiply_add_fusion.packed_ref), custom_call_target="tpu_custom_call" | custom-call | tf_op jit(solution)/shard_map/plan/pallas_call | solution.py:243
  12.6 0.0 copy-start.2
  12.6 0.9 %copy-done.2 = f32[4,128,128]{2,1,0:T(8,128)S(1)} copy-done((f32[4,128,128]{2,1,0:T(8,128)S(1)}, f32[4,128,128]{2,1,0:T(8,128)}, u32[]{:S(2)}) %copy-start.2) | copy-done | bytes 262168
  13.6 0.7 copy-done.4
  14.2 2.6 %operators.1 = (bf16[24,128,256]{2,1,0:T(8,128)(2,1)S(1)}, bf16[24,128,256]{2,1,0:T(8,128)(2,1)S(1)}, bf16[256,512]{1,0:T(8,128)(2,1)S(1)}, bf16[128,512]{1,0:T(8,128)(2,1)S(1)}) custom-call(s32[120]{0:T(128)S(1)} %plan.1.plan_ref.refs_0_, s32[40]{0:T(128)S(1)} %copy-done.4, f32[40,128,128]{2,1,0:T(8,128)} %left_ref.1, f32[4,128,128]{2,1,0:T(8,128)S(1)} %copy-done.2), custom_call_target="tpu_custom_call" | custom-call | tf_op jit(solution)/shard_map/operators/pallas_call | solution.py:243
  16.8 0.7 %collective-permute-done.6.refs_3_ = f32[200,128]{1,0:T(8,128)S(1)} collective-permute-done((f32[200,128]{1,0:T(8,128)S(1)}, f32[200,128]{1,0:T(8,128)S(1)}, u32[]{:S(2)}, u32[]{:S(2)}) %collective-permute-start.6) | collective-permute-done | bytes 102432 | tf_op jit(solution)/shard_map/ppermute | solution.py:276
  17.6 0.5 collective-permute-start.7
  18.1 3.7 %collective-permute-start.12 = (f32[256,128]{1,0:T(8,128)S(1)}, f32[256,128]{1,0:T(8,128)S(1)}, u32[]{:S(2)}, u32[]{:S(2)}) collective-permute-start(f32[256,128]{1,0:T(8,128)S(1)} %get-tuple-element.42.refs_12_), channel_id=1, source_target_pairs={{8,0},{0,4},{4,12},{12,8},{9,1},{1,5},{5,13},{13,9},{10,2},{2,6},{... | collective-permute-start | bytes 393224 | tf_op jit(solution)/shard_map/ppermute | solution.py:26
  21.9 0.1 collective-permute-start.17
  21.9 0.6 collective-permute-start.1
  22.5 0.6 collective-permute-start.2
  23.1 1.9 %collective-permute-done.7.refs_10_ = f32[264,128]{1,0:T(8,128)S(1)} collective-permute-done((f32[264,128]{1,0:T(8,128)S(1)}, f32[264,128]{1,0:T(8,128)S(1)}, u32[]{:S(2)}, u32[]{:S(2)}) %collective-permute-start.7) | collective-permute-done | bytes 135200 | tf_op jit(solution)/shard_map/ppermute | solution.py:26
  25.0 0.8 %collective-permute-start.8 = (f32[264,128]{1,0:T(8,128)S(1)}, f32[264,128]{1,0:T(8,128)S(1)}, u32[]{:S(2)}, u32[]{:S(2)}) collective-permute-start(f32[264,128]{1,0:T(8,128)S(1)} %collective-permute-done.7.refs_10_), channel_id=1, source_target_pairs={{8,0},{0,4},{4,12},{12,8},{9,1},{1,5},{5,13},{13,9},{10,2},{2,6},{... | collective-permute-start | bytes 405512 | tf_op jit(solution)/shard_map/ppermute | solution.py:26
  25.8 2.0 %collective-permute-done.12.refs_13_ = f32[256,128]{1,0:T(8,128)S(1)} collective-permute-done((f32[256,128]{1,0:T(8,128)S(1)}, f32[256,128]{1,0:T(8,128)S(1)}, u32[]{:S(2)}, u32[]{:S(2)}) %collective-permute-start.12) | collective-permute-done | bytes 131104 | tf_op jit(solution)/shard_map/ppermute | solution.py:26
  27.8 1.4 %collective-permute-start.13 = (f32[256,128]{1,0:T(8,128)S(1)}, f32[256,128]{1,0:T(8,128)S(1)}, u32[]{:S(2)}, u32[]{:S(2)}) collective-permute-start(f32[256,128]{1,0:T(8,128)S(1)} %collective-permute-done.12.refs_13_), channel_id=1, source_target_pairs={{8,0},{0,4},{4,12},{12,8},{9,1},{1,5},{5,13},{13,9},{10,2},{2,6},{... | collective-permute-start | bytes 393224 | tf_op jit(solution)/shard_map/ppermute | solution.py:26
  29.2 1.4 %collective-permute-done.17.refs_16_ = f32[256,128]{1,0:T(8,128)S(1)} collective-permute-done((f32[256,128]{1,0:T(8,128)S(1)}, f32[256,128]{1,0:T(8,128)S(1)}, u32[]{:S(2)}, u32[]{:S(2)}) %collective-permute-start.17) | collective-permute-done | bytes 131104 | tf_op jit(solution)/shard_map/ppermute | solution.py:26
  30.6 1.4 %collective-permute-start.18 = (f32[256,128]{1,0:T(8,128)S(1)}, f32[256,128]{1,0:T(8,128)S(1)}, u32[]{:S(2)}, u32[]{:S(2)}) collective-permute-start(f32[256,128]{1,0:T(8,128)S(1)} %collective-permute-done.17.refs_16_), channel_id=1, source_target_pairs={{8,0},{0,4},{4,12},{12,8},{9,1},{1,5},{5,13},{13,9},{10,2},{2,6},{... | collective-permute-start | bytes 393224 | tf_op jit(solution)/shard_map/ppermute | solution.py:26
  32.0 1.5 %collective-permute-done.8.refs_11_ = f32[264,128]{1,0:T(8,128)S(1)} collective-permute-done((f32[264,128]{1,0:T(8,128)S(1)}, f32[264,128]{1,0:T(8,128)S(1)}, u32[]{:S(2)}, u32[]{:S(2)}) %collective-permute-start.8) | collective-permute-done | bytes 135200 | tf_op jit(solution)/shard_map/ppermute | solution.py:26
  33.5 2.4 %apply.3 = (f32[8,32,128]{2,1,0:T(8,128)S(1)}, f32[8,32,128]{2,1,0:T(8,128)S(1)}, f32[8,32,128]{2,1,0:T(8,128)S(1)}, f32[8,32,128]{2,1,0:T(8,128)S(1)}, f32[8,128]{1,0:T(8,128)S(1)}) custom-call(s32[120]{0:T(128)S(1)} %plan.1.plan_ref.refs_0_, bf16[24,128,256]{2,1,0:T(8,128)(2,1)S(1)} %get-tuple-element.28.refs_1_, ...), custom_call_target="tpu_custom_call" | custom-call | flops 1 | bytes 1 | tf_op jit(solution)/shard_map/apply/pallas_call | solution.py:243
  35.9 1.3 %collective-permute-start.9 = (f32[8,32,128]{2,1,0:T(8,128)S(1)}, f32[8,32,128]{2,1,0:T(8,128)S(1)}, u32[]{:S(2)}, u32[]{:S(2)}) collective-permute-start(f32[8,32,128]{2,1,0:T(8,128)S(1)} %get-tuple-element.41), channel_id=1, source_target_pairs={{8,0},{0,4},{4,12},{12,8},{9,1},{1,5},{5,13},{13,9},{10,2},{2,6},{... | collective-permute-start | bytes 393224 | tf_op jit(solution)/shard_map/ppermute | solution.py:26
  37.3 2.4 %apply.4 = (f32[8,32,128]{2,1,0:T(8,128)S(1)}, f32[8,32,128]{2,1,0:T(8,128)S(1)}, f32[8,32,128]{2,1,0:T(8,128)S(1)}, f32[8,32,128]{2,1,0:T(8,128)S(1)}) custom-call(s32[120]{0:T(128)S(1)} %plan.1.plan_ref.refs_0_, bf16[24,128,256]{2,1,0:T(8,128)(2,1)S(1)} %get-tuple-element.28.refs_1_, bf16[24,128,256]{2,1,0:T(8,128)(2,1)S(1)} %get-tuple-element.29.refs_2_, ...), custom_call_target="tpu_custom_call" | custom-call | flops 1 | bytes 1 | tf_op jit(solution)/shard_map/apply/pallas_call | solution.py:243
  39.7 2.9 %collective-permute-start.14 = (f32[8,32,128]{2,1,0:T(8,128)S(1)}, f32[8,32,128]{2,1,0:T(8,128)S(1)}, u32[]{:S(2)}, u32[]{:S(2)}) collective-permute-start(f32[8,32,128]{2,1,0:T(8,128)S(1)} %get-tuple-element.46), channel_id=1, source_target_pairs={{8,0},{0,4},{4,12},{12,8},{9,1},{1,5},{5,13},{13,9},{10,2},{2,6},{... | collective-permute-start | bytes 393224 | tf_op jit(solution)/shard_map/ppermute | solution.py:26
  42.7 2.5 %apply.5 = (f32[8,32,128]{2,1,0:T(8,128)S(1)}, f32[8,32,128]{2,1,0:T(8,128)S(1)}, f32[8,32,128]{2,1,0:T(8,128)S(1)}, f32[8,32,128]{2,1,0:T(8,128)S(1)}) custom-call(s32[120]{0:T(128)S(1)} %plan.1.plan_ref.refs_0_, bf16[24,128,256]{2,1,0:T(8,128)(2,1)S(1)} %get-tuple-element.28.refs_1_, bf16[24,128,256]{2,1,0:T(8,128)(2,1)S(1)} %get-tuple-element.29.refs_2_, ...), custom_call_target="tpu_custom_call" | custom-call | flops 1 | bytes 1 | tf_op jit(solution)/shard_map/apply/pallas_call | solution.py:243
  45.2 0.4 collective-permute-start.19
  45.5 0.8 %basis.1 = f32[3,8,32,128]{3,2,1,0:T(8,128)} custom-call(f32[8,128]{1,0:T(8,128)S(1)} %get-tuple-element.37.inverse_ref.refs_15_.refs_18_, f32[3,8,32,128]{3,2,1,0:T(8,128)S(1)} %copy-done.1), custom_call_target="tpu_custom_call" | custom-call | tf_op jit(solution)/shard_map/basis/pallas_call | solution.py:243
  46.3 0.5 collective-permute-start.10
  46.9 1.7 %collective-permute-start.15 = (f32[8,32,128]{2,1,0:T(8,128)S(1)}, f32[8,32,128]{2,1,0:T(8,128)S(1)}, u32[]{:S(2)}, u32[]{:S(2)}) collective-permute-start(f32[8,32,128]{2,1,0:T(8,128)S(1)} %add.28), channel_id=1, source_target_pairs={{8,0},{0,4},{4,12},{12,8},{9,1},{1,5},{5,13},{13,9},{10,2},{2,6},{... | collective-permute-start | bytes 393224 | tf_op jit(solution)/shard_map/ppermute | solution.py:26
  48.6 3.9 %collective-permute-done.19 = f32[8,32,128]{2,1,0:T(8,128)S(1)} collective-permute-done((f32[8,32,128]{2,1,0:T(8,128)S(1)}, f32[8,32,128]{2,1,0:T(8,128)S(1)}, u32[]{:S(2)}, u32[]{:S(2)}) %collective-permute-start.19) | collective-permute-done | bytes 131104 | tf_op jit(solution)/shard_map/ppermute | solution.py:26
  52.6 0.1 collective-permute-start.20
  52.6 2.7 %collective-permute-done.10 = f32[8,32,128]{2,1,0:T(8,128)S(1)} collective-permute-done((f32[8,32,128]{2,1,0:T(8,128)S(1)}, f32[8,32,128]{2,1,0:T(8,128)S(1)}, u32[]{:S(2)}, u32[]{:S(2)}) %collective-permute-start.10) | collective-permute-done | bytes 131104 | tf_op jit(solution)/shard_map/ppermute | solution.py:26
  55.4 0.1 collective-permute-start.11
  55.4 2.7 %collective-permute-done.15 = f32[8,32,128]{2,1,0:T(8,128)S(1)} collective-permute-done((f32[8,32,128]{2,1,0:T(8,128)S(1)}, f32[8,32,128]{2,1,0:T(8,128)S(1)}, u32[]{:S(2)}, u32[]{:S(2)}) %collective-permute-start.15) | collective-permute-done | bytes 131104 | tf_op jit(solution)/shard_map/ppermute | solution.py:26
  58.2 0.1 collective-permute-start.16
  58.2 2.7 %collective-permute-done.20 = f32[8,32,128]{2,1,0:T(8,128)S(1)} collective-permute-done((f32[8,32,128]{2,1,0:T(8,128)S(1)}, f32[8,32,128]{2,1,0:T(8,128)S(1)}, u32[]{:S(2)}, u32[]{:S(2)}) %collective-permute-start.20) | collective-permute-done | bytes 131104 | tf_op jit(solution)/shard_map/ppermute | solution.py:26
  61.0 0.1 collective-permute-start.21
  61.1 2.7 %collective-permute-done.11.arrived_ref = f32[8,32,128]{2,1,0:T(8,128)S(1)} collective-permute-done((f32[8,32,128]{2,1,0:T(8,128)S(1)}, f32[8,32,128]{2,1,0:T(8,128)S(1)}, u32[]{:S(2)}, u32[]{:S(2)}) %collective-permute-start.11) | collective-permute-done | bytes 131104 | tf_op jit(solution)/shard_map/ppermute | solution.py:26
  63.8 1.6 %collective-permute-done.16.arrived_ref = f32[8,32,128]{2,1,0:T(8,128)S(1)} collective-permute-done((f32[8,32,128]{2,1,0:T(8,128)S(1)}, f32[8,32,128]{2,1,0:T(8,128)S(1)}, u32[]{:S(2)}, u32[]{:S(2)}) %collective-permute-start.16) | collective-permute-done | bytes 131104 | tf_op jit(solution)/shard_map/ppermute | solution.py:26
  65.4 1.5 %collective-permute-done.21.refs_3_ = f32[8,32,128]{2,1,0:T(8,128)S(1)} collective-permute-done((f32[8,32,128]{2,1,0:T(8,128)S(1)}, f32[8,32,128]{2,1,0:T(8,128)S(1)}, u32[]{:S(2)}, u32[]{:S(2)}) %collective-permute-start.21) | collective-permute-done | bytes 131104 | tf_op jit(solution)/shard_map/ppermute | solution.py:26
  66.9 0.8 %finish.1 = f32[3,8,32,128]{3,2,1,0:T(8,128)} custom-call(f32[8,32,128]{2,1,0:T(8,128)S(1)} %part.2.refs_0_, f32[8,32,128]{2,1,0:T(8,128)S(1)} %part.3.refs_1_, f32[8,32,128]{2,1,0:T(8,128)S(1)} %get-tuple-element.49.refs_2_, f32[8,32,128]{2,1,0:T(8,128)S(1)} %collective-permute-done.21.refs_3_), custom_call_target="tpu_custom_call" | custom-call | tf_op jit(solution)/shard_map/finish/pallas_call | solution.py:243
  (24 shorter events, 0.2 us)
Async XLA Ops:
  0.6 1.0 %copy-start = (f32[3,8,32,128]{3,2,1,0:T(8,128)S(1)}, f32[3,8,32,128]{3,2,1,0:T(8,128)}, u32[]{:S(2)}) copy-start(f32[3,8,32,128]{3,2,1,0:T(8,128)} %correction_ref.3) | copy-start | bytes 1179652
  1.6 0.7 %copy-start.3 = (s32[1,4,2]{1,2,0:T(2,128)S(1)}, s32[1,4,2]{1,2,0:T(2,128)}, u32[]{:S(2)}) copy-start(s32[1,4,2]{1,2,0:T(2,128)} %param.11) | copy-start | bytes 100
  3.0 19.5 %collective-permute-start = (f32[200,128]{1,0:T(8,128)S(1)}, f32[200,128]{1,0:T(8,128)S(1)}, u32[]{:S(2)}, u32[]{:S(2)}) collective-permute-start(f32[200,128]{1,0:T(8,128)S(1)} %get-tuple-element.33), channel_id=1, source_target_pairs={{0,1},{1,0},{2,3},{3,2},{4,5},{5,4},{6,7},{7,6},{8,9},{9,8},{10,11... | collective-permute-start | bytes 307208 | tf_op jit(solution)/shard_map/ppermute | solution.py:288
  3.5 13.3 %collective-permute-start.4 = (f32[200,128]{1,0:T(8,128)S(1)}, f32[200,128]{1,0:T(8,128)S(1)}, u32[]{:S(2)}, u32[]{:S(2)}) collective-permute-start(f32[200,128]{1,0:T(8,128)S(1)} %get-tuple-element.33), channel_id=1, source_target_pairs={{8,1},{9,0},{10,3},{11,2},{0,5},{1,4},{2,7},{3,6},{4,13},{5,12},{6... | collective-permute-start | bytes 307208 | tf_op jit(solution)/shard_map/ppermute | solution.py:276
  6.2 10.6 %collective-permute-start.3 = (f32[200,128]{1,0:T(8,128)S(1)}, f32[200,128]{1,0:T(8,128)S(1)}, u32[]{:S(2)}, u32[]{:S(2)}) collective-permute-start(f32[200,128]{1,0:T(8,128)S(1)} %get-tuple-element.32.refs_5_), channel_id=1, source_target_pairs={{8,0},{9,1},{10,2},{11,3},{0,4},{1,5},{2,6},{3,7},{4,12},{5,13},{6... | collective-permute-start | bytes 307208 | tf_op jit(solution)/shard_map/ppermute | solution.py:276
  8.8 8.1 %collective-permute-start.5 = (f32[200,128]{1,0:T(8,128)S(1)}, f32[200,128]{1,0:T(8,128)S(1)}, u32[]{:S(2)}, u32[]{:S(2)}) collective-permute-start(f32[200,128]{1,0:T(8,128)S(1)} %get-tuple-element.34), channel_id=1, source_target_pairs={{8,2},{9,3},{10,0},{11,1},{0,6},{1,7},{2,4},{3,5},{4,14},{5,15},{6... | collective-permute-start | bytes 307208 | tf_op jit(solution)/shard_map/ppermute | solution.py:276
  10.1 7.4 %collective-permute-start.6 = (f32[200,128]{1,0:T(8,128)S(1)}, f32[200,128]{1,0:T(8,128)S(1)}, u32[]{:S(2)}, u32[]{:S(2)}) collective-permute-start(f32[200,128]{1,0:T(8,128)S(1)} %get-tuple-element.35), channel_id=1, source_target_pairs={{8,3},{9,2},{10,1},{11,0},{0,7},{1,6},{2,5},{3,4},{4,15},{5,14},{6... | collective-permute-start | bytes 307208 | tf_op jit(solution)/shard_map/ppermute | solution.py:276
  12.6 1.0 %copy-start.2 = (f32[4,128,128]{2,1,0:T(8,128)S(1)}, f32[4,128,128]{2,1,0:T(8,128)}, u32[]{:S(2)}) copy-start(f32[4,128,128]{2,1,0:T(8,128)} %right_ref.1) | copy-start | bytes 786436
  13.6 0.7 copy-start.4
  17.6 7.4 %collective-permute-start.7 = (f32[264,128]{1,0:T(8,128)S(1)}, f32[264,128]{1,0:T(8,128)S(1)}, u32[]{:S(2)}, u32[]{:S(2)}) collective-permute-start(f32[264,128]{1,0:T(8,128)S(1)} %get-tuple-element.36.refs_9_), channel_id=1, source_target_pairs={{8,0},{0,4},{4,12},{12,8},{9,1},{1,5},{5,13},{13,9},{10,2},{2,6},{... | collective-permute-start | bytes 405512 | tf_op jit(solution)/shard_map/ppermute | solution.py:26
  18.1 9.7 %collective-permute-start.12 = (f32[256,128]{1,0:T(8,128)S(1)}, f32[256,128]{1,0:T(8,128)S(1)}, u32[]{:S(2)}, u32[]{:S(2)}) collective-permute-start(f32[256,128]{1,0:T(8,128)S(1)} %get-tuple-element.42.refs_12_), channel_id=1, source_target_pairs={{8,0},{0,4},{4,12},{12,8},{9,1},{1,5},{5,13},{13,9},{10,2},{2,6},{... | collective-permute-start | bytes 393224 | tf_op jit(solution)/shard_map/ppermute | solution.py:26
  21.9 8.8 %collective-permute-start.17 = (f32[256,128]{1,0:T(8,128)S(1)}, f32[256,128]{1,0:T(8,128)S(1)}, u32[]{:S(2)}, u32[]{:S(2)}) collective-permute-start(f32[256,128]{1,0:T(8,128)S(1)} %get-tuple-element.47.refs_15_), channel_id=1, source_target_pairs={{8,0},{0,4},{4,12},{12,8},{9,1},{1,5},{5,13},{13,9},{10,2},{2,6},{... | collective-permute-start | bytes 393224 | tf_op jit(solution)/shard_map/ppermute | solution.py:26
  21.9 7.2 %collective-permute-start.1 = (f32[200,128]{1,0:T(8,128)S(1)}, f32[200,128]{1,0:T(8,128)S(1)}, u32[]{:S(2)}, u32[]{:S(2)}) collective-permute-start(f32[200,128]{1,0:T(8,128)S(1)} %get-tuple-element.34), channel_id=1, source_target_pairs={{0,2},{1,3},{2,0},{3,1},{4,6},{5,7},{6,4},{7,5},{8,10},{9,11},{10,... | collective-permute-start | bytes 307208 | tf_op jit(solution)/shard_map/ppermute | solution.py:288
  22.5 6.7 %collective-permute-start.2 = (f32[200,128]{1,0:T(8,128)S(1)}, f32[200,128]{1,0:T(8,128)S(1)}, u32[]{:S(2)}, u32[]{:S(2)}) collective-permute-start(f32[200,128]{1,0:T(8,128)S(1)} %get-tuple-element.35), channel_id=1, source_target_pairs={{0,3},{1,2},{2,1},{3,0},{4,7},{5,6},{6,5},{7,4},{8,11},{9,10},{10,... | collective-permute-start | bytes 307208 | tf_op jit(solution)/shard_map/ppermute | solution.py:288
  25.0 8.5 %collective-permute-start.8 = (f32[264,128]{1,0:T(8,128)S(1)}, f32[264,128]{1,0:T(8,128)S(1)}, u32[]{:S(2)}, u32[]{:S(2)}) collective-permute-start(f32[264,128]{1,0:T(8,128)S(1)} %collective-permute-done.7.refs_10_), channel_id=1, source_target_pairs={{8,0},{0,4},{4,12},{12,8},{9,1},{1,5},{5,13},{13,9},{10,2},{2,6},{... | collective-permute-start | bytes 405512 | tf_op jit(solution)/shard_map/ppermute | solution.py:26
  27.8 9.5 %collective-permute-start.13 = (f32[256,128]{1,0:T(8,128)S(1)}, f32[256,128]{1,0:T(8,128)S(1)}, u32[]{:S(2)}, u32[]{:S(2)}) collective-permute-start(f32[256,128]{1,0:T(8,128)S(1)} %collective-permute-done.12.refs_13_), channel_id=1, source_target_pairs={{8,0},{0,4},{4,12},{12,8},{9,1},{1,5},{5,13},{13,9},{10,2},{2,6},{... | collective-permute-start | bytes 393224 | tf_op jit(solution)/shard_map/ppermute | solution.py:26
  30.6 12.1 %collective-permute-start.18 = (f32[256,128]{1,0:T(8,128)S(1)}, f32[256,128]{1,0:T(8,128)S(1)}, u32[]{:S(2)}, u32[]{:S(2)}) collective-permute-start(f32[256,128]{1,0:T(8,128)S(1)} %collective-permute-done.17.refs_16_), channel_id=1, source_target_pairs={{8,0},{0,4},{4,12},{12,8},{9,1},{1,5},{5,13},{13,9},{10,2},{2,6},{... | collective-permute-start | bytes 393224 | tf_op jit(solution)/shard_map/ppermute | solution.py:26
  35.9 10.4 %collective-permute-start.9 = (f32[8,32,128]{2,1,0:T(8,128)S(1)}, f32[8,32,128]{2,1,0:T(8,128)S(1)}, u32[]{:S(2)}, u32[]{:S(2)}) collective-permute-start(f32[8,32,128]{2,1,0:T(8,128)S(1)} %get-tuple-element.41), channel_id=1, source_target_pairs={{8,0},{0,4},{4,12},{12,8},{9,1},{1,5},{5,13},{13,9},{10,2},{2,6},{... | collective-permute-start | bytes 393224 | tf_op jit(solution)/shard_map/ppermute | solution.py:26
  39.7 5.8 %copy-start.1 = (f32[3,8,32,128]{3,2,1,0:T(8,128)S(1)}, f32[3,8,32,128]{3,2,1,0:T(8,128)}, u32[]{:S(2)}) copy-start(f32[3,8,32,128]{3,2,1,0:T(8,128)} %correction_ref.3) | copy-start | bytes 1179652
  39.7 7.1 %collective-permute-start.14 = (f32[8,32,128]{2,1,0:T(8,128)S(1)}, f32[8,32,128]{2,1,0:T(8,128)S(1)}, u32[]{:S(2)}, u32[]{:S(2)}) collective-permute-start(f32[8,32,128]{2,1,0:T(8,128)S(1)} %get-tuple-element.46), channel_id=1, source_target_pairs={{8,0},{0,4},{4,12},{12,8},{9,1},{1,5},{5,13},{13,9},{10,2},{2,6},{... | collective-permute-start | bytes 393224 | tf_op jit(solution)/shard_map/ppermute | solution.py:26
  45.2 7.4 %collective-permute-start.19 = (f32[8,32,128]{2,1,0:T(8,128)S(1)}, f32[8,32,128]{2,1,0:T(8,128)S(1)}, u32[]{:S(2)}, u32[]{:S(2)}) collective-permute-start(f32[8,32,128]{2,1,0:T(8,128)S(1)} %get-tuple-element.52), channel_id=1, source_target_pairs={{8,0},{0,4},{4,12},{12,8},{9,1},{1,5},{5,13},{13,9},{10,2},{2,6},{... | collective-permute-start | bytes 393224 | tf_op jit(solution)/shard_map/ppermute | solution.py:26
  46.3 9.0 %collective-permute-start.10 = (f32[8,32,128]{2,1,0:T(8,128)S(1)}, f32[8,32,128]{2,1,0:T(8,128)S(1)}, u32[]{:S(2)}, u32[]{:S(2)}) collective-permute-start(f32[8,32,128]{2,1,0:T(8,128)S(1)} %add.26), channel_id=1, source_target_pairs={{8,0},{0,4},{4,12},{12,8},{9,1},{1,5},{5,13},{13,9},{10,2},{2,6},{... | collective-permute-start | bytes 393224 | tf_op jit(solution)/shard_map/ppermute | solution.py:26
  46.9 11.3 %collective-permute-start.15 = (f32[8,32,128]{2,1,0:T(8,128)S(1)}, f32[8,32,128]{2,1,0:T(8,128)S(1)}, u32[]{:S(2)}, u32[]{:S(2)}) collective-permute-start(f32[8,32,128]{2,1,0:T(8,128)S(1)} %add.28), channel_id=1, source_target_pairs={{8,0},{0,4},{4,12},{12,8},{9,1},{1,5},{5,13},{13,9},{10,2},{2,6},{... | collective-permute-start | bytes 393224 | tf_op jit(solution)/shard_map/ppermute | solution.py:26
  52.6 8.4 %collective-permute-start.20 = (f32[8,32,128]{2,1,0:T(8,128)S(1)}, f32[8,32,128]{2,1,0:T(8,128)S(1)}, u32[]{:S(2)}, u32[]{:S(2)}) collective-permute-start(f32[8,32,128]{2,1,0:T(8,128)S(1)} %add.30), channel_id=1, source_target_pairs={{8,0},{0,4},{4,12},{12,8},{9,1},{1,5},{5,13},{13,9},{10,2},{2,6},{... | collective-permute-start | bytes 393224 | tf_op jit(solution)/shard_map/ppermute | solution.py:26
  55.4 8.4 %collective-permute-start.11 = (f32[8,32,128]{2,1,0:T(8,128)S(1)}, f32[8,32,128]{2,1,0:T(8,128)S(1)}, u32[]{:S(2)}, u32[]{:S(2)}) collective-permute-start(f32[8,32,128]{2,1,0:T(8,128)S(1)} %add.27), channel_id=1, source_target_pairs={{8,0},{0,4},{4,12},{12,8},{9,1},{1,5},{5,13},{13,9},{10,2},{2,6},{... | collective-permute-start | bytes 393224 | tf_op jit(solution)/shard_map/ppermute | solution.py:26
  58.2 7.2 %collective-permute-start.16 = (f32[8,32,128]{2,1,0:T(8,128)S(1)}, f32[8,32,128]{2,1,0:T(8,128)S(1)}, u32[]{:S(2)}, u32[]{:S(2)}) collective-permute-start(f32[8,32,128]{2,1,0:T(8,128)S(1)} %add.29), channel_id=1, source_target_pairs={{8,0},{0,4},{4,12},{12,8},{9,1},{1,5},{5,13},{13,9},{10,2},{2,6},{... | collective-permute-start | bytes 393224 | tf_op jit(solution)/shard_map/ppermute | solution.py:26
  61.0 5.9 %collective-permute-start.21 = (f32[8,32,128]{2,1,0:T(8,128)S(1)}, f32[8,32,128]{2,1,0:T(8,128)S(1)}, u32[]{:S(2)}, u32[]{:S(2)}) collective-permute-start(f32[8,32,128]{2,1,0:T(8,128)S(1)} %add.31), channel_id=1, source_target_pairs={{8,0},{0,4},{4,12},{12,8},{9,1},{1,5},{5,13},{13,9},{10,2},{2,6},{... | collective-permute-start | bytes 393224 | tf_op jit(solution)/shard_map/ppermute | solution.py:26

commit v4 on v3

--- a/solution.py
+++ b/solution.py
@@ -10,6 +10,7 @@
 epsilon = 1e-06
 vmem = pl.BlockSpec(memory_space=pltpu.VMEM)
 smem = pl.BlockSpec(memory_space=pltpu.SMEM)
+hbm = pl.BlockSpec(memory_space=pltpu.HBM)
 anywhere = pl.BlockSpec(memory_space=pl.ANY)
 limit = pltpu.CompilerParams(vmem_limit_bytes=48 * 1024 * 1024)
 pairs_of_three = ((0, 0), (0, 1), (0, 2), (1, 1), (1, 2), (2, 2))
@@ -36,6 +37,10 @@
     return lax.axis_index("sec") * lax.axis_size("rep") + lax.axis_index("rep")
 
 
+def main_memory(value):
+    return pltpu.with_memory_space_constraint(value, pltpu.HBM)
+
+
 def follow(value, others):
     return lax.optimization_barrier((value,) + tuple(others))[0] if others else value
 
@@ -45,7 +50,14 @@
     return high, (value - high.astype(f32)).astype(bf16)
 
 
-def pack_kernel(holders, table_ref, correction_ref, *outs):
+def pack_kernel(table_in, correction_in, *refs):
+    *outs, table_ref, correction_ref, table_sem, correction_sem = refs
+    table_copy = pltpu.make_async_copy(table_in, table_ref, table_sem)
+    correction_copy = pltpu.make_async_copy(correction_in, correction_ref, correction_sem)
+    correction_copy.start()
+    table_copy.start()
+    table_copy.wait()
+    correction_copy.wait()
     vectors, _, rows, width = correction_ref.shape
     cap = table_ref.shape[0]
     here = holder_index()
@@ -119,9 +131,24 @@
     lax.fori_loop(0, pairs, place_step, 0, unroll=4)
 
 
-def operator_kernel(plan_ref, live_ref, left_ref, right_ref, *refs):
-    high_ref, low_ref, right_both_ref, right_low_ref = refs[-4:]
+def operator_kernel(plan_ref, live_in, left_in, right_in, *refs):
+    high_ref, low_ref, right_both_ref, right_low_ref, live_ref, left_ref, right_ref, live_sem, left_sem, right_sem = refs
     width, terms = left_ref.shape[1], right_ref.shape[0]
+    right_copy = pltpu.make_async_copy(right_in, right_ref, right_sem)
+    live_copy = pltpu.make_async_copy(live_in, live_ref, live_sem)
+    left_copy = pltpu.make_async_copy(left_in, left_ref, left_sem)
+    right_copy.start()
+    live_copy.start()
+    left_copy.start()
+    right_copy.wait()
+    for term in range(terms):
+        high, low = split(right_ref[term].T)
+        columns = slice(term * width, (term + 1) * width)
+        right_both_ref[:width, columns] = high
+        right_both_ref[width:, columns] = high
+        right_low_ref[:, columns] = low
+    live_copy.wait()
+    left_copy.wait()
 
     def couple_step(couple, carry):
         for side in range(2):
@@ -135,12 +162,6 @@
         return carry
 
     lax.fori_loop(0, high_ref.shape[0], couple_step, 0, unroll=4)
-    for term in range(terms):
-        high, low = split(right_ref[term].T)
-        columns = slice(term * width, (term + 1) * width)
-        right_both_ref[:width, columns] = high
-        right_both_ref[width:, columns] = high
-        right_low_ref[:, columns] = low
 
 
 def inverse_rows(gram, entry_count):
@@ -219,27 +240,28 @@
         outs[steps][...] = total_ref[:, pl.ds(start, rows), :]
 
 
-def basis_kernel(inverse_ref, correction_ref, out_ref):
+def part_kernel(vector, kept_ref, arrived_ref, _, out, sum_ref, sum_sem):
+    sum_ref[...] = kept_ref[...] + arrived_ref[...]
+    copy = pltpu.make_async_copy(sum_ref, out.at[vector], sum_sem)
+    copy.start()
+    copy.wait()
+
+
+def part_and_basis_kernel(kept_ref, arrived_ref, inverse_ref, correction_ref, out, basis_ref, sum_ref, sum_sem):
+    sum_ref[...] = kept_ref[...] + arrived_ref[...]
+    copy = pltpu.make_async_copy(sum_ref, out.at[0], sum_sem)
+    copy.start()
     inverse = inverse_ref[...]
-    for k in range(out_ref.shape[0]):
+    for k in range(basis_ref.shape[0]):
         picked = [(i, j) for i, (j, column) in enumerate(pairs_of_three) if column == k]
-        out_ref[k] = sum(correction_ref[j] * inverse[i : i + 1, :] for i, j in picked)
-
-
-def part_kernel(kept_ref, arrived_ref, out_ref):
-    out_ref[...] = kept_ref[...] + arrived_ref[...]
-
-
-def finish_kernel(counts, *refs):
-    refs, out = list(refs[:-1]), refs[-1]
-    for vector, count in enumerate(counts):
-        out[vector] = sum(refs.pop(0)[...] for _ in range(count))
+        basis_ref[k] = sum(correction_ref[j] * inverse[i : i + 1, :] for i, j in picked)
+    copy.wait()
 
 
 small = pl.CostEstimate(flops=1, bytes_accessed=1, transcendentals=0)
 
 
-def call(kernel, out, inputs, specs, out_specs, name, scratch=(), cost=None):
+def call(kernel, out, inputs, specs, out_specs, name, scratch=(), cost=None, aliases={}):
     return pl.pallas_call(
         kernel,
         out_shape=[jax.ShapeDtypeStruct(shape, dtype) for shape, dtype in out],
@@ -248,6 +270,7 @@
         scratch_shapes=list(scratch),
         compiler_params=limit,
         cost_estimate=cost,
+        input_output_aliases=aliases,
         name=name,
     )(*inputs)
 
@@ -264,12 +287,18 @@
     couples = (pairs + min(pairs, sectors)) // 2
 
     packed = call(
-        functools.partial(pack_kernel, holders),
+        pack_kernel,
         [((vectors * block + 8, width), f32)] * holders,
-        (send_sector[0].T, correction),
-        [smem, vmem],
+        (main_memory(send_sector[0].T), main_memory(correction)),
+        [hbm] * 2,
         [vmem] * holders,
         "pack",
+        [
+            pltpu.SMEM((cap, holders), jnp.int32),
+            pltpu.VMEM(correction.shape, f32),
+            pltpu.SemaphoreType.DMA,
+            pltpu.SemaphoreType.DMA,
+        ],
     )
     order = ring_order(ops)
     received = [
@@ -305,10 +334,16 @@
             ((2 * width, terms * width), bf16),
             ((width, terms * width), bf16),
         ],
-        (plan, pair_live, left_blocks, right_blocks),
-        [smem] * 2 + [vmem] * 2,
+        (plan, main_memory(pair_live), main_memory(left_blocks), main_memory(right_blocks)),
+        [smem] + [hbm] * 3,
         [vmem] * 4,
         "operators",
+        [
+            pltpu.SMEM((pairs,), jnp.int32),
+            pltpu.VMEM(left_blocks.shape, f32),
+            pltpu.VMEM(right_blocks.shape, f32),
+        ]
+        + [pltpu.SemaphoreType.DMA] * 3,
     )
 
     joined = call(
@@ -328,7 +363,6 @@
             pieces[vector].append(ring_step(value, ops))
 
     inverse = None
-    sums = []
     for vector in range(vectors):
         arguments = [plan, high, low, right_both, right_low]
         arguments += near + sum(pieces[: vector + 1], [])
@@ -350,28 +384,34 @@
         )
         if vector == 0:
             inverse = parts[ops]
-            (search_basis,) = call(
-                basis_kernel, [(correction.shape, f32)], (inverse, correction), [vmem] * 2, [vmem], "basis"
-            )
         total = parts[1]
         for step in range(2, ops):
-            if vector == 2 and step == 3:
-                total = follow(total, (search_basis,))
             total = parts[step] + ring_step(total, ops)
         ends = [parts[0], ring_step(total, ops)]
-        if vector < 2:
-            ends = list(call(
-                part_kernel, [((sectors, rows, width), f32)], ends, [vmem] * 2, [vmem], "part", cost=small)
+        scratch = [pltpu.VMEM((sectors, rows, width), f32), pltpu.SemaphoreType.DMA]
+        if vector == 0:
+            sigma_blocks, search_basis = call(
+                part_and_basis_kernel,
+                [(correction.shape, f32)] * 2,
+                ends + [inverse, correction],
+                [vmem] * 4,
+                [hbm, vmem],
+                "part",
+                scratch,
+                small,
             )
-        sums.append(ends)
-    (sigma_blocks,) = call(
-        functools.partial(finish_kernel, [len(ends) for ends in sums]),
-        [(correction.shape, f32)],
-        sum(sums, []),
-        [vmem] * sum(len(ends) for ends in sums),
-        [vmem],
-        "finish",
-    )
+        else:
+            (sigma_blocks,) = call(
+                functools.partial(part_kernel, vector),
+                [(correction.shape, f32)],
+                ends + [main_memory(sigma_blocks)],
+                [vmem] * 2 + [hbm],
+                [hbm],
+                "part",
+                scratch,
+                small,
+                {2: 0},
+            )
     return (search_basis, sigma_blocks)
 
 

time: 67.9 us -> 66.2 us (0.975)
  local copies, waits for them, and re-layouts: 3.28 us -> 0.01 us
  Pallas kernels: 14 us -> 16.2 us
  starting transfers between devices: 23.3 us -> 21.9 us
  waiting for transfers between devices: 25.5 us -> 26.3 us
    unnamed x10 -> x2, local copies, waits for them, and re-layouts: 3.28 us -> 0.01 us
    pallas_call x11 -> x10, Pallas kernels: 14 us -> 16.2 us  [call(): pl.pallas_call(kernel, out_shape=[jax.ShapeDtypeStruct(shape, dtype) for...]
    ppermute x15, starting transfers between devices: 15 us -> 13.3 us  [ring_step(): lax.ppermute(value, 'ops', [(order[i - 1], order[i]) for i in range(ops)])]
    ppermute x4, waiting for transfers between devices: 0.73 us -> 2 us  [local(): lax.ppermute(packed[mask], ('ops', 'sec', 'rep'), [(order[i - 1] * holder...]
  transfers between devices with their start and end apart: 22 -> 22, of which waited for: 12 -> 12; matrix products, arithmetic and copies ran while one was open for 1% -> 1% of each run, Pallas kernels for 19% -> 22%
where the time goes in v4:
time: 66.2 us; the launch traced here: 66 us
  waiting for transfers between devices  26.3 us (40%)
  starting transfers between devices  21.9 us (33%)
  Pallas kernels  16.2 us (24%)
  other arithmetic  0.81 us (1%)
  between operations  0.8 us (1%)
    ppermute x15, waiting for transfers between devices, ring_step(): lax.ppermute(value, 'ops', [(order[i - 1], order[i]) for i in range(ops)])  24.3 us
    pallas_call x10, Pallas kernels, call(): pl.pallas_call(kernel, out_shape=[jax.ShapeDtypeStruct(shape, dtype) for...  16.2 us
    ppermute x15, starting transfers between devices, ring_step(): lax.ppermute(value, 'ops', [(order[i - 1], order[i]) for i in range(ops)])  13.3 us
    ppermute x4, starting transfers between devices, local(): lax.ppermute(packed[mask], ('ops', 'sec', 'rep'), [(order[i - 1] * holder...  6.48 us
    ppermute x3, starting transfers between devices, local(): lax.ppermute(packed[mask], ('sec', 'rep'), [(e, e ^ mask) for e in range(...  2.17 us
    ppermute x4, waiting for transfers between devices, local(): lax.ppermute(packed[mask], ('ops', 'sec', 'rep'), [(order[i - 1] * holder...  2 us
  transfers between devices with their start and end apart: 22, of which 12 were waited for; matrix products, arithmetic and copies ran while one was open for 1% of the time, Pallas kernels for 22%

profile of v4, /device:TPU:0, one launch (start us, length us, event | category | flops | bytes accessed | tf_op | source)
XLA Modules:
  0.0 66.0 jit_solution(5243052454908488716)
XLA Ops:
  0.6 1.2 %pack.1 = (f32[200,128]{1,0:T(8,128)S(1)}, f32[200,128]{1,0:T(8,128)S(1)}, f32[200,128]{1,0:T(8,128)S(1)}, f32[200,128]{1,0:T(8,128)S(1)}) custom-call(s32[2,4]{1,0:T(2,128)} %bitcast.3, f32[3,8,32,128]{3,2,1,0:T(8,128)} %correction_ref.1), custom_call_target="tpu_custom_call" | custom-call | tf_op jit(solution)/shard_map/pack/pallas_call | solution.py:265
  1.8 2.5 %collective-permute-start.4 = (f32[200,128]{1,0:T(8,128)S(1)}, f32[200,128]{1,0:T(8,128)S(1)}, u32[]{:S(2)}, u32[]{:S(2)}) collective-permute-start(f32[200,128]{1,0:T(8,128)S(1)} %get-tuple-element.34), channel_id=1, source_target_pairs={{8,1},{9,0},{10,3},{11,2},{0,5},{1,4},{2,7},{3,6},{4,13},{5,12},{6... | collective-permute-start | bytes 307208 | tf_op jit(solution)/shard_map/ppermute | solution.py:305
  4.3 0.7 %collective-permute-start = (f32[200,128]{1,0:T(8,128)S(1)}, f32[200,128]{1,0:T(8,128)S(1)}, u32[]{:S(2)}, u32[]{:S(2)}) collective-permute-start(f32[200,128]{1,0:T(8,128)S(1)} %get-tuple-element.34), channel_id=1, source_target_pairs={{0,1},{1,0},{2,3},{3,2},{4,5},{5,4},{6,7},{7,6},{8,9},{9,8},{10,11... | collective-permute-start | bytes 307208 | tf_op jit(solution)/shard_map/ppermute | solution.py:317
  5.0 3.5 %collective-permute-start.5 = (f32[200,128]{1,0:T(8,128)S(1)}, f32[200,128]{1,0:T(8,128)S(1)}, u32[]{:S(2)}, u32[]{:S(2)}) collective-permute-start(f32[200,128]{1,0:T(8,128)S(1)} %get-tuple-element.35), channel_id=1, source_target_pairs={{8,2},{9,3},{10,0},{11,1},{0,6},{1,7},{2,4},{3,5},{4,14},{5,15},{6... | collective-permute-start | bytes 307208 | tf_op jit(solution)/shard_map/ppermute | solution.py:305
  8.5 0.0 collective-permute-start.6
  8.5 0.4 collective-permute-start.3
  9.0 0.7 %multiply_add_fusion.packed_ref = s32[40]{0:T(128)S(1)} fusion(s32[40]{0:T(128)} %param.14, s32[40]{0:T(128)} %param.13, s32[40]{0:T(128)} %param.12), kind=kLoop, calls=%fused_computation | loop fusion | flops 160 | bytes 640 | tf_op jit(solution)/shard_map/add | solution.py:323
  9.7 1.8 %plan.1.plan_ref.refs_0_ = s32[120]{0:T(128)S(1)} custom-call(s32[40]{0:T(128)S(1)} %multiply_add_fusion.packed_ref), custom_call_target="tpu_custom_call" | custom-call | tf_op jit(solution)/shard_map/plan/pallas_call | solution.py:265
  11.4 3.1 %operators.1 = (bf16[24,128,256]{2,1,0:T(8,128)(2,1)S(1)}, bf16[24,128,256]{2,1,0:T(8,128)(2,1)S(1)}, bf16[256,512]{1,0:T(8,128)(2,1)S(1)}, bf16[128,512]{1,0:T(8,128)(2,1)S(1)}) custom-call(s32[120]{0:T(128)S(1)} %plan.1.plan_ref.refs_0_, s32[40]{0:T(128)} %live_in.1, f32[40,128,128]{2,1,0:T(8,128)} %left_in.1, f32[4,128,128]{2,1,0:T(8,128)} %right_in.1), custom_call_target="tpu_custom_call" | custom-call | tf_op jit(solution)/shard_map/operators/pallas_call | solution.py:265
  14.6 0.9 %collective-permute-done.6.refs_3_ = f32[200,128]{1,0:T(8,128)S(1)} collective-permute-done((f32[200,128]{1,0:T(8,128)S(1)}, f32[200,128]{1,0:T(8,128)S(1)}, u32[]{:S(2)}, u32[]{:S(2)}) %collective-permute-start.6) | collective-permute-done | bytes 102432 | tf_op jit(solution)/shard_map/ppermute | solution.py:305
  15.5 1.1 %collective-permute-done.3.refs_0_ = f32[200,128]{1,0:T(8,128)S(1)} collective-permute-done((f32[200,128]{1,0:T(8,128)S(1)}, f32[200,128]{1,0:T(8,128)S(1)}, u32[]{:S(2)}, u32[]{:S(2)}) %collective-permute-start.3) | collective-permute-done | bytes 102432 | tf_op jit(solution)/shard_map/ppermute | solution.py:305
  16.6 1.2 %collective-permute-start.7 = (f32[264,128]{1,0:T(8,128)S(1)}, f32[264,128]{1,0:T(8,128)S(1)}, u32[]{:S(2)}, u32[]{:S(2)}) collective-permute-start(f32[264,128]{1,0:T(8,128)S(1)} %get-tuple-element.37.refs_9_), channel_id=1, source_target_pairs={{8,0},{0,4},{4,12},{12,8},{9,1},{1,5},{5,13},{13,9},{10,2},{2,6},{... | collective-permute-start | bytes 405512 | tf_op jit(solution)/shard_map/ppermute | solution.py:27
  17.8 2.4 %collective-permute-start.12 = (f32[256,128]{1,0:T(8,128)S(1)}, f32[256,128]{1,0:T(8,128)S(1)}, u32[]{:S(2)}, u32[]{:S(2)}) collective-permute-start(f32[256,128]{1,0:T(8,128)S(1)} %get-tuple-element.44.refs_12_), channel_id=1, source_target_pairs={{8,0},{0,4},{4,12},{12,8},{9,1},{1,5},{5,13},{13,9},{10,2},{2,6},{... | collective-permute-start | bytes 393224 | tf_op jit(solution)/shard_map/ppermute | solution.py:27
  20.2 0.1 collective-permute-start.14
  20.3 1.5 %collective-permute-start.1 = (f32[200,128]{1,0:T(8,128)S(1)}, f32[200,128]{1,0:T(8,128)S(1)}, u32[]{:S(2)}, u32[]{:S(2)}) collective-permute-start(f32[200,128]{1,0:T(8,128)S(1)} %get-tuple-element.35), channel_id=1, source_target_pairs={{0,2},{1,3},{2,0},{3,1},{4,6},{5,7},{6,4},{7,5},{8,10},{9,11},{10,... | collective-permute-start | bytes 307208 | tf_op jit(solution)/shard_map/ppermute | solution.py:317
  21.8 0.0 collective-permute-done.refs_6_
  21.8 0.0 collective-permute-start.2
  21.8 2.2 %collective-permute-done.7.refs_10_ = f32[264,128]{1,0:T(8,128)S(1)} collective-permute-done((f32[264,128]{1,0:T(8,128)S(1)}, f32[264,128]{1,0:T(8,128)S(1)}, u32[]{:S(2)}, u32[]{:S(2)}) %collective-permute-start.7) | collective-permute-done | bytes 135200 | tf_op jit(solution)/shard_map/ppermute | solution.py:27
  24.0 0.2 collective-permute-start.8
  24.2 2.6 %collective-permute-done.12.refs_13_ = f32[256,128]{1,0:T(8,128)S(1)} collective-permute-done((f32[256,128]{1,0:T(8,128)S(1)}, f32[256,128]{1,0:T(8,128)S(1)}, u32[]{:S(2)}, u32[]{:S(2)}) %collective-permute-start.12) | collective-permute-done | bytes 131104 | tf_op jit(solution)/shard_map/ppermute | solution.py:27
  26.8 0.8 %collective-permute-start.13 = (f32[256,128]{1,0:T(8,128)S(1)}, f32[256,128]{1,0:T(8,128)S(1)}, u32[]{:S(2)}, u32[]{:S(2)}) collective-permute-start(f32[256,128]{1,0:T(8,128)S(1)} %collective-permute-done.12.refs_13_), channel_id=1, source_target_pairs={{8,0},{0,4},{4,12},{12,8},{9,1},{1,5},{5,13},{13,9},{10,2},{2,6},{... | collective-permute-start | bytes 393224 | tf_op jit(solution)/shard_map/ppermute | solution.py:27
  27.6 2.0 %collective-permute-done.14.refs_16_ = f32[256,128]{1,0:T(8,128)S(1)} collective-permute-done((f32[256,128]{1,0:T(8,128)S(1)}, f32[256,128]{1,0:T(8,128)S(1)}, u32[]{:S(2)}, u32[]{:S(2)}) %collective-permute-start.14) | collective-permute-done | bytes 131104 | tf_op jit(solution)/shard_map/ppermute | solution.py:27
  29.6 0.8 %collective-permute-start.15 = (f32[256,128]{1,0:T(8,128)S(1)}, f32[256,128]{1,0:T(8,128)S(1)}, u32[]{:S(2)}, u32[]{:S(2)}) collective-permute-start(f32[256,128]{1,0:T(8,128)S(1)} %collective-permute-done.14.refs_16_), channel_id=1, source_target_pairs={{8,0},{0,4},{4,12},{12,8},{9,1},{1,5},{5,13},{13,9},{10,2},{2,6},{... | collective-permute-start | bytes 393224 | tf_op jit(solution)/shard_map/ppermute | solution.py:27
  30.4 2.1 %collective-permute-done.8.refs_11_ = f32[264,128]{1,0:T(8,128)S(1)} collective-permute-done((f32[264,128]{1,0:T(8,128)S(1)}, f32[264,128]{1,0:T(8,128)S(1)}, u32[]{:S(2)}, u32[]{:S(2)}) %collective-permute-start.8) | collective-permute-done | bytes 135200 | tf_op jit(solution)/shard_map/ppermute | solution.py:27
  32.5 2.4 %apply.3 = (f32[8,32,128]{2,1,0:T(8,128)S(1)}, f32[8,32,128]{2,1,0:T(8,128)S(1)}, f32[8,32,128]{2,1,0:T(8,128)S(1)}, f32[8,32,128]{2,1,0:T(8,128)S(1)}, f32[8,128]{1,0:T(8,128)S(1)}) custom-call(s32[120]{0:T(128)S(1)} %plan.1.plan_ref.refs_0_, bf16[24,128,256]{2,1,0:T(8,128)(2,1)S(1)} %get-tuple-element.29.refs_1_, ...), custom_call_target="tpu_custom_call" | custom-call | flops 1 | bytes 1 | tf_op jit(solution)/shard_map/apply/pallas_call | solution.py:265
  35.0 0.7 %collective-permute-start.9 = (f32[8,32,128]{2,1,0:T(8,128)S(1)}, f32[8,32,128]{2,1,0:T(8,128)S(1)}, u32[]{:S(2)}, u32[]{:S(2)}) collective-permute-start(f32[8,32,128]{2,1,0:T(8,128)S(1)} %get-tuple-element.41), channel_id=1, source_target_pairs={{8,0},{0,4},{4,12},{12,8},{9,1},{1,5},{5,13},{13,9},{10,2},{2,6},{... | collective-permute-start | bytes 393224 | tf_op jit(solution)/shard_map/ppermute | solution.py:27
  35.7 2.4 %apply.5 = (f32[8,32,128]{2,1,0:T(8,128)S(1)}, f32[8,32,128]{2,1,0:T(8,128)S(1)}, f32[8,32,128]{2,1,0:T(8,128)S(1)}, f32[8,32,128]{2,1,0:T(8,128)S(1)}) custom-call(s32[120]{0:T(128)S(1)} %plan.1.plan_ref.refs_0_, bf16[24,128,256]{2,1,0:T(8,128)(2,1)S(1)} %get-tuple-element.29.refs_1_, bf16[24,128,256]{2,1,0:T(8,128)(2,1)S(1)} %get-tuple-element.30.refs_2_, ...), custom_call_target="tpu_custom_call" | custom-call | flops 1 | bytes 1 | tf_op jit(solution)/shard_map/apply/pallas_call | solution.py:265
  38.1 2.9 %collective-permute-start.19 = (f32[8,32,128]{2,1,0:T(8,128)S(1)}, f32[8,32,128]{2,1,0:T(8,128)S(1)}, u32[]{:S(2)}, u32[]{:S(2)}) collective-permute-start(f32[8,32,128]{2,1,0:T(8,128)S(1)} %get-tuple-element.54), channel_id=1, source_target_pairs={{8,0},{0,4},{4,12},{12,8},{9,1},{1,5},{5,13},{13,9},{10,2},{2,6},{... | collective-permute-start | bytes 393224 | tf_op jit(solution)/shard_map/ppermute | solution.py:27
  41.1 0.0 collective-permute-done.15.refs_17_
  41.1 2.5 %apply.4 = (f32[8,32,128]{2,1,0:T(8,128)S(1)}, f32[8,32,128]{2,1,0:T(8,128)S(1)}, f32[8,32,128]{2,1,0:T(8,128)S(1)}, f32[8,32,128]{2,1,0:T(8,128)S(1)}) custom-call(s32[120]{0:T(128)S(1)} %plan.1.plan_ref.refs_0_, bf16[24,128,256]{2,1,0:T(8,128)(2,1)S(1)} %get-tuple-element.29.refs_1_, bf16[24,128,256]{2,1,0:T(8,128)(2,1)S(1)} %get-tuple-element.30.refs_2_, ...), custom_call_target="tpu_custom_call" | custom-call | flops 1 | bytes 1 | tf_op jit(solution)/shard_map/apply/pallas_call | solution.py:265
  43.6 0.0 copy-start
  43.6 0.4 collective-permute-start.16
  43.9 0.0 collective-permute-done.9
  43.9 1.1 %collective-permute-start.10 = (f32[8,32,128]{2,1,0:T(8,128)S(1)}, f32[8,32,128]{2,1,0:T(8,128)S(1)}, u32[]{:S(2)}, u32[]{:S(2)}) collective-permute-start(f32[8,32,128]{2,1,0:T(8,128)S(1)} %add.26), channel_id=1, source_target_pairs={{8,0},{0,4},{4,12},{12,8},{9,1},{1,5},{5,13},{13,9},{10,2},{2,6},{... | collective-permute-start | bytes 393224 | tf_op jit(solution)/shard_map/ppermute | solution.py:27
  45.1 2.4 %collective-permute-start.20 = (f32[8,32,128]{2,1,0:T(8,128)S(1)}, f32[8,32,128]{2,1,0:T(8,128)S(1)}, u32[]{:S(2)}, u32[]{:S(2)}) collective-permute-start(f32[8,32,128]{2,1,0:T(8,128)S(1)} %add.30), channel_id=1, source_target_pairs={{8,0},{0,4},{4,12},{12,8},{9,1},{1,5},{5,13},{13,9},{10,2},{2,6},{... | collective-permute-start | bytes 393224 | tf_op jit(solution)/shard_map/ppermute | solution.py:27
  47.5 3.4 %collective-permute-done.16 = f32[8,32,128]{2,1,0:T(8,128)S(1)} collective-permute-done((f32[8,32,128]{2,1,0:T(8,128)S(1)}, f32[8,32,128]{2,1,0:T(8,128)S(1)}, u32[]{:S(2)}, u32[]{:S(2)}) %collective-permute-start.16) | collective-permute-done | bytes 131104 | tf_op jit(solution)/shard_map/ppermute | solution.py:27
  51.0 0.1 collective-permute-start.17
  51.0 2.7 %collective-permute-done.10 = f32[8,32,128]{2,1,0:T(8,128)S(1)} collective-permute-done((f32[8,32,128]{2,1,0:T(8,128)S(1)}, f32[8,32,128]{2,1,0:T(8,128)S(1)}, u32[]{:S(2)}, u32[]{:S(2)}) %collective-permute-start.10) | collective-permute-done | bytes 131104 | tf_op jit(solution)/shard_map/ppermute | solution.py:27
  53.8 0.1 collective-permute-start.11
  53.8 2.7 %collective-permute-done.20 = f32[8,32,128]{2,1,0:T(8,128)S(1)} collective-permute-done((f32[8,32,128]{2,1,0:T(8,128)S(1)}, f32[8,32,128]{2,1,0:T(8,128)S(1)}, u32[]{:S(2)}, u32[]{:S(2)}) %collective-permute-start.20) | collective-permute-done | bytes 131104 | tf_op jit(solution)/shard_map/ppermute | solution.py:27
  56.6 0.1 collective-permute-start.21
  56.7 2.7 %collective-permute-done.17 = f32[8,32,128]{2,1,0:T(8,128)S(1)} collective-permute-done((f32[8,32,128]{2,1,0:T(8,128)S(1)}, f32[8,32,128]{2,1,0:T(8,128)S(1)}, u32[]{:S(2)}, u32[]{:S(2)}) %collective-permute-start.17) | collective-permute-done | bytes 131104 | tf_op jit(solution)/shard_map/ppermute | solution.py:27
  59.4 0.1 collective-permute-start.18
  59.5 2.4 %collective-permute-done.11.arrived_ref = f32[8,32,128]{2,1,0:T(8,128)S(1)} collective-permute-done((f32[8,32,128]{2,1,0:T(8,128)S(1)}, f32[8,32,128]{2,1,0:T(8,128)S(1)}, u32[]{:S(2)}, u32[]{:S(2)}) %collective-permute-start.11) | collective-permute-done | bytes 131104 | tf_op jit(solution)/shard_map/ppermute | solution.py:27
  61.8 1.4 %part.3 = (f32[3,8,32,128]{3,2,1,0:T(8,128)}, f32[3,8,32,128]{3,2,1,0:T(8,128)}) custom-call(f32[8,32,128]{2,1,0:T(8,128)S(1)} %get-tuple-element.38.kept_ref, f32[8,32,128]{2,1,0:T(8,128)S(1)} %collective-permute-done.11.arrived_ref, f32[8,128]{1,0:T(8,128)S(1)} %get-tuple-element.42.inverse_ref.refs_18_.refs_15_, f32[3,8,32,128]{3,2,1,0:T(8,128)S(1)} %copy-done), custom_call_target="tpu_custom_call" | custom-call | flops 1 | bytes 1 | tf_op jit(solution)/shard_map/part/pallas_call | solution.py:265
  63.3 0.7 %part.4._ = f32[3,8,32,128]{3,2,1,0:T(8,128)} custom-call(f32[8,32,128]{2,1,0:T(8,128)S(1)} %get-tuple-element.51.kept_ref, f32[8,32,128]{2,1,0:T(8,128)S(1)} %collective-permute-done.21.arrived_ref, f32[3,8,32,128]{3,2,1,0:T(8,128)} %get-tuple-element.55._), custom_call_target="tpu_custom_call", output_to_operand_aliasing={{}: (2, {})} | custom-call | flops 1 | bytes 1 | tf_op jit(solution)/shard_map/part/pallas_call | solution.py:265
  64.0 1.4 %collective-permute-done.18.arrived_ref = f32[8,32,128]{2,1,0:T(8,128)S(1)} collective-permute-done((f32[8,32,128]{2,1,0:T(8,128)S(1)}, f32[8,32,128]{2,1,0:T(8,128)S(1)}, u32[]{:S(2)}, u32[]{:S(2)}) %collective-permute-start.18) | collective-permute-done | bytes 131104 | tf_op jit(solution)/shard_map/ppermute | solution.py:27
  65.3 0.7 %part.5 = f32[3,8,32,128]{3,2,1,0:T(8,128)} custom-call(f32[8,32,128]{2,1,0:T(8,128)S(1)} %get-tuple-element.47.kept_ref, f32[8,32,128]{2,1,0:T(8,128)S(1)} %collective-permute-done.18.arrived_ref, f32[3,8,32,128]{3,2,1,0:T(8,128)} %part.4._), custom_call_target="tpu_custom_call", output_to_operand_aliasing={{}: (2, {})} | custom-call | flops 1 | bytes 1 | tf_op jit(solution)/shard_map/part/pallas_call | solution.py:265
  (15 shorter events, 0.2 us)
Async XLA Ops:
  1.8 12.7 %collective-permute-start.4 = (f32[200,128]{1,0:T(8,128)S(1)}, f32[200,128]{1,0:T(8,128)S(1)}, u32[]{:S(2)}, u32[]{:S(2)}) collective-permute-start(f32[200,128]{1,0:T(8,128)S(1)} %get-tuple-element.34), channel_id=1, source_target_pairs={{8,1},{9,0},{10,3},{11,2},{0,5},{1,4},{2,7},{3,6},{4,13},{5,12},{6... | collective-permute-start | bytes 307208 | tf_op jit(solution)/shard_map/ppermute | solution.py:305
  4.3 17.5 %collective-permute-start = (f32[200,128]{1,0:T(8,128)S(1)}, f32[200,128]{1,0:T(8,128)S(1)}, u32[]{:S(2)}, u32[]{:S(2)}) collective-permute-start(f32[200,128]{1,0:T(8,128)S(1)} %get-tuple-element.34), channel_id=1, source_target_pairs={{0,1},{1,0},{2,3},{3,2},{4,5},{5,4},{6,7},{7,6},{8,9},{9,8},{10,11... | collective-permute-start | bytes 307208 | tf_op jit(solution)/shard_map/ppermute | solution.py:317
  5.0 9.6 %collective-permute-start.5 = (f32[200,128]{1,0:T(8,128)S(1)}, f32[200,128]{1,0:T(8,128)S(1)}, u32[]{:S(2)}, u32[]{:S(2)}) collective-permute-start(f32[200,128]{1,0:T(8,128)S(1)} %get-tuple-element.35), channel_id=1, source_target_pairs={{8,2},{9,3},{10,0},{11,1},{0,6},{1,7},{2,4},{3,5},{4,14},{5,15},{6... | collective-permute-start | bytes 307208 | tf_op jit(solution)/shard_map/ppermute | solution.py:305
  8.5 7.0 %collective-permute-start.6 = (f32[200,128]{1,0:T(8,128)S(1)}, f32[200,128]{1,0:T(8,128)S(1)}, u32[]{:S(2)}, u32[]{:S(2)}) collective-permute-start(f32[200,128]{1,0:T(8,128)S(1)} %get-tuple-element.36), channel_id=1, source_target_pairs={{8,3},{9,2},{10,1},{11,0},{0,7},{1,6},{2,5},{3,4},{4,15},{5,14},{6... | collective-permute-start | bytes 307208 | tf_op jit(solution)/shard_map/ppermute | solution.py:305
  8.5 8.0 %collective-permute-start.3 = (f32[200,128]{1,0:T(8,128)S(1)}, f32[200,128]{1,0:T(8,128)S(1)}, u32[]{:S(2)}, u32[]{:S(2)}) collective-permute-start(f32[200,128]{1,0:T(8,128)S(1)} %get-tuple-element.33.refs_5_), channel_id=1, source_target_pairs={{8,0},{9,1},{10,2},{11,3},{0,4},{1,5},{2,6},{3,7},{4,12},{5,13},{6... | collective-permute-start | bytes 307208 | tf_op jit(solution)/shard_map/ppermute | solution.py:305
  16.6 7.4 %collective-permute-start.7 = (f32[264,128]{1,0:T(8,128)S(1)}, f32[264,128]{1,0:T(8,128)S(1)}, u32[]{:S(2)}, u32[]{:S(2)}) collective-permute-start(f32[264,128]{1,0:T(8,128)S(1)} %get-tuple-element.37.refs_9_), channel_id=1, source_target_pairs={{8,0},{0,4},{4,12},{12,8},{9,1},{1,5},{5,13},{13,9},{10,2},{2,6},{... | collective-permute-start | bytes 405512 | tf_op jit(solution)/shard_map/ppermute | solution.py:27
  17.8 9.0 %collective-permute-start.12 = (f32[256,128]{1,0:T(8,128)S(1)}, f32[256,128]{1,0:T(8,128)S(1)}, u32[]{:S(2)}, u32[]{:S(2)}) collective-permute-start(f32[256,128]{1,0:T(8,128)S(1)} %get-tuple-element.44.refs_12_), channel_id=1, source_target_pairs={{8,0},{0,4},{4,12},{12,8},{9,1},{1,5},{5,13},{13,9},{10,2},{2,6},{... | collective-permute-start | bytes 393224 | tf_op jit(solution)/shard_map/ppermute | solution.py:27
  20.2 9.4 %collective-permute-start.14 = (f32[256,128]{1,0:T(8,128)S(1)}, f32[256,128]{1,0:T(8,128)S(1)}, u32[]{:S(2)}, u32[]{:S(2)}) collective-permute-start(f32[256,128]{1,0:T(8,128)S(1)} %get-tuple-element.45.refs_15_), channel_id=1, source_target_pairs={{8,0},{0,4},{4,12},{12,8},{9,1},{1,5},{5,13},{13,9},{10,2},{2,6},{... | collective-permute-start | bytes 393224 | tf_op jit(solution)/shard_map/ppermute | solution.py:27
  20.3 7.3 %collective-permute-start.1 = (f32[200,128]{1,0:T(8,128)S(1)}, f32[200,128]{1,0:T(8,128)S(1)}, u32[]{:S(2)}, u32[]{:S(2)}) collective-permute-start(f32[200,128]{1,0:T(8,128)S(1)} %get-tuple-element.35), channel_id=1, source_target_pairs={{0,2},{1,3},{2,0},{3,1},{4,6},{5,7},{6,4},{7,5},{8,10},{9,11},{10,... | collective-permute-start | bytes 307208 | tf_op jit(solution)/shard_map/ppermute | solution.py:317
  21.8 5.8 %collective-permute-start.2 = (f32[200,128]{1,0:T(8,128)S(1)}, f32[200,128]{1,0:T(8,128)S(1)}, u32[]{:S(2)}, u32[]{:S(2)}) collective-permute-start(f32[200,128]{1,0:T(8,128)S(1)} %get-tuple-element.36), channel_id=1, source_target_pairs={{0,3},{1,2},{2,1},{3,0},{4,7},{5,6},{6,5},{7,4},{8,11},{9,10},{10,... | collective-permute-start | bytes 307208 | tf_op jit(solution)/shard_map/ppermute | solution.py:317
  24.0 8.5 %collective-permute-start.8 = (f32[264,128]{1,0:T(8,128)S(1)}, f32[264,128]{1,0:T(8,128)S(1)}, u32[]{:S(2)}, u32[]{:S(2)}) collective-permute-start(f32[264,128]{1,0:T(8,128)S(1)} %collective-permute-done.7.refs_10_), channel_id=1, source_target_pairs={{8,0},{0,4},{4,12},{12,8},{9,1},{1,5},{5,13},{13,9},{10,2},{2,6},{... | collective-permute-start | bytes 405512 | tf_op jit(solution)/shard_map/ppermute | solution.py:27
  26.8 8.9 %collective-permute-start.13 = (f32[256,128]{1,0:T(8,128)S(1)}, f32[256,128]{1,0:T(8,128)S(1)}, u32[]{:S(2)}, u32[]{:S(2)}) collective-permute-start(f32[256,128]{1,0:T(8,128)S(1)} %collective-permute-done.12.refs_13_), channel_id=1, source_target_pairs={{8,0},{0,4},{4,12},{12,8},{9,1},{1,5},{5,13},{13,9},{10,2},{2,6},{... | collective-permute-start | bytes 393224 | tf_op jit(solution)/shard_map/ppermute | solution.py:27
  29.6 11.5 %collective-permute-start.15 = (f32[256,128]{1,0:T(8,128)S(1)}, f32[256,128]{1,0:T(8,128)S(1)}, u32[]{:S(2)}, u32[]{:S(2)}) collective-permute-start(f32[256,128]{1,0:T(8,128)S(1)} %collective-permute-done.14.refs_16_), channel_id=1, source_target_pairs={{8,0},{0,4},{4,12},{12,8},{9,1},{1,5},{5,13},{13,9},{10,2},{2,6},{... | collective-permute-start | bytes 393224 | tf_op jit(solution)/shard_map/ppermute | solution.py:27
  35.0 9.0 %collective-permute-start.9 = (f32[8,32,128]{2,1,0:T(8,128)S(1)}, f32[8,32,128]{2,1,0:T(8,128)S(1)}, u32[]{:S(2)}, u32[]{:S(2)}) collective-permute-start(f32[8,32,128]{2,1,0:T(8,128)S(1)} %get-tuple-element.41), channel_id=1, source_target_pairs={{8,0},{0,4},{4,12},{12,8},{9,1},{1,5},{5,13},{13,9},{10,2},{2,6},{... | collective-permute-start | bytes 393224 | tf_op jit(solution)/shard_map/ppermute | solution.py:27
  38.1 7.0 %collective-permute-start.19 = (f32[8,32,128]{2,1,0:T(8,128)S(1)}, f32[8,32,128]{2,1,0:T(8,128)S(1)}, u32[]{:S(2)}, u32[]{:S(2)}) collective-permute-start(f32[8,32,128]{2,1,0:T(8,128)S(1)} %get-tuple-element.54), channel_id=1, source_target_pairs={{8,0},{0,4},{4,12},{12,8},{9,1},{1,5},{5,13},{13,9},{10,2},{2,6},{... | collective-permute-start | bytes 393224 | tf_op jit(solution)/shard_map/ppermute | solution.py:27
  43.6 18.3 %copy-start = (f32[3,8,32,128]{3,2,1,0:T(8,128)S(1)}, f32[3,8,32,128]{3,2,1,0:T(8,128)}, u32[]{:S(2)}) copy-start(f32[3,8,32,128]{3,2,1,0:T(8,128)} %correction_ref.1) | copy-start | bytes 1179652
  43.6 7.4 %collective-permute-start.16 = (f32[8,32,128]{2,1,0:T(8,128)S(1)}, f32[8,32,128]{2,1,0:T(8,128)S(1)}, u32[]{:S(2)}, u32[]{:S(2)}) collective-permute-start(f32[8,32,128]{2,1,0:T(8,128)S(1)} %get-tuple-element.50), channel_id=1, source_target_pairs={{8,0},{0,4},{4,12},{12,8},{9,1},{1,5},{5,13},{13,9},{10,2},{2,6},{... | collective-permute-start | bytes 393224 | tf_op jit(solution)/shard_map/ppermute | solution.py:27
  43.9 9.8 %collective-permute-start.10 = (f32[8,32,128]{2,1,0:T(8,128)S(1)}, f32[8,32,128]{2,1,0:T(8,128)S(1)}, u32[]{:S(2)}, u32[]{:S(2)}) collective-permute-start(f32[8,32,128]{2,1,0:T(8,128)S(1)} %add.26), channel_id=1, source_target_pairs={{8,0},{0,4},{4,12},{12,8},{9,1},{1,5},{5,13},{13,9},{10,2},{2,6},{... | collective-permute-start | bytes 393224 | tf_op jit(solution)/shard_map/ppermute | solution.py:27
  45.1 11.5 %collective-permute-start.20 = (f32[8,32,128]{2,1,0:T(8,128)S(1)}, f32[8,32,128]{2,1,0:T(8,128)S(1)}, u32[]{:S(2)}, u32[]{:S(2)}) collective-permute-start(f32[8,32,128]{2,1,0:T(8,128)S(1)} %add.30), channel_id=1, source_target_pairs={{8,0},{0,4},{4,12},{12,8},{9,1},{1,5},{5,13},{13,9},{10,2},{2,6},{... | collective-permute-start | bytes 393224 | tf_op jit(solution)/shard_map/ppermute | solution.py:27
  51.0 8.4 %collective-permute-start.17 = (f32[8,32,128]{2,1,0:T(8,128)S(1)}, f32[8,32,128]{2,1,0:T(8,128)S(1)}, u32[]{:S(2)}, u32[]{:S(2)}) collective-permute-start(f32[8,32,128]{2,1,0:T(8,128)S(1)} %add.28), channel_id=1, source_target_pairs={{8,0},{0,4},{4,12},{12,8},{9,1},{1,5},{5,13},{13,9},{10,2},{2,6},{... | collective-permute-start | bytes 393224 | tf_op jit(solution)/shard_map/ppermute | solution.py:27
  53.8 8.0 %collective-permute-start.11 = (f32[8,32,128]{2,1,0:T(8,128)S(1)}, f32[8,32,128]{2,1,0:T(8,128)S(1)}, u32[]{:S(2)}, u32[]{:S(2)}) collective-permute-start(f32[8,32,128]{2,1,0:T(8,128)S(1)} %add.27), channel_id=1, source_target_pairs={{8,0},{0,4},{4,12},{12,8},{9,1},{1,5},{5,13},{13,9},{10,2},{2,6},{... | collective-permute-start | bytes 393224 | tf_op jit(solution)/shard_map/ppermute | solution.py:27
  56.6 6.7 %collective-permute-start.21 = (f32[8,32,128]{2,1,0:T(8,128)S(1)}, f32[8,32,128]{2,1,0:T(8,128)S(1)}, u32[]{:S(2)}, u32[]{:S(2)}) collective-permute-start(f32[8,32,128]{2,1,0:T(8,128)S(1)} %add.31), channel_id=1, source_target_pairs={{8,0},{0,4},{4,12},{12,8},{9,1},{1,5},{5,13},{13,9},{10,2},{2,6},{... | collective-permute-start | bytes 393224 | tf_op jit(solution)/shard_map/ppermute | solution.py:27
  59.4 5.9 %collective-permute-start.18 = (f32[8,32,128]{2,1,0:T(8,128)S(1)}, f32[8,32,128]{2,1,0:T(8,128)S(1)}, u32[]{:S(2)}, u32[]{:S(2)}) collective-permute-start(f32[8,32,128]{2,1,0:T(8,128)S(1)} %add.29), channel_id=1, source_target_pairs={{8,0},{0,4},{4,12},{12,8},{9,1},{1,5},{5,13},{13,9},{10,2},{2,6},{... | collective-permute-start | bytes 393224 | tf_op jit(solution)/shard_map/ppermute | solution.py:27

commit v5 on v4

--- a/solution.py
+++ b/solution.py
@@ -22,8 +22,9 @@
     return [0] + list(range(1, ops, 2)) + list(range(ops - 2, 0, -2))
 
 
-def ring_step(value, ops):
+def ring_step(value, ops, back=False):
     order = ring_order(ops)
+    order = order[::-1] if back else order
     return lax.ppermute(value, "ops", [(order[i - 1], order[i]) for i in range(ops)])
 
 
@@ -240,15 +241,17 @@
         outs[steps][...] = total_ref[:, pl.ds(start, rows), :]
 
 
-def part_kernel(vector, kept_ref, arrived_ref, _, out, sum_ref, sum_sem):
-    sum_ref[...] = kept_ref[...] + arrived_ref[...]
+def part_kernel(vector, *refs):
+    *terms, _, out, sum_ref, sum_sem = refs
+    sum_ref[...] = sum(ref[...] for ref in terms)
     copy = pltpu.make_async_copy(sum_ref, out.at[vector], sum_sem)
     copy.start()
     copy.wait()
 
 
-def part_and_basis_kernel(kept_ref, arrived_ref, inverse_ref, correction_ref, out, basis_ref, sum_ref, sum_sem):
-    sum_ref[...] = kept_ref[...] + arrived_ref[...]
+def part_and_basis_kernel(*refs):
+    *terms, inverse_ref, correction_ref, out, basis_ref, sum_ref, sum_sem = refs
+    sum_ref[...] = sum(ref[...] for ref in terms)
     copy = pltpu.make_async_copy(sum_ref, out.at[0], sum_sem)
     copy.start()
     inverse = inverse_ref[...]
@@ -384,17 +387,23 @@
         )
         if vector == 0:
             inverse = parts[ops]
-        total = parts[1]
-        for step in range(2, ops):
+        ends = [parts[0]]
+        ahead = ops // 2
+        total = parts[ahead]
+        for step in range(ahead + 1, ops):
             total = parts[step] + ring_step(total, ops)
-        ends = [parts[0], ring_step(total, ops)]
+        ends.append(ring_step(total, ops))
+        total = parts[ahead - 1]
+        for step in range(ahead - 2, 0, -1):
+            total = parts[step] + ring_step(total, ops, True)
+        ends.append(ring_step(total, ops, True))
         scratch = [pltpu.VMEM((sectors, rows, width), f32), pltpu.SemaphoreType.DMA]
         if vector == 0:
             sigma_blocks, search_basis = call(
                 part_and_basis_kernel,
                 [(correction.shape, f32)] * 2,
                 ends + [inverse, correction],
-                [vmem] * 4,
+                [vmem] * (len(ends) + 2),
                 [hbm, vmem],
                 "part",
                 scratch,
@@ -405,12 +414,12 @@
                 functools.partial(part_kernel, vector),
                 [(correction.shape, f32)],
                 ends + [main_memory(sigma_blocks)],
-                [vmem] * 2 + [hbm],
+                [vmem] * len(ends) + [hbm],
                 [hbm],
                 "part",
                 scratch,
                 small,
-                {2: 0},
+                {len(ends): 0},
             )
     return (search_basis, sigma_blocks)
 

time: 66.2 us -> 65.8 us (level)
  waiting for transfers between devices: 26.3 us -> 22.6 us
  starting transfers between devices: 21.9 us -> 25.3 us
    ppermute x15, waiting for transfers between devices: 24.3 us -> 20.6 us  [ring_step(): lax.ppermute(value, 'ops', [(order[i - 1], order[i]) for i in range(ops)])]
    ppermute x15, starting transfers between devices: 13.3 us -> 16.6 us  [ring_step(): lax.ppermute(value, 'ops', [(order[i - 1], order[i]) for i in range(ops)])]
  transfers between devices with their start and end apart: 22 -> 22, of which waited for: 12 -> 10; matrix products, arithmetic and copies ran while one was open for 1% -> 1% of each run, Pallas kernels for 22% -> 22%
where the time goes in v5:
time: 65.8 us; the launch traced here: 65.6 us
  starting transfers between devices  25.3 us (38%)
  waiting for transfers between devices  22.6 us (34%)
  Pallas kernels  16.2 us (25%)
  between operations  0.78 us (1%)
  other arithmetic  0.75 us (1%)
    ppermute x15, waiting for transfers between devices, ring_step(): lax.ppermute(value, 'ops', [(order[i - 1], order[i]) for i in range(ops)])  20.6 us
    ppermute x15, starting transfers between devices, ring_step(): lax.ppermute(value, 'ops', [(order[i - 1], order[i]) for i in range(ops)])  16.6 us
    pallas_call x10, Pallas kernels, call(): pl.pallas_call(kernel, out_shape=[jax.ShapeDtypeStruct(shape, dtype) for...  16.2 us
    ppermute x4, starting transfers between devices, local(): lax.ppermute(packed[mask], ('ops', 'sec', 'rep'), [(order[i - 1] * holder...  6.48 us
    ppermute x3, starting transfers between devices, local(): lax.ppermute(packed[mask], ('sec', 'rep'), [(e, e ^ mask) for e in range(...  2.17 us
    ppermute x4, waiting for transfers between devices, local(): lax.ppermute(packed[mask], ('ops', 'sec', 'rep'), [(order[i - 1] * holder...  2 us
  transfers between devices with their start and end apart: 22, of which 10 were waited for; matrix products, arithmetic and copies ran while one was open for 1% of the time, Pallas kernels for 22%

profile of v5, /device:TPU:0, one launch (start us, length us, event | category | flops | bytes accessed | tf_op | source)
XLA Modules:
  0.0 65.6 jit_solution(17204343557769601125)
XLA Ops:
  0.6 1.2 %pack.1 = (f32[200,128]{1,0:T(8,128)S(1)}, f32[200,128]{1,0:T(8,128)S(1)}, f32[200,128]{1,0:T(8,128)S(1)}, f32[200,128]{1,0:T(8,128)S(1)}) custom-call(s32[2,4]{1,0:T(2,128)} %bitcast.3, f32[3,8,32,128]{3,2,1,0:T(8,128)} %refs_4_.1), custom_call_target="tpu_custom_call" | custom-call | tf_op jit(solution)/shard_map/pack/pallas_call | solution.py:268
  1.8 2.5 %collective-permute-start.4 = (f32[200,128]{1,0:T(8,128)S(1)}, f32[200,128]{1,0:T(8,128)S(1)}, u32[]{:S(2)}, u32[]{:S(2)}) collective-permute-start(f32[200,128]{1,0:T(8,128)S(1)} %get-tuple-element.34), channel_id=1, source_target_pairs={{8,1},{9,0},{10,3},{11,2},{0,5},{1,4},{2,7},{3,6},{4,13},{5,12},{6... | collective-permute-start | bytes 307208 | tf_op jit(solution)/shard_map/ppermute | solution.py:308
  4.3 0.7 %collective-permute-start = (f32[200,128]{1,0:T(8,128)S(1)}, f32[200,128]{1,0:T(8,128)S(1)}, u32[]{:S(2)}, u32[]{:S(2)}) collective-permute-start(f32[200,128]{1,0:T(8,128)S(1)} %get-tuple-element.34), channel_id=1, source_target_pairs={{0,1},{1,0},{2,3},{3,2},{4,5},{5,4},{6,7},{7,6},{8,9},{9,8},{10,11... | collective-permute-start | bytes 307208 | tf_op jit(solution)/shard_map/ppermute | solution.py:320
  5.0 3.5 %collective-permute-start.5 = (f32[200,128]{1,0:T(8,128)S(1)}, f32[200,128]{1,0:T(8,128)S(1)}, u32[]{:S(2)}, u32[]{:S(2)}) collective-permute-start(f32[200,128]{1,0:T(8,128)S(1)} %get-tuple-element.35), channel_id=1, source_target_pairs={{8,2},{9,3},{10,0},{11,1},{0,6},{1,7},{2,4},{3,5},{4,14},{5,15},{6... | collective-permute-start | bytes 307208 | tf_op jit(solution)/shard_map/ppermute | solution.py:308
  8.5 0.4 collective-permute-start.3
  9.0 0.7 %multiply_add_fusion.packed_ref = s32[40]{0:T(128)S(1)} fusion(s32[40]{0:T(128)} %param.14, s32[40]{0:T(128)} %param.13, s32[40]{0:T(128)} %param.12), kind=kLoop, calls=%fused_computation | loop fusion | flops 160 | bytes 640 | tf_op jit(solution)/shard_map/add | solution.py:326
  9.7 1.8 %plan.1.plan_ref.refs_0_ = s32[120]{0:T(128)S(1)} custom-call(s32[40]{0:T(128)S(1)} %multiply_add_fusion.packed_ref), custom_call_target="tpu_custom_call" | custom-call | tf_op jit(solution)/shard_map/plan/pallas_call | solution.py:268
  11.4 3.1 %operators.1 = (bf16[24,128,256]{2,1,0:T(8,128)(2,1)S(1)}, bf16[24,128,256]{2,1,0:T(8,128)(2,1)S(1)}, bf16[256,512]{1,0:T(8,128)(2,1)S(1)}, bf16[128,512]{1,0:T(8,128)(2,1)S(1)}) custom-call(s32[120]{0:T(128)S(1)} %plan.1.plan_ref.refs_0_, s32[40]{0:T(128)} %live_in.1, f32[40,128,128]{2,1,0:T(8,128)} %left_in.1, f32[4,128,128]{2,1,0:T(8,128)} %right_in.1), custom_call_target="tpu_custom_call" | custom-call | tf_op jit(solution)/shard_map/operators/pallas_call | solution.py:268
  14.6 0.0 collective-permute-done.4.refs_1_
  14.6 0.9 %collective-permute-done.6.refs_3_ = f32[200,128]{1,0:T(8,128)S(1)} collective-permute-done((f32[200,128]{1,0:T(8,128)S(1)}, f32[200,128]{1,0:T(8,128)S(1)}, u32[]{:S(2)}, u32[]{:S(2)}) %collective-permute-start.6) | collective-permute-done | bytes 102432 | tf_op jit(solution)/shard_map/ppermute | solution.py:308
  15.5 1.1 %collective-permute-done.3.refs_0_ = f32[200,128]{1,0:T(8,128)S(1)} collective-permute-done((f32[200,128]{1,0:T(8,128)S(1)}, f32[200,128]{1,0:T(8,128)S(1)}, u32[]{:S(2)}, u32[]{:S(2)}) %collective-permute-start.3) | collective-permute-done | bytes 102432 | tf_op jit(solution)/shard_map/ppermute | solution.py:308
  16.6 1.2 %collective-permute-start.7 = (f32[264,128]{1,0:T(8,128)S(1)}, f32[264,128]{1,0:T(8,128)S(1)}, u32[]{:S(2)}, u32[]{:S(2)}) collective-permute-start(f32[264,128]{1,0:T(8,128)S(1)} %get-tuple-element.37.refs_9_), channel_id=1, source_target_pairs={{8,0},{0,4},{4,12},{12,8},{9,1},{1,5},{5,13},{13,9},{10,2},{2,6},{... | collective-permute-start | bytes 405512 | tf_op jit(solution)/shard_map/ppermute | solution.py:28
  17.8 2.4 %collective-permute-start.12 = (f32[256,128]{1,0:T(8,128)S(1)}, f32[256,128]{1,0:T(8,128)S(1)}, u32[]{:S(2)}, u32[]{:S(2)}) collective-permute-start(f32[256,128]{1,0:T(8,128)S(1)} %get-tuple-element.44.refs_12_), channel_id=1, source_target_pairs={{8,0},{0,4},{4,12},{12,8},{9,1},{1,5},{5,13},{13,9},{10,2},{2,6},{... | collective-permute-start | bytes 393224 | tf_op jit(solution)/shard_map/ppermute | solution.py:28
  20.2 0.1 collective-permute-start.14
  20.3 1.5 %collective-permute-start.1 = (f32[200,128]{1,0:T(8,128)S(1)}, f32[200,128]{1,0:T(8,128)S(1)}, u32[]{:S(2)}, u32[]{:S(2)}) collective-permute-start(f32[200,128]{1,0:T(8,128)S(1)} %get-tuple-element.35), channel_id=1, source_target_pairs={{0,2},{1,3},{2,0},{3,1},{4,6},{5,7},{6,4},{7,5},{8,10},{9,11},{10,... | collective-permute-start | bytes 307208 | tf_op jit(solution)/shard_map/ppermute | solution.py:320
  21.8 0.0 collective-permute-done.refs_6_
  21.8 0.0 collective-permute-start.2
  21.8 2.2 %collective-permute-done.7.refs_10_ = f32[264,128]{1,0:T(8,128)S(1)} collective-permute-done((f32[264,128]{1,0:T(8,128)S(1)}, f32[264,128]{1,0:T(8,128)S(1)}, u32[]{:S(2)}, u32[]{:S(2)}) %collective-permute-start.7) | collective-permute-done | bytes 135200 | tf_op jit(solution)/shard_map/ppermute | solution.py:28
  24.0 0.2 collective-permute-start.8
  24.2 2.6 %collective-permute-done.12.refs_13_ = f32[256,128]{1,0:T(8,128)S(1)} collective-permute-done((f32[256,128]{1,0:T(8,128)S(1)}, f32[256,128]{1,0:T(8,128)S(1)}, u32[]{:S(2)}, u32[]{:S(2)}) %collective-permute-start.12) | collective-permute-done | bytes 131104 | tf_op jit(solution)/shard_map/ppermute | solution.py:28
  26.8 0.8 %collective-permute-start.13 = (f32[256,128]{1,0:T(8,128)S(1)}, f32[256,128]{1,0:T(8,128)S(1)}, u32[]{:S(2)}, u32[]{:S(2)}) collective-permute-start(f32[256,128]{1,0:T(8,128)S(1)} %collective-permute-done.12.refs_13_), channel_id=1, source_target_pairs={{8,0},{0,4},{4,12},{12,8},{9,1},{1,5},{5,13},{13,9},{10,2},{2,6},{... | collective-permute-start | bytes 393224 | tf_op jit(solution)/shard_map/ppermute | solution.py:28
  27.6 0.0 collective-permute-done.2.refs_8_
  27.6 2.0 %collective-permute-done.14.refs_16_ = f32[256,128]{1,0:T(8,128)S(1)} collective-permute-done((f32[256,128]{1,0:T(8,128)S(1)}, f32[256,128]{1,0:T(8,128)S(1)}, u32[]{:S(2)}, u32[]{:S(2)}) %collective-permute-start.14) | collective-permute-done | bytes 131104 | tf_op jit(solution)/shard_map/ppermute | solution.py:28
  29.6 0.8 %collective-permute-start.15 = (f32[256,128]{1,0:T(8,128)S(1)}, f32[256,128]{1,0:T(8,128)S(1)}, u32[]{:S(2)}, u32[]{:S(2)}) collective-permute-start(f32[256,128]{1,0:T(8,128)S(1)} %collective-permute-done.14.refs_16_), channel_id=1, source_target_pairs={{8,0},{0,4},{4,12},{12,8},{9,1},{1,5},{5,13},{13,9},{10,2},{2,6},{... | collective-permute-start | bytes 393224 | tf_op jit(solution)/shard_map/ppermute | solution.py:28
  30.4 2.1 %collective-permute-done.8.refs_11_ = f32[264,128]{1,0:T(8,128)S(1)} collective-permute-done((f32[264,128]{1,0:T(8,128)S(1)}, f32[264,128]{1,0:T(8,128)S(1)}, u32[]{:S(2)}, u32[]{:S(2)}) %collective-permute-start.8) | collective-permute-done | bytes 135200 | tf_op jit(solution)/shard_map/ppermute | solution.py:28
  32.5 2.4 %apply.3 = (f32[8,32,128]{2,1,0:T(8,128)S(1)}, f32[8,32,128]{2,1,0:T(8,128)S(1)}, f32[8,32,128]{2,1,0:T(8,128)S(1)}, f32[8,32,128]{2,1,0:T(8,128)S(1)}, f32[8,128]{1,0:T(8,128)S(1)}) custom-call(s32[120]{0:T(128)S(1)} %plan.1.plan_ref.refs_0_, bf16[24,128,256]{2,1,0:T(8,128)(2,1)S(1)} %get-tuple-element.29.refs_1_, ...), custom_call_target="tpu_custom_call" | custom-call | flops 1 | bytes 1 | tf_op jit(solution)/shard_map/apply/pallas_call | solution.py:268
  35.0 0.7 %collective-permute-start.9 = (f32[8,32,128]{2,1,0:T(8,128)S(1)}, f32[8,32,128]{2,1,0:T(8,128)S(1)}, u32[]{:S(2)}, u32[]{:S(2)}) collective-permute-start(f32[8,32,128]{2,1,0:T(8,128)S(1)} %get-tuple-element.40), channel_id=1, source_target_pairs={{8,0},{0,4},{4,12},{12,8},{9,1},{1,5},{5,13},{13,9},{10,2},{2,6},{... | collective-permute-start | bytes 393224 | tf_op jit(solution)/shard_map/ppermute | solution.py:28
  35.7 0.0 collective-permute-done.13.refs_14_
  35.7 2.4 %apply.5 = (f32[8,32,128]{2,1,0:T(8,128)S(1)}, f32[8,32,128]{2,1,0:T(8,128)S(1)}, f32[8,32,128]{2,1,0:T(8,128)S(1)}, f32[8,32,128]{2,1,0:T(8,128)S(1)}) custom-call(s32[120]{0:T(128)S(1)} %plan.1.plan_ref.refs_0_, bf16[24,128,256]{2,1,0:T(8,128)(2,1)S(1)} %get-tuple-element.29.refs_1_, bf16[24,128,256]{2,1,0:T(8,128)(2,1)S(1)} %get-tuple-element.30.refs_2_, ...), custom_call_target="tpu_custom_call" | custom-call | flops 1 | bytes 1 | tf_op jit(solution)/shard_map/apply/pallas_call | solution.py:268
  38.1 0.0 copy-start
  38.1 2.9 %collective-permute-start.19 = (f32[8,32,128]{2,1,0:T(8,128)S(1)}, f32[8,32,128]{2,1,0:T(8,128)S(1)}, u32[]{:S(2)}, u32[]{:S(2)}) collective-permute-start(f32[8,32,128]{2,1,0:T(8,128)S(1)} %get-tuple-element.53), channel_id=1, source_target_pairs={{8,0},{0,4},{4,12},{12,8},{9,1},{1,5},{5,13},{13,9},{10,2},{2,6},{... | collective-permute-start | bytes 393224 | tf_op jit(solution)/shard_map/ppermute | solution.py:28
  41.1 2.5 %apply.4 = (f32[8,32,128]{2,1,0:T(8,128)S(1)}, f32[8,32,128]{2,1,0:T(8,128)S(1)}, f32[8,32,128]{2,1,0:T(8,128)S(1)}, f32[8,32,128]{2,1,0:T(8,128)S(1)}) custom-call(s32[120]{0:T(128)S(1)} %plan.1.plan_ref.refs_0_, bf16[24,128,256]{2,1,0:T(8,128)(2,1)S(1)} %get-tuple-element.29.refs_1_, bf16[24,128,256]{2,1,0:T(8,128)(2,1)S(1)} %get-tuple-element.30.refs_2_, ...), custom_call_target="tpu_custom_call" | custom-call | flops 1 | bytes 1 | tf_op jit(solution)/shard_map/apply/pallas_call | solution.py:268
  43.6 0.4 collective-permute-start.16
  43.9 2.6 %collective-permute-start.11 = (f32[8,32,128]{2,1,0:T(8,128)S(1)}, f32[8,32,128]{2,1,0:T(8,128)S(1)}, u32[]{:S(2)}, u32[]{:S(2)}) collective-permute-start(f32[8,32,128]{2,1,0:T(8,128)S(1)} %get-tuple-element.41), channel_id=1, source_target_pairs={{0,8},{8,12},{12,4},{4,0},{1,9},{9,13},{13,5},{5,1},{2,10},{10,14}... | collective-permute-start | bytes 393224 | tf_op jit(solution)/shard_map/ppermute | solution.py:28
  46.5 0.0 collective-permute-start.21
  46.6 2.0 %collective-permute-start.10 = (f32[8,32,128]{2,1,0:T(8,128)S(1)}, f32[8,32,128]{2,1,0:T(8,128)S(1)}, u32[]{:S(2)}, u32[]{:S(2)}) collective-permute-start(f32[8,32,128]{2,1,0:T(8,128)S(1)} %add.17), channel_id=1, source_target_pairs={{8,0},{0,4},{4,12},{12,8},{9,1},{1,5},{5,13},{13,9},{10,2},{2,6},{... | collective-permute-start | bytes 393224 | tf_op jit(solution)/shard_map/ppermute | solution.py:28
  48.7 0.4 collective-permute-start.20
  49.0 6.4 %collective-permute-done.16 = f32[8,32,128]{2,1,0:T(8,128)S(1)} collective-permute-done((f32[8,32,128]{2,1,0:T(8,128)S(1)}, f32[8,32,128]{2,1,0:T(8,128)S(1)}, u32[]{:S(2)}, u32[]{:S(2)}) %collective-permute-start.16) | collective-permute-done | bytes 131104 | tf_op jit(solution)/shard_map/ppermute | solution.py:28
  55.5 0.0 collective-permute-done.11.refs_2_
  55.5 2.1 %collective-permute-start.17 = (f32[8,32,128]{2,1,0:T(8,128)S(1)}, f32[8,32,128]{2,1,0:T(8,128)S(1)}, u32[]{:S(2)}, u32[]{:S(2)}) collective-permute-start(f32[8,32,128]{2,1,0:T(8,128)S(1)} %add.18), channel_id=1, source_target_pairs={{8,0},{0,4},{4,12},{12,8},{9,1},{1,5},{5,13},{13,9},{10,2},{2,6},{... | collective-permute-start | bytes 393224 | tf_op jit(solution)/shard_map/ppermute | solution.py:28
  57.6 1.8 %collective-permute-done.10.refs_1_ = f32[8,32,128]{2,1,0:T(8,128)S(1)} collective-permute-done((f32[8,32,128]{2,1,0:T(8,128)S(1)}, f32[8,32,128]{2,1,0:T(8,128)S(1)}, u32[]{:S(2)}, u32[]{:S(2)}) %collective-permute-start.10) | collective-permute-done | bytes 131104 | tf_op jit(solution)/shard_map/ppermute | solution.py:28
  59.4 1.4 %part.3 = (f32[3,8,32,128]{3,2,1,0:T(8,128)}, f32[3,8,32,128]{3,2,1,0:T(8,128)}) custom-call(f32[8,32,128]{2,1,0:T(8,128)S(1)} %get-tuple-element.38.refs_0_, f32[8,32,128]{2,1,0:T(8,128)S(1)} %collective-permute-done.10.refs_1_, f32[8,32,128]{2,1,0:T(8,128)S(1)} %collective-permute-done.11.refs_2_, ...), custom_call_target="tpu_custom_call" | custom-call | flops 1 | bytes 1 | tf_op jit(solution)/shard_map/part/pallas_call | solution.py:268
  60.8 0.0 collective-permute-done.21.refs_2_
  60.8 2.7 %collective-permute-done.20.refs_1_ = f32[8,32,128]{2,1,0:T(8,128)S(1)} collective-permute-done((f32[8,32,128]{2,1,0:T(8,128)S(1)}, f32[8,32,128]{2,1,0:T(8,128)S(1)}, u32[]{:S(2)}, u32[]{:S(2)}) %collective-permute-start.20) | collective-permute-done | bytes 131104 | tf_op jit(solution)/shard_map/ppermute | solution.py:28
  63.5 0.7 %part.4.refs_3_ = f32[3,8,32,128]{3,2,1,0:T(8,128)} custom-call(f32[8,32,128]{2,1,0:T(8,128)S(1)} %get-tuple-element.51.refs_0_, f32[8,32,128]{2,1,0:T(8,128)S(1)} %collective-permute-done.20.refs_1_, f32[8,32,128]{2,1,0:T(8,128)S(1)} %collective-permute-done.21.refs_2_, f32[3,8,32,128]{3,2,1,0:T(8,128)} %get-tuple-element.55.refs_3_), custom_call_target="tpu_custom_call", output_to_operand_aliasing={{}: (3, {})} | custom-call | flops 1 | bytes 1 | tf_op jit(solution)/shard_map/part/pallas_call | solution.py:268
  64.2 0.0 collective-permute-done.18.refs_2_
  64.2 0.7 %collective-permute-done.17.refs_1_ = f32[8,32,128]{2,1,0:T(8,128)S(1)} collective-permute-done((f32[8,32,128]{2,1,0:T(8,128)S(1)}, f32[8,32,128]{2,1,0:T(8,128)S(1)}, u32[]{:S(2)}, u32[]{:S(2)}) %collective-permute-start.17) | collective-permute-done | bytes 131104 | tf_op jit(solution)/shard_map/ppermute | solution.py:28
  64.9 0.7 %part.5 = f32[3,8,32,128]{3,2,1,0:T(8,128)} custom-call(f32[8,32,128]{2,1,0:T(8,128)S(1)} %get-tuple-element.47.refs_0_, f32[8,32,128]{2,1,0:T(8,128)S(1)} %collective-permute-done.17.refs_1_, f32[8,32,128]{2,1,0:T(8,128)S(1)} %collective-permute-done.18.refs_2_, f32[3,8,32,128]{3,2,1,0:T(8,128)} %part.4.refs_3_), custom_call_target="tpu_custom_call", output_to_operand_aliasing={{}: (3, {})} | custom-call | flops 1 | bytes 1 | tf_op jit(solution)/shard_map/part/pallas_call | solution.py:268
  (12 shorter events, 0.1 us)
Async XLA Ops:
  1.8 12.7 %collective-permute-start.4 = (f32[200,128]{1,0:T(8,128)S(1)}, f32[200,128]{1,0:T(8,128)S(1)}, u32[]{:S(2)}, u32[]{:S(2)}) collective-permute-start(f32[200,128]{1,0:T(8,128)S(1)} %get-tuple-element.34), channel_id=1, source_target_pairs={{8,1},{9,0},{10,3},{11,2},{0,5},{1,4},{2,7},{3,6},{4,13},{5,12},{6... | collective-permute-start | bytes 307208 | tf_op jit(solution)/shard_map/ppermute | solution.py:308
  4.3 17.5 %collective-permute-start = (f32[200,128]{1,0:T(8,128)S(1)}, f32[200,128]{1,0:T(8,128)S(1)}, u32[]{:S(2)}, u32[]{:S(2)}) collective-permute-start(f32[200,128]{1,0:T(8,128)S(1)} %get-tuple-element.34), channel_id=1, source_target_pairs={{0,1},{1,0},{2,3},{3,2},{4,5},{5,4},{6,7},{7,6},{8,9},{9,8},{10,11... | collective-permute-start | bytes 307208 | tf_op jit(solution)/shard_map/ppermute | solution.py:320
  5.0 9.6 %collective-permute-start.5 = (f32[200,128]{1,0:T(8,128)S(1)}, f32[200,128]{1,0:T(8,128)S(1)}, u32[]{:S(2)}, u32[]{:S(2)}) collective-permute-start(f32[200,128]{1,0:T(8,128)S(1)} %get-tuple-element.35), channel_id=1, source_target_pairs={{8,2},{9,3},{10,0},{11,1},{0,6},{1,7},{2,4},{3,5},{4,14},{5,15},{6... | collective-permute-start | bytes 307208 | tf_op jit(solution)/shard_map/ppermute | solution.py:308
  8.5 7.0 %collective-permute-start.6 = (f32[200,128]{1,0:T(8,128)S(1)}, f32[200,128]{1,0:T(8,128)S(1)}, u32[]{:S(2)}, u32[]{:S(2)}) collective-permute-start(f32[200,128]{1,0:T(8,128)S(1)} %get-tuple-element.36), channel_id=1, source_target_pairs={{8,3},{9,2},{10,1},{11,0},{0,7},{1,6},{2,5},{3,4},{4,15},{5,14},{6... | collective-permute-start | bytes 307208 | tf_op jit(solution)/shard_map/ppermute | solution.py:308
  8.5 8.0 %collective-permute-start.3 = (f32[200,128]{1,0:T(8,128)S(1)}, f32[200,128]{1,0:T(8,128)S(1)}, u32[]{:S(2)}, u32[]{:S(2)}) collective-permute-start(f32[200,128]{1,0:T(8,128)S(1)} %get-tuple-element.33.refs_5_), channel_id=1, source_target_pairs={{8,0},{9,1},{10,2},{11,3},{0,4},{1,5},{2,6},{3,7},{4,12},{5,13},{6... | collective-permute-start | bytes 307208 | tf_op jit(solution)/shard_map/ppermute | solution.py:308
  16.6 7.4 %collective-permute-start.7 = (f32[264,128]{1,0:T(8,128)S(1)}, f32[264,128]{1,0:T(8,128)S(1)}, u32[]{:S(2)}, u32[]{:S(2)}) collective-permute-start(f32[264,128]{1,0:T(8,128)S(1)} %get-tuple-element.37.refs_9_), channel_id=1, source_target_pairs={{8,0},{0,4},{4,12},{12,8},{9,1},{1,5},{5,13},{13,9},{10,2},{2,6},{... | collective-permute-start | bytes 405512 | tf_op jit(solution)/shard_map/ppermute | solution.py:28
  17.8 9.0 %collective-permute-start.12 = (f32[256,128]{1,0:T(8,128)S(1)}, f32[256,128]{1,0:T(8,128)S(1)}, u32[]{:S(2)}, u32[]{:S(2)}) collective-permute-start(f32[256,128]{1,0:T(8,128)S(1)} %get-tuple-element.44.refs_12_), channel_id=1, source_target_pairs={{8,0},{0,4},{4,12},{12,8},{9,1},{1,5},{5,13},{13,9},{10,2},{2,6},{... | collective-permute-start | bytes 393224 | tf_op jit(solution)/shard_map/ppermute | solution.py:28
  20.2 9.4 %collective-permute-start.14 = (f32[256,128]{1,0:T(8,128)S(1)}, f32[256,128]{1,0:T(8,128)S(1)}, u32[]{:S(2)}, u32[]{:S(2)}) collective-permute-start(f32[256,128]{1,0:T(8,128)S(1)} %get-tuple-element.45.refs_15_), channel_id=1, source_target_pairs={{8,0},{0,4},{4,12},{12,8},{9,1},{1,5},{5,13},{13,9},{10,2},{2,6},{... | collective-permute-start | bytes 393224 | tf_op jit(solution)/shard_map/ppermute | solution.py:28
  20.3 7.3 %collective-permute-start.1 = (f32[200,128]{1,0:T(8,128)S(1)}, f32[200,128]{1,0:T(8,128)S(1)}, u32[]{:S(2)}, u32[]{:S(2)}) collective-permute-start(f32[200,128]{1,0:T(8,128)S(1)} %get-tuple-element.35), channel_id=1, source_target_pairs={{0,2},{1,3},{2,0},{3,1},{4,6},{5,7},{6,4},{7,5},{8,10},{9,11},{10,... | collective-permute-start | bytes 307208 | tf_op jit(solution)/shard_map/ppermute | solution.py:320
  21.8 5.8 %collective-permute-start.2 = (f32[200,128]{1,0:T(8,128)S(1)}, f32[200,128]{1,0:T(8,128)S(1)}, u32[]{:S(2)}, u32[]{:S(2)}) collective-permute-start(f32[200,128]{1,0:T(8,128)S(1)} %get-tuple-element.36), channel_id=1, source_target_pairs={{0,3},{1,2},{2,1},{3,0},{4,7},{5,6},{6,5},{7,4},{8,11},{9,10},{10,... | collective-permute-start | bytes 307208 | tf_op jit(solution)/shard_map/ppermute | solution.py:320
  24.0 8.5 %collective-permute-start.8 = (f32[264,128]{1,0:T(8,128)S(1)}, f32[264,128]{1,0:T(8,128)S(1)}, u32[]{:S(2)}, u32[]{:S(2)}) collective-permute-start(f32[264,128]{1,0:T(8,128)S(1)} %collective-permute-done.7.refs_10_), channel_id=1, source_target_pairs={{8,0},{0,4},{4,12},{12,8},{9,1},{1,5},{5,13},{13,9},{10,2},{2,6},{... | collective-permute-start | bytes 405512 | tf_op jit(solution)/shard_map/ppermute | solution.py:28
  26.8 8.9 %collective-permute-start.13 = (f32[256,128]{1,0:T(8,128)S(1)}, f32[256,128]{1,0:T(8,128)S(1)}, u32[]{:S(2)}, u32[]{:S(2)}) collective-permute-start(f32[256,128]{1,0:T(8,128)S(1)} %collective-permute-done.12.refs_13_), channel_id=1, source_target_pairs={{8,0},{0,4},{4,12},{12,8},{9,1},{1,5},{5,13},{13,9},{10,2},{2,6},{... | collective-permute-start | bytes 393224 | tf_op jit(solution)/shard_map/ppermute | solution.py:28
  29.6 11.5 %collective-permute-start.15 = (f32[256,128]{1,0:T(8,128)S(1)}, f32[256,128]{1,0:T(8,128)S(1)}, u32[]{:S(2)}, u32[]{:S(2)}) collective-permute-start(f32[256,128]{1,0:T(8,128)S(1)} %collective-permute-done.14.refs_16_), channel_id=1, source_target_pairs={{8,0},{0,4},{4,12},{12,8},{9,1},{1,5},{5,13},{13,9},{10,2},{2,6},{... | collective-permute-start | bytes 393224 | tf_op jit(solution)/shard_map/ppermute | solution.py:28
  35.0 11.6 %collective-permute-start.9 = (f32[8,32,128]{2,1,0:T(8,128)S(1)}, f32[8,32,128]{2,1,0:T(8,128)S(1)}, u32[]{:S(2)}, u32[]{:S(2)}) collective-permute-start(f32[8,32,128]{2,1,0:T(8,128)S(1)} %get-tuple-element.40), channel_id=1, source_target_pairs={{8,0},{0,4},{4,12},{12,8},{9,1},{1,5},{5,13},{13,9},{10,2},{2,6},{... | collective-permute-start | bytes 393224 | tf_op jit(solution)/shard_map/ppermute | solution.py:28
  38.1 21.3 %copy-start = (f32[3,8,32,128]{3,2,1,0:T(8,128)S(1)}, f32[3,8,32,128]{3,2,1,0:T(8,128)}, u32[]{:S(2)}) copy-start(f32[3,8,32,128]{3,2,1,0:T(8,128)} %refs_4_.1) | copy-start | bytes 1179652
  38.1 10.5 %collective-permute-start.19 = (f32[8,32,128]{2,1,0:T(8,128)S(1)}, f32[8,32,128]{2,1,0:T(8,128)S(1)}, u32[]{:S(2)}, u32[]{:S(2)}) collective-permute-start(f32[8,32,128]{2,1,0:T(8,128)S(1)} %get-tuple-element.53), channel_id=1, source_target_pairs={{8,0},{0,4},{4,12},{12,8},{9,1},{1,5},{5,13},{13,9},{10,2},{2,6},{... | collective-permute-start | bytes 393224 | tf_op jit(solution)/shard_map/ppermute | solution.py:28
  43.6 11.9 %collective-permute-start.16 = (f32[8,32,128]{2,1,0:T(8,128)S(1)}, f32[8,32,128]{2,1,0:T(8,128)S(1)}, u32[]{:S(2)}, u32[]{:S(2)}) collective-permute-start(f32[8,32,128]{2,1,0:T(8,128)S(1)} %get-tuple-element.49), channel_id=1, source_target_pairs={{8,0},{0,4},{4,12},{12,8},{9,1},{1,5},{5,13},{13,9},{10,2},{2,6},{... | collective-permute-start | bytes 393224 | tf_op jit(solution)/shard_map/ppermute | solution.py:28
  43.9 11.6 %collective-permute-start.11 = (f32[8,32,128]{2,1,0:T(8,128)S(1)}, f32[8,32,128]{2,1,0:T(8,128)S(1)}, u32[]{:S(2)}, u32[]{:S(2)}) collective-permute-start(f32[8,32,128]{2,1,0:T(8,128)S(1)} %get-tuple-element.41), channel_id=1, source_target_pairs={{0,8},{8,12},{12,4},{4,0},{1,9},{9,13},{13,5},{5,1},{2,10},{10,14}... | collective-permute-start | bytes 393224 | tf_op jit(solution)/shard_map/ppermute | solution.py:28
  46.5 14.3 %collective-permute-start.21 = (f32[8,32,128]{2,1,0:T(8,128)S(1)}, f32[8,32,128]{2,1,0:T(8,128)S(1)}, u32[]{:S(2)}, u32[]{:S(2)}) collective-permute-start(f32[8,32,128]{2,1,0:T(8,128)S(1)} %get-tuple-element.54), channel_id=1, source_target_pairs={{0,8},{8,12},{12,4},{4,0},{1,9},{9,13},{13,5},{5,1},{2,10},{10,14}... | collective-permute-start | bytes 393224 | tf_op jit(solution)/shard_map/ppermute | solution.py:28
  46.6 12.8 %collective-permute-start.10 = (f32[8,32,128]{2,1,0:T(8,128)S(1)}, f32[8,32,128]{2,1,0:T(8,128)S(1)}, u32[]{:S(2)}, u32[]{:S(2)}) collective-permute-start(f32[8,32,128]{2,1,0:T(8,128)S(1)} %add.17), channel_id=1, source_target_pairs={{8,0},{0,4},{4,12},{12,8},{9,1},{1,5},{5,13},{13,9},{10,2},{2,6},{... | collective-permute-start | bytes 393224 | tf_op jit(solution)/shard_map/ppermute | solution.py:28
  48.7 14.8 %collective-permute-start.20 = (f32[8,32,128]{2,1,0:T(8,128)S(1)}, f32[8,32,128]{2,1,0:T(8,128)S(1)}, u32[]{:S(2)}, u32[]{:S(2)}) collective-permute-start(f32[8,32,128]{2,1,0:T(8,128)S(1)} %add.19), channel_id=1, source_target_pairs={{8,0},{0,4},{4,12},{12,8},{9,1},{1,5},{5,13},{13,9},{10,2},{2,6},{... | collective-permute-start | bytes 393224 | tf_op jit(solution)/shard_map/ppermute | solution.py:28
  55.5 8.8 %collective-permute-start.18 = (f32[8,32,128]{2,1,0:T(8,128)S(1)}, f32[8,32,128]{2,1,0:T(8,128)S(1)}, u32[]{:S(2)}, u32[]{:S(2)}) collective-permute-start(f32[8,32,128]{2,1,0:T(8,128)S(1)} %get-tuple-element.50), channel_id=1, source_target_pairs={{0,8},{8,12},{12,4},{4,0},{1,9},{9,13},{13,5},{5,1},{2,10},{10,14}... | collective-permute-start | bytes 393224 | tf_op jit(solution)/shard_map/ppermute | solution.py:28
  55.5 9.4 %collective-permute-start.17 = (f32[8,32,128]{2,1,0:T(8,128)S(1)}, f32[8,32,128]{2,1,0:T(8,128)S(1)}, u32[]{:S(2)}, u32[]{:S(2)}) collective-permute-start(f32[8,32,128]{2,1,0:T(8,128)S(1)} %add.18), channel_id=1, source_target_pairs={{8,0},{0,4},{4,12},{12,8},{9,1},{1,5},{5,13},{13,9},{10,2},{2,6},{... | collective-permute-start | bytes 393224 | tf_op jit(solution)/shard_map/ppermute | solution.py:28

commit v6 on v5

--- a/solution.py
+++ b/solution.py
@@ -82,11 +82,14 @@
 
 
 def join_kernel(holders, block, *refs):
-    received, outs = refs[:holders], refs[holders + 1 :]
-    for index, out in enumerate(outs):
-        for sender, part_ref in enumerate(received):
-            out[sender * block : (sender + 1) * block, :] = part_ref[index * block : (index + 1) * block, :]
-    outs[0][holders * block :, :] = sum(ref[ref.shape[0] - 8 :, :] for ref in received)
+    both, outs = refs[: 2 * holders], refs[2 * holders + 1 :]
+    vectors = len(outs) // 2
+    for side in range(2):
+        received, mine = both[side * holders : (side + 1) * holders], outs[side * vectors : (side + 1) * vectors]
+        for index, out in enumerate(mine):
+            for sender, part_ref in enumerate(received):
+                out[sender * block : (sender + 1) * block, :] = part_ref[index * block : (index + 1) * block, :]
+        mine[0][holders * block :, :] = sum(ref[ref.shape[0] - 8 :, :] for ref in received)
 
 
 def plan_kernel(pairs, sectors, cap, terms, packed_ref, plan_ref, next_ref):
@@ -349,21 +352,33 @@
         + [pltpu.SemaphoreType.DMA] * 3,
     )
 
-    joined = call(
-        functools.partial(join_kernel, holders, block),
-        [((slots * rows + (0 if vector else 8), width), f32) for vector in range(vectors)],
-        received + [right_low],
-        [vmem] * holders + [anywhere],
-        [vmem] * vectors,
-        "join",
-    )
-    pieces = [[value] for value in joined]
-    for step in range(2, ops):
+    def join(parts, after):
+        return call(
+            functools.partial(join_kernel, holders, block),
+            [((slots * rows + (0 if vector else 8), width), f32) for vector in range(vectors)] * 2,
+            list(parts) + [after],
+            [vmem] * 2 * holders + [anywhere],
+            [vmem] * 2 * vectors,
+            "join",
+        )
+
+    ahead = ops // 2
+    joined = join(received + near, right_low)
+    joined, own = joined[:vectors], joined[vectors:]
+    pieces = [[value] + [None] * (ops - 2) for value in joined]
+    back = [[value] for value in own]
+    for vector in range(vectors):
+        for step in range(1, ops - ahead):
+            value = back[vector][-1]
+            if vector == 2:
+                value = follow(value, [back[0][1]])
+            back[vector].append(ring_step(value, ops, True))
+            pieces[vector][ops - 1 - step] = back[vector][-1]
+    for step in range(2, ahead + 1):
         for vector in range(vectors):
-            value = pieces[vector][-1]
-            if vector == 2 and step == 3:
-                value = follow(value, near[1:])
-            pieces[vector].append(ring_step(value, ops))
+            value = pieces[vector][step - 2]
+            others = [back[0][1]] if vector == 2 else []
+            pieces[vector][step - 1] = ring_step(follow(value, others), ops)
 
     inverse = None
     for vector in range(vectors):

time: 65.8 us -> 66.5 us (1.011)
  starting transfers between devices: 25.3 us -> 28 us
  waiting for transfers between devices: 22.6 us -> 20.6 us
    ppermute x15, waiting for transfers between devices: 20.6 us -> 18.5 us  [ring_step(): lax.ppermute(value, 'ops', [(order[i - 1], order[i]) for i in range(ops)])]
    ppermute x3, waiting for transfers between devices: 0.01 us -> 2.03 us  [local(): lax.ppermute(packed[mask], ('sec', 'rep'), [(e, e ^ mask) for e in range(...]
    ppermute x4, waiting for transfers between devices: 2 us -> 0.01 us  [local(): lax.ppermute(packed[mask], ('ops', 'sec', 'rep'), [(order[i - 1] * holder...]
    ppermute x15, starting transfers between devices: 16.6 us -> 18.4 us  [ring_step(): lax.ppermute(value, 'ops', [(order[i - 1], order[i]) for i in range(ops)])]
    ppermute x4, starting transfers between devices: 6.48 us -> 7.16 us  [local(): lax.ppermute(packed[mask], ('ops', 'sec', 'rep'), [(order[i - 1] * holder...]
  transfers between devices with their start and end apart: 22 -> 22, of which waited for: 10 -> 11; matrix products, arithmetic and copies ran while one was open for 1% -> 1% of each run, Pallas kernels for 22% -> 22%
where the time goes in v6:
time: 66.5 us; the launch traced here: 66.3 us
  starting transfers between devices  28 us (42%)
  waiting for transfers between devices  20.6 us (31%)
  Pallas kernels  16.2 us (24%)
  between operations  0.78 us (1%)
  other arithmetic  0.75 us (1%)
    ppermute x15, waiting for transfers between devices, ring_step(): lax.ppermute(value, 'ops', [(order[i - 1], order[i]) for i in range(ops)])  18.5 us
    ppermute x15, starting transfers between devices, ring_step(): lax.ppermute(value, 'ops', [(order[i - 1], order[i]) for i in range(ops)])  18.4 us
    pallas_call x10, Pallas kernels, call(): pl.pallas_call(kernel, out_shape=[jax.ShapeDtypeStruct(shape, dtype) for...  16.2 us
    ppermute x4, starting transfers between devices, local(): lax.ppermute(packed[mask], ('ops', 'sec', 'rep'), [(order[i - 1] * holder...  7.16 us
    ppermute x3, starting transfers between devices, local(): lax.ppermute(packed[mask], ('sec', 'rep'), [(e, e ^ mask) for e in range(...  2.4 us
    ppermute x3, waiting for transfers between devices, local(): lax.ppermute(packed[mask], ('sec', 'rep'), [(e, e ^ mask) for e in range(...  2.03 us
  transfers between devices with their start and end apart: 22, of which 11 were waited for; matrix products, arithmetic and copies ran while one was open for 1% of the time, Pallas kernels for 22%

profile of v6, /device:TPU:0, one launch (start us, length us, event | category | flops | bytes accessed | tf_op | source)
XLA Modules:
  0.0 66.3 jit_solution(16390715908144787804)
XLA Ops:
  0.6 1.2 %pack.1 = (f32[200,128]{1,0:T(8,128)S(1)}, f32[200,128]{1,0:T(8,128)S(1)}, f32[200,128]{1,0:T(8,128)S(1)}, f32[200,128]{1,0:T(8,128)S(1)}) custom-call(s32[2,4]{1,0:T(2,128)} %bitcast.3, f32[3,8,32,128]{3,2,1,0:T(8,128)} %refs_4_.1), custom_call_target="tpu_custom_call" | custom-call | tf_op jit(solution)/shard_map/pack/pallas_call | solution.py:271
  1.8 2.5 %collective-permute-start.4 = (f32[200,128]{1,0:T(8,128)S(1)}, f32[200,128]{1,0:T(8,128)S(1)}, u32[]{:S(2)}, u32[]{:S(2)}) collective-permute-start(f32[200,128]{1,0:T(8,128)S(1)} %get-tuple-element.38), channel_id=1, source_target_pairs={{8,1},{9,0},{10,3},{11,2},{0,5},{1,4},{2,7},{3,6},{4,13},{5,12},{6... | collective-permute-start | bytes 307208 | tf_op jit(solution)/shard_map/ppermute | solution.py:311
  4.3 0.7 %collective-permute-start = (f32[200,128]{1,0:T(8,128)S(1)}, f32[200,128]{1,0:T(8,128)S(1)}, u32[]{:S(2)}, u32[]{:S(2)}) collective-permute-start(f32[200,128]{1,0:T(8,128)S(1)} %get-tuple-element.38), channel_id=1, source_target_pairs={{0,1},{1,0},{2,3},{3,2},{4,5},{5,4},{6,7},{7,6},{8,9},{9,8},{10,11... | collective-permute-start | bytes 307208 | tf_op jit(solution)/shard_map/ppermute | solution.py:323
  5.0 3.5 %collective-permute-start.5 = (f32[200,128]{1,0:T(8,128)S(1)}, f32[200,128]{1,0:T(8,128)S(1)}, u32[]{:S(2)}, u32[]{:S(2)}) collective-permute-start(f32[200,128]{1,0:T(8,128)S(1)} %get-tuple-element.39), channel_id=1, source_target_pairs={{8,2},{9,3},{10,0},{11,1},{0,6},{1,7},{2,4},{3,5},{4,14},{5,15},{6... | collective-permute-start | bytes 307208 | tf_op jit(solution)/shard_map/ppermute | solution.py:311
  8.5 0.5 collective-permute-start.1
  9.1 0.4 collective-permute-start.6
  9.5 1.2 %collective-permute-start.2 = (f32[200,128]{1,0:T(8,128)S(1)}, f32[200,128]{1,0:T(8,128)S(1)}, u32[]{:S(2)}, u32[]{:S(2)}) collective-permute-start(f32[200,128]{1,0:T(8,128)S(1)} %get-tuple-element.40), channel_id=1, source_target_pairs={{0,3},{1,2},{2,1},{3,0},{4,7},{5,6},{6,5},{7,4},{8,11},{9,10},{10,... | collective-permute-start | bytes 307208 | tf_op jit(solution)/shard_map/ppermute | solution.py:323
  10.7 0.7 %collective-permute-start.3 = (f32[200,128]{1,0:T(8,128)S(1)}, f32[200,128]{1,0:T(8,128)S(1)}, u32[]{:S(2)}, u32[]{:S(2)}) collective-permute-start(f32[200,128]{1,0:T(8,128)S(1)} %get-tuple-element.37.refs_4_.refs_5_), channel_id=1, source_target_pairs={{8,0},{9,1},{10,2},{11,3},{0,4},{1,5},{2,6},{3,7},{4,12},{5,13},{6... | collective-permute-start | bytes 307208 | tf_op jit(solution)/shard_map/ppermute | solution.py:311
  11.4 0.7 %multiply_add_fusion.packed_ref = s32[40]{0:T(128)S(1)} fusion(s32[40]{0:T(128)} %param.14, s32[40]{0:T(128)} %param.13, s32[40]{0:T(128)} %param.12), kind=kLoop, calls=%fused_computation | loop fusion | flops 160 | bytes 640 | tf_op jit(solution)/shard_map/add | solution.py:329
  12.1 1.8 %plan.1.plan_ref.refs_0_ = s32[120]{0:T(128)S(1)} custom-call(s32[40]{0:T(128)S(1)} %multiply_add_fusion.packed_ref), custom_call_target="tpu_custom_call" | custom-call | tf_op jit(solution)/shard_map/plan/pallas_call | solution.py:271
  13.8 3.1 %operators.1 = (bf16[24,128,256]{2,1,0:T(8,128)(2,1)S(1)}, bf16[24,128,256]{2,1,0:T(8,128)(2,1)S(1)}, bf16[256,512]{1,0:T(8,128)(2,1)S(1)}, bf16[128,512]{1,0:T(8,128)(2,1)S(1)}) custom-call(s32[120]{0:T(128)S(1)} %plan.1.plan_ref.refs_0_, s32[40]{0:T(128)} %live_in.1, f32[40,128,128]{2,1,0:T(8,128)} %left_in.1, f32[4,128,128]{2,1,0:T(8,128)} %right_in.1), custom_call_target="tpu_custom_call" | custom-call | tf_op jit(solution)/shard_map/operators/pallas_call | solution.py:271
  17.0 0.0 collective-permute-done.5.refs_2_
  17.0 0.0 collective-permute-done.1.refs_6_.refs_7_
  17.0 0.0 collective-permute-done.6.refs_3_
  17.0 2.0 %collective-permute-done.2.refs_7_.refs_8_ = f32[200,128]{1,0:T(8,128)S(1)} collective-permute-done((f32[200,128]{1,0:T(8,128)S(1)}, f32[200,128]{1,0:T(8,128)S(1)}, u32[]{:S(2)}, u32[]{:S(2)}) %collective-permute-start.2) | collective-permute-done | bytes 102432 | tf_op jit(solution)/shard_map/ppermute | solution.py:323
  19.0 0.1 join.1
  19.1 0.3 collective-permute-start.8
  19.4 1.8 %collective-permute-start.7 = (f32[264,128]{1,0:T(8,128)S(1)}, f32[264,128]{1,0:T(8,128)S(1)}, u32[]{:S(2)}, u32[]{:S(2)}) collective-permute-start(f32[264,128]{1,0:T(8,128)S(1)} %get-tuple-element.41.refs_9_), channel_id=1, source_target_pairs={{8,0},{0,4},{4,12},{12,8},{9,1},{1,5},{5,13},{13,9},{10,2},{2,6},{... | collective-permute-start | bytes 405512 | tf_op jit(solution)/shard_map/ppermute | solution.py:28
  21.1 1.2 %collective-permute-start.13 = (f32[256,128]{1,0:T(8,128)S(1)}, f32[256,128]{1,0:T(8,128)S(1)}, u32[]{:S(2)}, u32[]{:S(2)}) collective-permute-start(f32[256,128]{1,0:T(8,128)S(1)} %get-tuple-element.50), channel_id=1, source_target_pairs={{0,8},{8,12},{12,4},{4,0},{1,9},{9,13},{13,5},{5,1},{2,10},{10,14}... | collective-permute-start | bytes 393224 | tf_op jit(solution)/shard_map/ppermute | solution.py:28
  22.3 1.2 %collective-permute-start.12 = (f32[256,128]{1,0:T(8,128)S(1)}, f32[256,128]{1,0:T(8,128)S(1)}, u32[]{:S(2)}, u32[]{:S(2)}) collective-permute-start(f32[256,128]{1,0:T(8,128)S(1)} %get-tuple-element.49.refs_12_), channel_id=1, source_target_pairs={{8,0},{0,4},{4,12},{12,8},{9,1},{1,5},{5,13},{13,9},{10,2},{2,6},{... | collective-permute-start | bytes 393224 | tf_op jit(solution)/shard_map/ppermute | solution.py:28
  23.5 3.0 %collective-permute-done.8.refs_11_ = f32[264,128]{1,0:T(8,128)S(1)} collective-permute-done((f32[264,128]{1,0:T(8,128)S(1)}, f32[264,128]{1,0:T(8,128)S(1)}, u32[]{:S(2)}, u32[]{:S(2)}) %collective-permute-start.8) | collective-permute-done | bytes 135200 | tf_op jit(solution)/shard_map/ppermute | solution.py:28
  26.5 1.5 %collective-permute-start.14 = (f32[256,128]{1,0:T(8,128)S(1)}, f32[256,128]{1,0:T(8,128)S(1)}, u32[]{:S(2)}, u32[]{:S(2)}) collective-permute-start(f32[256,128]{1,0:T(8,128)S(1)} %get-tuple-element.52.refs_15_), channel_id=1, source_target_pairs={{8,0},{0,4},{4,12},{12,8},{9,1},{1,5},{5,13},{13,9},{10,2},{2,6},{... | collective-permute-start | bytes 393224 | tf_op jit(solution)/shard_map/ppermute | solution.py:28
  27.9 1.5 %collective-permute-start.15 = (f32[256,128]{1,0:T(8,128)S(1)}, f32[256,128]{1,0:T(8,128)S(1)}, u32[]{:S(2)}, u32[]{:S(2)}) collective-permute-start(f32[256,128]{1,0:T(8,128)S(1)} %get-tuple-element.54), channel_id=1, source_target_pairs={{0,8},{8,12},{12,4},{4,0},{1,9},{9,13},{13,5},{5,1},{2,10},{10,14}... | collective-permute-start | bytes 393224 | tf_op jit(solution)/shard_map/ppermute | solution.py:28
  29.4 0.9 %collective-permute-done.7.refs_10_ = f32[264,128]{1,0:T(8,128)S(1)} collective-permute-done((f32[264,128]{1,0:T(8,128)S(1)}, f32[264,128]{1,0:T(8,128)S(1)}, u32[]{:S(2)}, u32[]{:S(2)}) %collective-permute-start.7) | collective-permute-done | bytes 135200 | tf_op jit(solution)/shard_map/ppermute | solution.py:28
  30.3 2.4 %apply.3 = (f32[8,32,128]{2,1,0:T(8,128)S(1)}, f32[8,32,128]{2,1,0:T(8,128)S(1)}, f32[8,32,128]{2,1,0:T(8,128)S(1)}, f32[8,32,128]{2,1,0:T(8,128)S(1)}, f32[8,128]{1,0:T(8,128)S(1)}) custom-call(s32[120]{0:T(128)S(1)} %plan.1.plan_ref.refs_0_, bf16[24,128,256]{2,1,0:T(8,128)(2,1)S(1)} %get-tuple-element.33.refs_1_, ...), custom_call_target="tpu_custom_call" | custom-call | flops 1 | bytes 1 | tf_op jit(solution)/shard_map/apply/pallas_call | solution.py:271
  32.8 0.1 collective-permute-start.9
  32.9 0.0 collective-permute-done.13.refs_14_
  32.9 2.3 %collective-permute-done.12.refs_13_ = f32[256,128]{1,0:T(8,128)S(1)} collective-permute-done((f32[256,128]{1,0:T(8,128)S(1)}, f32[256,128]{1,0:T(8,128)S(1)}, u32[]{:S(2)}, u32[]{:S(2)}) %collective-permute-start.12) | collective-permute-done | bytes 131104 | tf_op jit(solution)/shard_map/ppermute | solution.py:28
  35.2 2.4 %apply.5 = (f32[8,32,128]{2,1,0:T(8,128)S(1)}, f32[8,32,128]{2,1,0:T(8,128)S(1)}, f32[8,32,128]{2,1,0:T(8,128)S(1)}, f32[8,32,128]{2,1,0:T(8,128)S(1)}) custom-call(s32[120]{0:T(128)S(1)} %plan.1.plan_ref.refs_0_, bf16[24,128,256]{2,1,0:T(8,128)(2,1)S(1)} %get-tuple-element.33.refs_1_, bf16[24,128,256]{2,1,0:T(8,128)(2,1)S(1)} %get-tuple-element.34.refs_2_, ...), custom_call_target="tpu_custom_call" | custom-call | flops 1 | bytes 1 | tf_op jit(solution)/shard_map/apply/pallas_call | solution.py:271
  37.6 0.0 copy-start
  37.6 1.1 %collective-permute-start.19 = (f32[8,32,128]{2,1,0:T(8,128)S(1)}, f32[8,32,128]{2,1,0:T(8,128)S(1)}, u32[]{:S(2)}, u32[]{:S(2)}) collective-permute-start(f32[8,32,128]{2,1,0:T(8,128)S(1)} %get-tuple-element.61), channel_id=1, source_target_pairs={{8,0},{0,4},{4,12},{12,8},{9,1},{1,5},{5,13},{13,9},{10,2},{2,6},{... | collective-permute-start | bytes 393224 | tf_op jit(solution)/shard_map/ppermute | solution.py:28
  38.7 0.1 collective-permute-done.14.refs_16_
  38.8 0.6 collective-permute-done.15.refs_17_
  39.4 2.5 %apply.4 = (f32[8,32,128]{2,1,0:T(8,128)S(1)}, f32[8,32,128]{2,1,0:T(8,128)S(1)}, f32[8,32,128]{2,1,0:T(8,128)S(1)}, f32[8,32,128]{2,1,0:T(8,128)S(1)}) custom-call(s32[120]{0:T(128)S(1)} %plan.1.plan_ref.refs_0_, bf16[24,128,256]{2,1,0:T(8,128)(2,1)S(1)} %get-tuple-element.33.refs_1_, bf16[24,128,256]{2,1,0:T(8,128)(2,1)S(1)} %get-tuple-element.34.refs_2_, ...), custom_call_target="tpu_custom_call" | custom-call | flops 1 | bytes 1 | tf_op jit(solution)/shard_map/apply/pallas_call | solution.py:271
  41.9 2.8 %collective-permute-start.16 = (f32[8,32,128]{2,1,0:T(8,128)S(1)}, f32[8,32,128]{2,1,0:T(8,128)S(1)}, u32[]{:S(2)}, u32[]{:S(2)}) collective-permute-start(f32[8,32,128]{2,1,0:T(8,128)S(1)} %get-tuple-element.57), channel_id=1, source_target_pairs={{8,0},{0,4},{4,12},{12,8},{9,1},{1,5},{5,13},{13,9},{10,2},{2,6},{... | collective-permute-start | bytes 393224 | tf_op jit(solution)/shard_map/ppermute | solution.py:28
  44.7 0.2 collective-permute-start.11
  44.9 0.6 collective-permute-start.21
  45.4 1.5 %collective-permute-start.10 = (f32[8,32,128]{2,1,0:T(8,128)S(1)}, f32[8,32,128]{2,1,0:T(8,128)S(1)}, u32[]{:S(2)}, u32[]{:S(2)}) collective-permute-start(f32[8,32,128]{2,1,0:T(8,128)S(1)} %add.17), channel_id=1, source_target_pairs={{8,0},{0,4},{4,12},{12,8},{9,1},{1,5},{5,13},{13,9},{10,2},{2,6},{... | collective-permute-start | bytes 393224 | tf_op jit(solution)/shard_map/ppermute | solution.py:28
  47.0 2.8 %collective-permute-start.20 = (f32[8,32,128]{2,1,0:T(8,128)S(1)}, f32[8,32,128]{2,1,0:T(8,128)S(1)}, u32[]{:S(2)}, u32[]{:S(2)}) collective-permute-start(f32[8,32,128]{2,1,0:T(8,128)S(1)} %add.19), channel_id=1, source_target_pairs={{8,0},{0,4},{4,12},{12,8},{9,1},{1,5},{5,13},{13,9},{10,2},{2,6},{... | collective-permute-start | bytes 393224 | tf_op jit(solution)/shard_map/ppermute | solution.py:28
  49.8 4.4 %collective-permute-done.16 = f32[8,32,128]{2,1,0:T(8,128)S(1)} collective-permute-done((f32[8,32,128]{2,1,0:T(8,128)S(1)}, f32[8,32,128]{2,1,0:T(8,128)S(1)}, u32[]{:S(2)}, u32[]{:S(2)}) %collective-permute-start.16) | collective-permute-done | bytes 131104 | tf_op jit(solution)/shard_map/ppermute | solution.py:28
  54.2 2.1 %collective-permute-start.17 = (f32[8,32,128]{2,1,0:T(8,128)S(1)}, f32[8,32,128]{2,1,0:T(8,128)S(1)}, u32[]{:S(2)}, u32[]{:S(2)}) collective-permute-start(f32[8,32,128]{2,1,0:T(8,128)S(1)} %add.18), channel_id=1, source_target_pairs={{8,0},{0,4},{4,12},{12,8},{9,1},{1,5},{5,13},{13,9},{10,2},{2,6},{... | collective-permute-start | bytes 393224 | tf_op jit(solution)/shard_map/ppermute | solution.py:28
  56.3 1.6 %collective-permute-done.10.refs_1_ = f32[8,32,128]{2,1,0:T(8,128)S(1)} collective-permute-done((f32[8,32,128]{2,1,0:T(8,128)S(1)}, f32[8,32,128]{2,1,0:T(8,128)S(1)}, u32[]{:S(2)}, u32[]{:S(2)}) %collective-permute-start.10) | collective-permute-done | bytes 131104 | tf_op jit(solution)/shard_map/ppermute | solution.py:28
  57.8 1.4 %part.3 = (f32[3,8,32,128]{3,2,1,0:T(8,128)}, f32[3,8,32,128]{3,2,1,0:T(8,128)}) custom-call(f32[8,32,128]{2,1,0:T(8,128)S(1)} %get-tuple-element.43.refs_0_, f32[8,32,128]{2,1,0:T(8,128)S(1)} %collective-permute-done.10.refs_1_, f32[8,32,128]{2,1,0:T(8,128)S(1)} %collective-permute-done.11.refs_2_, ...), custom_call_target="tpu_custom_call" | custom-call | flops 1 | bytes 1 | tf_op jit(solution)/shard_map/part/pallas_call | solution.py:271
  59.3 3.3 %collective-permute-done.20.refs_1_ = f32[8,32,128]{2,1,0:T(8,128)S(1)} collective-permute-done((f32[8,32,128]{2,1,0:T(8,128)S(1)}, f32[8,32,128]{2,1,0:T(8,128)S(1)}, u32[]{:S(2)}, u32[]{:S(2)}) %collective-permute-start.20) | collective-permute-done | bytes 131104 | tf_op jit(solution)/shard_map/ppermute | solution.py:28
  62.6 0.7 %part.4.refs_3_ = f32[3,8,32,128]{3,2,1,0:T(8,128)} custom-call(f32[8,32,128]{2,1,0:T(8,128)S(1)} %get-tuple-element.59.refs_0_, f32[8,32,128]{2,1,0:T(8,128)S(1)} %collective-permute-done.20.refs_1_, f32[8,32,128]{2,1,0:T(8,128)S(1)} %collective-permute-done.21.refs_2_, f32[3,8,32,128]{3,2,1,0:T(8,128)} %get-tuple-element.63.refs_3_), custom_call_target="tpu_custom_call", output_to_operand_aliasing={{}: (3, {})} | custom-call | flops 1 | bytes 1 | tf_op jit(solution)/shard_map/part/pallas_call | solution.py:271
  63.3 0.7 collective-permute-done.18.refs_2_
  64.0 1.6 %collective-permute-done.17.refs_1_ = f32[8,32,128]{2,1,0:T(8,128)S(1)} collective-permute-done((f32[8,32,128]{2,1,0:T(8,128)S(1)}, f32[8,32,128]{2,1,0:T(8,128)S(1)}, u32[]{:S(2)}, u32[]{:S(2)}) %collective-permute-start.17) | collective-permute-done | bytes 131104 | tf_op jit(solution)/shard_map/ppermute | solution.py:28
  65.6 0.7 %part.5 = f32[3,8,32,128]{3,2,1,0:T(8,128)} custom-call(f32[8,32,128]{2,1,0:T(8,128)S(1)} %get-tuple-element.55.refs_0_, f32[8,32,128]{2,1,0:T(8,128)S(1)} %collective-permute-done.17.refs_1_, f32[8,32,128]{2,1,0:T(8,128)S(1)} %collective-permute-done.18.refs_2_, f32[3,8,32,128]{3,2,1,0:T(8,128)} %part.4.refs_3_), custom_call_target="tpu_custom_call", output_to_operand_aliasing={{}: (3, {})} | custom-call | flops 1 | bytes 1 | tf_op jit(solution)/shard_map/part/pallas_call | solution.py:271
  (12 shorter events, 0.1 us)
Async XLA Ops:
  1.8 7.7 %collective-permute-start.4 = (f32[200,128]{1,0:T(8,128)S(1)}, f32[200,128]{1,0:T(8,128)S(1)}, u32[]{:S(2)}, u32[]{:S(2)}) collective-permute-start(f32[200,128]{1,0:T(8,128)S(1)} %get-tuple-element.38), channel_id=1, source_target_pairs={{8,1},{9,0},{10,3},{11,2},{0,5},{1,4},{2,7},{3,6},{4,13},{5,12},{6... | collective-permute-start | bytes 307208 | tf_op jit(solution)/shard_map/ppermute | solution.py:311
  4.3 6.4 %collective-permute-start = (f32[200,128]{1,0:T(8,128)S(1)}, f32[200,128]{1,0:T(8,128)S(1)}, u32[]{:S(2)}, u32[]{:S(2)}) collective-permute-start(f32[200,128]{1,0:T(8,128)S(1)} %get-tuple-element.38), channel_id=1, source_target_pairs={{0,1},{1,0},{2,3},{3,2},{4,5},{5,4},{6,7},{7,6},{8,9},{9,8},{10,11... | collective-permute-start | bytes 307208 | tf_op jit(solution)/shard_map/ppermute | solution.py:323
  5.0 12.0 %collective-permute-start.5 = (f32[200,128]{1,0:T(8,128)S(1)}, f32[200,128]{1,0:T(8,128)S(1)}, u32[]{:S(2)}, u32[]{:S(2)}) collective-permute-start(f32[200,128]{1,0:T(8,128)S(1)} %get-tuple-element.39), channel_id=1, source_target_pairs={{8,2},{9,3},{10,0},{11,1},{0,6},{1,7},{2,4},{3,5},{4,14},{5,15},{6... | collective-permute-start | bytes 307208 | tf_op jit(solution)/shard_map/ppermute | solution.py:311
  8.5 8.5 %collective-permute-start.1 = (f32[200,128]{1,0:T(8,128)S(1)}, f32[200,128]{1,0:T(8,128)S(1)}, u32[]{:S(2)}, u32[]{:S(2)}) collective-permute-start(f32[200,128]{1,0:T(8,128)S(1)} %get-tuple-element.39), channel_id=1, source_target_pairs={{0,2},{1,3},{2,0},{3,1},{4,6},{5,7},{6,4},{7,5},{8,10},{9,11},{10,... | collective-permute-start | bytes 307208 | tf_op jit(solution)/shard_map/ppermute | solution.py:323
  9.1 7.9 %collective-permute-start.6 = (f32[200,128]{1,0:T(8,128)S(1)}, f32[200,128]{1,0:T(8,128)S(1)}, u32[]{:S(2)}, u32[]{:S(2)}) collective-permute-start(f32[200,128]{1,0:T(8,128)S(1)} %get-tuple-element.40), channel_id=1, source_target_pairs={{8,3},{9,2},{10,1},{11,0},{0,7},{1,6},{2,5},{3,4},{4,15},{5,14},{6... | collective-permute-start | bytes 307208 | tf_op jit(solution)/shard_map/ppermute | solution.py:311
  9.5 9.5 %collective-permute-start.2 = (f32[200,128]{1,0:T(8,128)S(1)}, f32[200,128]{1,0:T(8,128)S(1)}, u32[]{:S(2)}, u32[]{:S(2)}) collective-permute-start(f32[200,128]{1,0:T(8,128)S(1)} %get-tuple-element.40), channel_id=1, source_target_pairs={{0,3},{1,2},{2,1},{3,0},{4,7},{5,6},{6,5},{7,4},{8,11},{9,10},{10,... | collective-permute-start | bytes 307208 | tf_op jit(solution)/shard_map/ppermute | solution.py:323
  10.7 8.3 %collective-permute-start.3 = (f32[200,128]{1,0:T(8,128)S(1)}, f32[200,128]{1,0:T(8,128)S(1)}, u32[]{:S(2)}, u32[]{:S(2)}) collective-permute-start(f32[200,128]{1,0:T(8,128)S(1)} %get-tuple-element.37.refs_4_.refs_5_), channel_id=1, source_target_pairs={{8,0},{9,1},{10,2},{11,3},{0,4},{1,5},{2,6},{3,7},{4,12},{5,13},{6... | collective-permute-start | bytes 307208 | tf_op jit(solution)/shard_map/ppermute | solution.py:311
  19.1 7.4 %collective-permute-start.8 = (f32[264,128]{1,0:T(8,128)S(1)}, f32[264,128]{1,0:T(8,128)S(1)}, u32[]{:S(2)}, u32[]{:S(2)}) collective-permute-start(f32[264,128]{1,0:T(8,128)S(1)} %get-tuple-element.42), channel_id=1, source_target_pairs={{0,8},{8,12},{12,4},{4,0},{1,9},{9,13},{13,5},{5,1},{2,10},{10,14}... | collective-permute-start | bytes 405512 | tf_op jit(solution)/shard_map/ppermute | solution.py:28
  19.4 11.0 %collective-permute-start.7 = (f32[264,128]{1,0:T(8,128)S(1)}, f32[264,128]{1,0:T(8,128)S(1)}, u32[]{:S(2)}, u32[]{:S(2)}) collective-permute-start(f32[264,128]{1,0:T(8,128)S(1)} %get-tuple-element.41.refs_9_), channel_id=1, source_target_pairs={{8,0},{0,4},{4,12},{12,8},{9,1},{1,5},{5,13},{13,9},{10,2},{2,6},{... | collective-permute-start | bytes 405512 | tf_op jit(solution)/shard_map/ppermute | solution.py:28
  21.1 11.7 %collective-permute-start.13 = (f32[256,128]{1,0:T(8,128)S(1)}, f32[256,128]{1,0:T(8,128)S(1)}, u32[]{:S(2)}, u32[]{:S(2)}) collective-permute-start(f32[256,128]{1,0:T(8,128)S(1)} %get-tuple-element.50), channel_id=1, source_target_pairs={{0,8},{8,12},{12,4},{4,0},{1,9},{9,13},{13,5},{5,1},{2,10},{10,14}... | collective-permute-start | bytes 393224 | tf_op jit(solution)/shard_map/ppermute | solution.py:28
  22.3 12.9 %collective-permute-start.12 = (f32[256,128]{1,0:T(8,128)S(1)}, f32[256,128]{1,0:T(8,128)S(1)}, u32[]{:S(2)}, u32[]{:S(2)}) collective-permute-start(f32[256,128]{1,0:T(8,128)S(1)} %get-tuple-element.49.refs_12_), channel_id=1, source_target_pairs={{8,0},{0,4},{4,12},{12,8},{9,1},{1,5},{5,13},{13,9},{10,2},{2,6},{... | collective-permute-start | bytes 393224 | tf_op jit(solution)/shard_map/ppermute | solution.py:28
  26.5 12.3 %collective-permute-start.14 = (f32[256,128]{1,0:T(8,128)S(1)}, f32[256,128]{1,0:T(8,128)S(1)}, u32[]{:S(2)}, u32[]{:S(2)}) collective-permute-start(f32[256,128]{1,0:T(8,128)S(1)} %get-tuple-element.52.refs_15_), channel_id=1, source_target_pairs={{8,0},{0,4},{4,12},{12,8},{9,1},{1,5},{5,13},{13,9},{10,2},{2,6},{... | collective-permute-start | bytes 393224 | tf_op jit(solution)/shard_map/ppermute | solution.py:28
  27.9 11.5 %collective-permute-start.15 = (f32[256,128]{1,0:T(8,128)S(1)}, f32[256,128]{1,0:T(8,128)S(1)}, u32[]{:S(2)}, u32[]{:S(2)}) collective-permute-start(f32[256,128]{1,0:T(8,128)S(1)} %get-tuple-element.54), channel_id=1, source_target_pairs={{0,8},{8,12},{12,4},{4,0},{1,9},{9,13},{13,5},{5,1},{2,10},{10,14}... | collective-permute-start | bytes 393224 | tf_op jit(solution)/shard_map/ppermute | solution.py:28
  32.8 12.6 %collective-permute-start.9 = (f32[8,32,128]{2,1,0:T(8,128)S(1)}, f32[8,32,128]{2,1,0:T(8,128)S(1)}, u32[]{:S(2)}, u32[]{:S(2)}) collective-permute-start(f32[8,32,128]{2,1,0:T(8,128)S(1)} %get-tuple-element.45), channel_id=1, source_target_pairs={{8,0},{0,4},{4,12},{12,8},{9,1},{1,5},{5,13},{13,9},{10,2},{2,6},{... | collective-permute-start | bytes 393224 | tf_op jit(solution)/shard_map/ppermute | solution.py:28
  37.6 20.2 %copy-start = (f32[3,8,32,128]{3,2,1,0:T(8,128)S(1)}, f32[3,8,32,128]{3,2,1,0:T(8,128)}, u32[]{:S(2)}) copy-start(f32[3,8,32,128]{3,2,1,0:T(8,128)} %refs_4_.1) | copy-start | bytes 1179652
  37.6 9.4 %collective-permute-start.19 = (f32[8,32,128]{2,1,0:T(8,128)S(1)}, f32[8,32,128]{2,1,0:T(8,128)S(1)}, u32[]{:S(2)}, u32[]{:S(2)}) collective-permute-start(f32[8,32,128]{2,1,0:T(8,128)S(1)} %get-tuple-element.61), channel_id=1, source_target_pairs={{8,0},{0,4},{4,12},{12,8},{9,1},{1,5},{5,13},{13,9},{10,2},{2,6},{... | collective-permute-start | bytes 393224 | tf_op jit(solution)/shard_map/ppermute | solution.py:28
  41.9 12.3 %collective-permute-start.16 = (f32[8,32,128]{2,1,0:T(8,128)S(1)}, f32[8,32,128]{2,1,0:T(8,128)S(1)}, u32[]{:S(2)}, u32[]{:S(2)}) collective-permute-start(f32[8,32,128]{2,1,0:T(8,128)S(1)} %get-tuple-element.57), channel_id=1, source_target_pairs={{8,0},{0,4},{4,12},{12,8},{9,1},{1,5},{5,13},{13,9},{10,2},{2,6},{... | collective-permute-start | bytes 393224 | tf_op jit(solution)/shard_map/ppermute | solution.py:28
  44.7 9.5 %collective-permute-start.11 = (f32[8,32,128]{2,1,0:T(8,128)S(1)}, f32[8,32,128]{2,1,0:T(8,128)S(1)}, u32[]{:S(2)}, u32[]{:S(2)}) collective-permute-start(f32[8,32,128]{2,1,0:T(8,128)S(1)} %get-tuple-element.46), channel_id=1, source_target_pairs={{0,8},{8,12},{12,4},{4,0},{1,9},{9,13},{13,5},{5,1},{2,10},{10,14}... | collective-permute-start | bytes 393224 | tf_op jit(solution)/shard_map/ppermute | solution.py:28
  44.9 14.4 %collective-permute-start.21 = (f32[8,32,128]{2,1,0:T(8,128)S(1)}, f32[8,32,128]{2,1,0:T(8,128)S(1)}, u32[]{:S(2)}, u32[]{:S(2)}) collective-permute-start(f32[8,32,128]{2,1,0:T(8,128)S(1)} %get-tuple-element.62), channel_id=1, source_target_pairs={{0,8},{8,12},{12,4},{4,0},{1,9},{9,13},{13,5},{5,1},{2,10},{10,14}... | collective-permute-start | bytes 393224 | tf_op jit(solution)/shard_map/ppermute | solution.py:28
  45.4 12.4 %collective-permute-start.10 = (f32[8,32,128]{2,1,0:T(8,128)S(1)}, f32[8,32,128]{2,1,0:T(8,128)S(1)}, u32[]{:S(2)}, u32[]{:S(2)}) collective-permute-start(f32[8,32,128]{2,1,0:T(8,128)S(1)} %add.17), channel_id=1, source_target_pairs={{8,0},{0,4},{4,12},{12,8},{9,1},{1,5},{5,13},{13,9},{10,2},{2,6},{... | collective-permute-start | bytes 393224 | tf_op jit(solution)/shard_map/ppermute | solution.py:28
  47.0 15.6 %collective-permute-start.20 = (f32[8,32,128]{2,1,0:T(8,128)S(1)}, f32[8,32,128]{2,1,0:T(8,128)S(1)}, u32[]{:S(2)}, u32[]{:S(2)}) collective-permute-start(f32[8,32,128]{2,1,0:T(8,128)S(1)} %add.19), channel_id=1, source_target_pairs={{8,0},{0,4},{4,12},{12,8},{9,1},{1,5},{5,13},{13,9},{10,2},{2,6},{... | collective-permute-start | bytes 393224 | tf_op jit(solution)/shard_map/ppermute | solution.py:28
  54.2 9.8 %collective-permute-start.18 = (f32[8,32,128]{2,1,0:T(8,128)S(1)}, f32[8,32,128]{2,1,0:T(8,128)S(1)}, u32[]{:S(2)}, u32[]{:S(2)}) collective-permute-start(f32[8,32,128]{2,1,0:T(8,128)S(1)} %get-tuple-element.58), channel_id=1, source_target_pairs={{0,8},{8,12},{12,4},{4,0},{1,9},{9,13},{13,5},{5,1},{2,10},{10,14}... | collective-permute-start | bytes 393224 | tf_op jit(solution)/shard_map/ppermute | solution.py:28
  54.2 11.4 %collective-permute-start.17 = (f32[8,32,128]{2,1,0:T(8,128)S(1)}, f32[8,32,128]{2,1,0:T(8,128)S(1)}, u32[]{:S(2)}, u32[]{:S(2)}) collective-permute-start(f32[8,32,128]{2,1,0:T(8,128)S(1)} %add.18), channel_id=1, source_target_pairs={{8,0},{0,4},{4,12},{12,8},{9,1},{1,5},{5,13},{13,9},{10,2},{2,6},{... | collective-permute-start | bytes 393224 | tf_op jit(solution)/shard_map/ppermute | solution.py:28
